TPU v7x, 128 devices: a whole 4x4x4 slice. The times are simulated.
128 devices in a mesh: seq: 32 (over z_hi, x, y), fsdp: 4 (over z_lo, core).
Axes of the slice: x: 4, y: 4, z: 4 (z_hi: 2, z_lo: 2; z = z_hi * 2 + z_lo), core: 2. Of those that a mesh axis runs over, the one named last changes fastest.
Arguments:
- hidden_in: bfloat16 [4, 16384, 640], P('fsdp', 'seq'), may hold values from -6 to 6
- cotangent: bfloat16 [4, 16384, 640], P('fsdp', 'seq'), may hold values from -6 to 6
- positions: int32 [4, 16384], P('fsdp', 'seq'), may hold values from 0 to 15871, as said below
- query_weight: bfloat16 [640, 1024], P('fsdp'), may hold values from -0.25 to 0.25
- key_weight: bfloat16 [640, 256], P('fsdp'), may hold values from -0.25 to 0.25
- value_weight: bfloat16 [640, 256], P('fsdp'), may hold values from -0.25 to 0.25
- output_weight: bfloat16 [1024, 640], P('fsdp'), may hold values from -0.1875 to 0.1875
- gate_weight: bfloat16 [640, 2048], P('fsdp'), may hold values from -0.25 to 0.25
- up_weight: bfloat16 [640, 2048], P('fsdp'), may hold values from -0.25 to 0.25
- down_weight: bfloat16 [2048, 640], P('fsdp'), may hold values from -0.125 to 0.125
- norm_in: bfloat16 [640], P('fsdp'), may hold values from 0.5 to 1.5
- norm_attn: bfloat16 [640], P('fsdp'), may hold values from 0.5 to 1.5
- norm_ffn_in: bfloat16 [640], P('fsdp'), may hold values from 0.5 to 1.5
- norm_ffn_out: bfloat16 [640], P('fsdp'), may hold values from 0.5 to 1.5
- norm_query: bfloat16 [256], P('fsdp'), may hold values from 0.25 to 1.75
- norm_key: bfloat16 [256], P('fsdp'), may hold values from 0.25 to 1.75
Outputs:
- layer_out: bfloat16 [4, 16384, 640], P('fsdp', 'seq')
- grad_in: bfloat16 [4, 16384, 640], P('fsdp', 'seq')
- grad_query: float32 [640, 1024], P('fsdp')
- grad_key: float32 [640, 256], P('fsdp')
- grad_value: float32 [640, 256], P('fsdp')
- grad_output: float32 [1024, 640], P('fsdp')
- grad_gate: float32 [640, 2048], P('fsdp')
- grad_up: float32 [640, 2048], P('fsdp')
- grad_down: float32 [2048, 640], P('fsdp')
- grad_norm_in: float32 [640], P('fsdp')
- grad_norm_attn: float32 [640], P('fsdp')
- grad_norm_ffn_in: float32 [640], P('fsdp')
- grad_norm_ffn_out: float32 [640], P('fsdp')
- grad_norm_query: float32 [256], P('fsdp')
- grad_norm_key: float32 [256], P('fsdp')
Inputs may be any that keep to these rules, and one draw needn't show every extreme that they name: `positions`: within each sequence the offsets rise by one from token to token and restart at 0 where a document begins (token 0 begins one); one document begins within the first 512 tokens and spans exactly 15872 tokens.
All inputs are finite; a program needn't handle non-finite values.
Results may differ from a plain program's by a relative error of at most 0.03.
Values may be sent and summed in bfloat16 or wider, within the bound.
No kernel may reach another device: no remote copies, remote signals or barrier semaphores. Data moves between devices by JAX's collectives and lax.ppermute only.
A program may use at most 128 MiB of HBM per device.

v0:
```python
import jax
import jax.numpy as jnp
from jax import lax
from jax.experimental import pallas as pl
from jax.experimental.pallas import tpu as pltpu
from jax.sharding import PartitionSpec as P

WINDOW = 512
epsilon = 1e-06
rope_base = 10000.0
masked_value = -1e30
bf16 = jnp.bfloat16
f32 = jnp.float32

rows_out = ((1,), (0,))
rows_both = ((1,), (1,))
cols_both = ((0,), (0,))


def dot(a, b, dims=rows_out):
    return lax.dot_general(a, b, (dims, ((), ())), preferred_element_type=f32)


def spec(*shape):
    return jax.ShapeDtypeStruct(shape[:-1], shape[-1])


def whole():
    return pl.BlockSpec(memory_space=pltpu.VMEM)


def params(mib):
    return pltpu.CompilerParams(vmem_limit_bytes=mib * 1024 * 1024)


def cost(flops, moved, exps=0):
    return pl.CostEstimate(flops=flops, bytes_accessed=moved, transcendentals=exps)


def inverse_rms(v):
    return lax.rsqrt(jnp.mean(v * v, axis=-1, keepdims=True) + epsilon)


def norm_back(v, r, gain, e):
    scaled = gain * e
    return r * scaled - v * (r * r * r * jnp.mean(v * scaled, axis=-1, keepdims=True))


def turn(v, cosine, sine):
    a, b = v[:, :128], v[:, 128:]
    return jnp.concatenate([a * cosine - b * sine, b * cosine + a * sine], axis=1)


def turn_back(v, cosine, sine):
    a, b = v[:, :128], v[:, 128:]
    return jnp.concatenate([a * cosine + b * sine, b * cosine - a * sine], axis=1)


def assemble(pieces, into, place, semaphores, first):
    rows = into.shape[0] // 4
    copies = []
    for r in range(4):
        at = pl.ds(pl.multiple_of((place ^ r) * rows, rows), rows)
        copies.append(
            pltpu.make_async_copy(
                pieces[r].at[pl.ds(0, rows), :], into.at[at, :], semaphores.at[first + r]
            )
        )
    for copy in copies:
        copy.start()
    return copies


def split_out(grads, kept, sent, place, semaphores, first):
    core = lax.rem(place, 2)
    copies = []
    for z in range(2):
        copies.append(
            pltpu.make_async_copy(
                grads.at[2 * z + 1 - core], sent.at[z], semaphores.at[first + 2 * z]
            )
        )
        copies.append(
            pltpu.make_async_copy(
                grads.at[2 * z + core], kept.at[z], semaphores.at[first + 2 * z + 1]
            )
        )
    for copy in copies:
        copy.start()
    return copies


def pack_kernel(g0, g1, g2, g3, g4, g5, k, v, kv, *rest):
    held, semaphores = rest[:6], rest[6]
    copies = [
        pltpu.make_async_copy(source, into, semaphores.at[i])
        for i, (source, into) in enumerate(zip((g0, g1, g2, g3, g4, g5), held))
    ]
    for copy in copies:
        copy.start()
    kv[:160, :256] = k[...]
    kv[:160, 256:] = v[...]
    tile = []
    for copy in copies:
        copy.wait()
    for i, ref in enumerate(held):
        n = ref.shape[0]
        row = ref[...].astype(f32).reshape(1, n)
        tile.append(jnp.concatenate([row, jnp.zeros((1, 512 - n), f32)], axis=1))
    tile.append(jnp.zeros((10, 512), f32))
    kv[160:, :] = jnp.concatenate(tile, axis=0).astype(bf16)


def pack(rows, key_weight, value_weight):
    return pl.pallas_call(
        pack_kernel,
        name="pack",
        in_specs=[pl.BlockSpec(memory_space=pl.ANY)] * 6 + [whole()] * 2,
        out_specs=whole(),
        out_shape=spec(176, 512, bf16),
        scratch_shapes=[pltpu.VMEM(row.shape, bf16) for row in rows]
        + [pltpu.SemaphoreType.DMA((6,))],
        compiler_params=params(4),
        cost_estimate=cost(100_000, 400_000),
    )(*rows, key_weight, value_weight)


def project_kernel(
    place,
    halo,
    own,
    gains,
    head_gains,
    q0,
    q1,
    q2,
    q3,
    kv0,
    kv1,
    kv2,
    kv3,
    cosine,
    sine,
    normed,
    q,
    k,
    v,
    q_proj,
    k_proj,
    wq,
    wkv,
    semaphores,
):
    i = pl.program_id(0)

    @pl.when(i == 0)
    def _():
        copies = assemble((kv0, kv1, kv2, kv3), wkv, place[0], semaphores, 0)
        copies += assemble((q0, q1, q2, q3), wq, place[0], semaphores, 4)
        for copy in copies:
            copy.wait()

    x = jnp.where(i < 2, halo[...], own[...]).astype(f32)
    n = (x * inverse_rms(x) * gains[0:1]).astype(bf16)
    normed[...] = n
    c, s = cosine[...], sine[...]
    kv = dot(n, wkv[...])
    kp = kv[:, :256]
    k_proj[...] = kp
    v[...] = kv[:, 256:].astype(bf16)
    k[...] = turn(kp * inverse_rms(kp) * head_gains[5:6], c, s).astype(bf16)

    @pl.when(i >= 2)
    def _():
        for h in range(4):
            cols = slice(256 * h, 256 * h + 256)
            qp = dot(n, wq[:, cols])
            q_proj[:, cols] = qp
            q[:, cols] = turn(qp * inverse_rms(qp) * head_gains[4:5], c, s).astype(bf16)


def project(place, halo, own, gains, head_gains, q_shares, kv_shares, cosine, sine):
    late = lambda i: (jnp.maximum(i - 2, 0), 0)
    row = lambda i: (i, 0)
    fixed = lambda i: (0, 0)
    return pl.pallas_call(
        project_kernel,
        name="project",
        grid=(4,),
        in_specs=[
            pl.BlockSpec(memory_space=pltpu.SMEM),
            pl.BlockSpec((256, 640), lambda i: (jnp.minimum(i, 1), 0)),
            pl.BlockSpec((256, 640), late),
            pl.BlockSpec((8, 640), fixed),
            pl.BlockSpec((8, 256), fixed),
        ]
        + [pl.BlockSpec(memory_space=pl.ANY)] * 8
        + [pl.BlockSpec((256, 128), row)] * 2,
        out_specs=[
            pl.BlockSpec((256, 640), row),
            pl.BlockSpec((256, 1024), late),
            pl.BlockSpec((256, 256), row),
            pl.BlockSpec((256, 256), row),
            pl.BlockSpec((256, 1024), late),
            pl.BlockSpec((256, 256), row),
        ],
        out_shape=[
            spec(1024, 640, bf16),
            spec(512, 1024, bf16),
            spec(1024, 256, bf16),
            spec(1024, 256, bf16),
            spec(512, 1024, f32),
            spec(1024, 256, f32),
        ],
        scratch_shapes=[
            pltpu.VMEM((640, 1024), bf16),
            pltpu.VMEM((640, 512), bf16),
            pltpu.SemaphoreType.DMA((8,)),
        ],
        compiler_params=params(20),
        cost_estimate=cost(1_350_000_000, 9_000_000),
    )(place, halo, own, gains, head_gains, *q_shares, *kv_shares, cosine, sine)


def visible_keys(offsets):
    distance = (
        lax.broadcasted_iota(jnp.int32, (256, 768), 0)
        + 512
        - lax.broadcasted_iota(jnp.int32, (256, 768), 1)
    )
    return (distance >= 0) & (distance < WINDOW) & (distance <= offsets)


def attend_kernel(q, k, v, offsets, attended, level):
    t = pl.program_id(0)
    near = pl.ds(pl.multiple_of(t * 256, 256), 768)
    keys, values = k[near, :], v[near, :]
    visible = visible_keys(offsets[...])
    for h in range(4):
        cols = slice(256 * h, 256 * h + 256)
        scores = jnp.where(visible, dot(q[:, cols], keys, rows_both) * 0.0625, masked_value)
        top = jnp.max(scores, axis=-1, keepdims=True)
        e = jnp.exp(scores - top)
        total = jnp.sum(e, axis=-1, keepdims=True)
        level[h] = top + jnp.log(total)
        probs = (e * (1.0 / total)).astype(bf16)
        attended[:, cols] = dot(probs, values).astype(bf16)


def attend(q, k, v, offsets):
    row = lambda i: (i, 0)
    fixed = lambda i: (0, 0)
    return pl.pallas_call(
        attend_kernel,
        name="attend",
        grid=(2,),
        in_specs=[
            pl.BlockSpec((256, 1024), row),
            pl.BlockSpec((1024, 256), fixed),
            pl.BlockSpec((1024, 256), fixed),
            pl.BlockSpec((256, 1), row),
        ],
        out_specs=[
            pl.BlockSpec((256, 1024), row),
            pl.BlockSpec((4, 256, 1), lambda i: (0, i, 0)),
        ],
        out_shape=[spec(512, 1024, bf16), spec(4, 512, 1, f32)],
        compiler_params=params(20),
        cost_estimate=cost(1_700_000_000, 4_000_000, 2_000_000),
    )(q, k, v, offsets)


def middle_kernel(
    place,
    x_ref,
    attended,
    upstream,
    gains,
    o0,
    o1,
    o2,
    o3,
    g0,
    g1,
    g2,
    g3,
    u0,
    u1,
    u2,
    u3,
    d0,
    d1,
    d2,
    d3,
    layer_out,
    back_middle,
    back_attn,
    back_attended,
    gain_grads,
    kept,
    sent,
    ffn_in,
    kept_a,
    kept_b,
    hidden,
    back_out,
    in_turned,
    out_turned,
    back_gate,
    back_up,
    wo,
    wg,
    wu,
    wd,
    grads,
    semaphores,
):
    output_copies = assemble((o0, o1, o2, o3), wo, place[0], semaphores, 0)
    gate_copies = assemble((g0, g1, g2, g3), wg, place[0], semaphores, 4)
    up_copies = assemble((u0, u1, u2, u3), wu, place[0], semaphores, 8)
    down_copies = assemble((d0, d1, d2, d3), wd, place[0], semaphores, 12)
    for copy in output_copies:
        copy.wait()
    g_attn, g_in, g_out = gains[1:2], gains[2:3], gains[3:4]
    ao = dot(attended[...], wo[...])
    r1 = inverse_rms(ao)
    mid = x_ref[...].astype(f32) + ao * r1 * g_attn
    r2 = inverse_rms(mid)
    ffn_in[...] = (mid * r2 * g_in).astype(bf16)
    for copy in gate_copies + up_copies:
        copy.wait()

    for j in range(8):
        cols = slice(256 * j, 256 * j + 256)
        u = dot(ffn_in[...], wg[:, cols])
        up = dot(ffn_in[...], wu[:, cols])
        root = 0.7978845608028654
        square = u * u
        t = jnp.tanh(u * (root + (root * 0.044715) * square))
        half = 0.5 + 0.5 * t
        act = u * half
        slope = half + act * (1.0 - t) * (root + (3 * 0.044715 * root) * square)
        hidden[:, cols] = (act * up).astype(bf16)
        kept_a[:, cols] = act
        kept_b[:, cols] = up * slope

    for copy in down_copies:
        copy.wait()
    fo = dot(hidden[...], wd[...])
    r3 = inverse_rms(fo)
    layer_out[...] = (mid + fo * r3 * g_out).astype(bf16)
    g = upstream[...].astype(f32)
    gain_grads[2:3] = jnp.sum(fo * r3 * g, axis=0, keepdims=True)
    bfo = norm_back(fo, r3, g_out, g)
    back_out[...] = bfo.astype(bf16)
    out_turned[...] = back_out[...].T
    in_turned[...] = ffn_in[...].T

    for j in range(8):
        cols = slice(256 * j, 256 * j + 256)
        bh = dot(back_out[...], wd[cols, :], rows_both)
        bu = (bh * kept_a[:, cols]).astype(bf16)
        bg = (bh * kept_b[:, cols]).astype(bf16)
        back_gate[:, cols] = bg
        back_up[:, cols] = bu

    for base, right in ((0, back_gate), (2560, back_up)):
        for j in range(2048 // 512):
            part = dot(in_turned[...], right[:, 512 * j : 512 * j + 512]).astype(bf16)
            for b in range(512 // 128):
                at = base + (512 // 128 * j + b) * 160
                for f in range(4):
                    grads[f, at : at + 160, :] = part[
                        160 * f : 160 * f + 160, 128 * b : 128 * b + 128
                    ]
    for f in range(4):
        part = dot(out_turned[...], hidden[:, 512 * f : 512 * f + 512]).astype(bf16)
        for b in range(4):
            at = 5120 + 640 * b
            grads[f, at : at + 640, :] = part[:, 128 * b : 128 * b + 128]

    outward = split_out(grads, kept, sent, place[0], semaphores, 16)
    e = dot(back_gate[...], wg[...], rows_both) + dot(back_up[...], wu[...], rows_both)
    gain_grads[1:2] = jnp.sum(mid * r2 * e, axis=0, keepdims=True)
    bm = g + norm_back(mid, r2, g_in, e)
    back_middle[...] = bm
    gain_grads[0:1] = jnp.sum(ao * r1 * bm, axis=0, keepdims=True)
    bao = norm_back(ao, r1, g_attn, bm).astype(bf16)
    back_attn[...] = bao
    back_attended[...] = dot(bao, wo[...], rows_both).astype(bf16)
    for copy in outward:
        copy.wait()


def middle_part(place, x, attended, upstream, gains, shares):
    return pl.pallas_call(
        middle_kernel,
        name="middle_part",
        in_specs=[pl.BlockSpec(memory_space=pltpu.SMEM)]
        + [whole()] * 4
        + [pl.BlockSpec(memory_space=pl.ANY)] * 16,
        out_specs=[whole()] * 5 + [pl.BlockSpec(memory_space=pl.ANY)] * 2,
        out_shape=[
            spec(512, 640, bf16),
            spec(512, 640, f32),
            spec(512, 640, bf16),
            spec(512, 1024, bf16),
            spec(8, 640, f32),
            spec(2, 7680, 128, bf16),
            spec(2, 7680, 128, bf16),
        ],
        scratch_shapes=[
            pltpu.VMEM((512, 640), bf16),
            pltpu.VMEM((512, 2048), f32),
            pltpu.VMEM((512, 2048), f32),
            pltpu.VMEM((512, 2048), bf16),
            pltpu.VMEM((512, 640), bf16),
            pltpu.VMEM((640, 512), bf16),
            pltpu.VMEM((640, 512), bf16),
            pltpu.VMEM((512, 2048), bf16),
            pltpu.VMEM((512, 2048), bf16),
            pltpu.VMEM((1024, 640), bf16),
            pltpu.VMEM((640, 2048), bf16),
            pltpu.VMEM((640, 2048), bf16),
            pltpu.VMEM((2048, 640), bf16),
            pltpu.VMEM((4, 7680, 128), bf16),
            pltpu.SemaphoreType.DMA((20,)),
        ],
        compiler_params=params(46),
        cost_estimate=cost(13_400_000_000, 23_000_000, 1_000_000),
    )(place, x, attended, upstream, gains, *shares)


def attend_back_kernel(
    q,
    k,
    v,
    offsets,
    level,
    back_attended,
    q_proj,
    k_proj,
    head_gains,
    cosine,
    sine,
    back_q,
    back_kv,
    gain_grads,
    sum_k,
    sum_v,
):
    t = pl.program_id(0)

    @pl.when(t == 0)
    def _():
        sum_k[...] = jnp.zeros_like(sum_k)
        sum_v[...] = jnp.zeros_like(sum_v)
        gain_grads[...] = jnp.zeros_like(gain_grads)

    near = pl.ds(pl.multiple_of(t * 256, 256), 768)
    mine = pl.ds(pl.multiple_of(t * 256 + 512, 256), 256)
    keys, values = k[near, :], v[near, :]
    visible = visible_keys(offsets[...])
    c, s = cosine[mine, :], sine[mine, :]
    for h in range(4):
        cols = slice(256 * h, 256 * h + 256)
        qh, bah = q[:, cols], back_attended[:, cols]
        scores = jnp.where(visible, dot(qh, keys, rows_both) * 0.0625, masked_value)
        probs = jnp.exp(scores - level[h])
        bp = dot(bah, values, rows_both)
        inner = jnp.sum(probs * bp, axis=-1, keepdims=True)
        bs = (probs * (bp - inner)).astype(bf16)
        sum_k[near, :] += dot(bs, qh, cols_both)
        sum_v[near, :] += dot(probs.astype(bf16), bah, cols_both)
        e = turn_back(dot(bs, keys) * 0.0625, c, s)
        qp = q_proj[:, cols]
        r = inverse_rms(qp)
        gain_grads[0:1] += jnp.sum(qp * r * e, axis=0, keepdims=True)
        back_q[:, cols] = norm_back(qp, r, head_gains[4:5], e).astype(bf16)

    @pl.when(t == 1)
    def _():
        e = turn_back(sum_k[...] * 0.0625, cosine[...], sine[...])
        kp = k_proj[...]
        r = inverse_rms(kp)
        gain_grads[1:2] = jnp.sum(kp * r * e, axis=0, keepdims=True)
        back_kv[:, :256] = norm_back(kp, r, head_gains[5:6], e).astype(bf16)
        back_kv[:, 256:] = sum_v[...].astype(bf16)


def attend_back(
    q, k, v, offsets, level, back_attended, q_proj, k_proj, head_gains, cosine, sine
):
    row = lambda i: (i, 0)
    fixed = lambda i: (0, 0)
    return pl.pallas_call(
        attend_back_kernel,
        name="attend_back",
        grid=(2,),
        in_specs=[
            pl.BlockSpec((256, 1024), row),
            pl.BlockSpec((1024, 256), fixed),
            pl.BlockSpec((1024, 256), fixed),
            pl.BlockSpec((256, 1), row),
            pl.BlockSpec((4, 256, 1), lambda i: (0, i, 0)),
            pl.BlockSpec((256, 1024), row),
            pl.BlockSpec((256, 1024), row),
            pl.BlockSpec((1024, 256), fixed),
            pl.BlockSpec((8, 256), fixed),
            pl.BlockSpec((1024, 128), fixed),
            pl.BlockSpec((1024, 128), fixed),
        ],
        out_specs=[
            pl.BlockSpec((256, 1024), row),
            pl.BlockSpec((1024, 512), fixed),
            pl.BlockSpec((8, 256), fixed),
        ],
        out_shape=[spec(512, 1024, bf16), spec(1024, 512, bf16), spec(8, 256, f32)],
        scratch_shapes=[pltpu.VMEM((1024, 256), f32), pltpu.VMEM((1024, 256), f32)],
        compiler_params=params(30),
        cost_estimate=cost(4_300_000_000, 10_000_000, 2_000_000),
    )(q, k, v, offsets, level, back_attended, q_proj, k_proj, head_gains, cosine, sine)


def weights_kernel(
    place,
    normed,
    back_q,
    back_kv,
    attended,
    back_attn,
    halo,
    own,
    gain_mid,
    gain_head,
    q0,
    q1,
    q2,
    q3,
    kv0,
    kv1,
    kv2,
    kv3,
    back_halo,
    back_own,
    kept,
    sent,
    wq,
    wkv,
    grads,
    semaphores,
):
    copies = assemble((kv0, kv1, kv2, kv3), wkv, place[0], semaphores, 0)
    copies += assemble((q0, q1, q2, q3), wq, place[0], semaphores, 4)
    turned = normed[...].astype(f32).T.astype(bf16)
    bq, bkv = back_q[...], back_kv[...]
    part = dot(turned[:, 512:], bq).astype(bf16)
    for b in range(8):
        for f in range(4):
            grads[f, 160 * b : 160 * b + 160, :] = part[
                160 * f : 160 * f + 160, 128 * b : 128 * b + 128
            ]
    part = dot(turned, bkv).astype(bf16)
    for b in range(4):
        for f in range(4):
            grads[f, 1280 + 160 * b : 1440 + 160 * b, :] = part[
                160 * f : 160 * f + 160, 128 * b : 128 * b + 128
            ]
    turned = back_attn[...].astype(f32).T.astype(bf16)
    part = dot(turned, attended[...]).astype(bf16)
    for f in range(4):
        for b in range(2):
            grads[f, 1920 + 640 * b : 2560 + 640 * b, :] = part[
                :, 256 * f + 128 * b : 256 * f + 128 * b + 128
            ]
    for copy in copies:
        copy.wait()
    e = dot(bkv[:512], wkv[...], rows_both)
    back_halo[...] = e.astype(bf16)
    x = halo[...].astype(f32)
    grad = jnp.sum(x * inverse_rms(x) * e, axis=0, keepdims=True)
    e = dot(bkv[512:], wkv[...], rows_both) + dot(bq, wq[...], rows_both)
    back_own[...] = e
    x = own[...].astype(f32)
    grad = grad + jnp.sum(x * inverse_rms(x) * e, axis=0, keepdims=True)
    each = jnp.concatenate([grad, gain_mid[0:3]], axis=0)
    heads = gain_head[0:2]
    for f in range(4):
        share = each[:, 160 * f : 160 * f + 160]
        rest = jnp.concatenate([share[:, 128:], jnp.zeros((4, 96), f32)], axis=1)
        ends = jnp.concatenate([heads[:, 64 * f : 64 * f + 64], jnp.zeros((2, 64), f32)], axis=1)
        tile = jnp.concatenate([share[:, :128], rest, ends, jnp.zeros((6, 128), f32)], axis=0)
        grads[f, 3200:3216, :] = tile.astype(bf16)
        grads[f, 3216:, :] = jnp.zeros((368, 128), bf16)
    for copy in split_out(grads, kept, sent, place[0], semaphores, 8):
        copy.wait()


def weights_part(
    place, normed, back_q, back_kv, attended, back_attn, halo, own, gain_mid, gain_head, shares
):
    return pl.pallas_call(
        weights_kernel,
        name="weights_part",
        in_specs=[pl.BlockSpec(memory_space=pltpu.SMEM)]
        + [whole()] * 9
        + [pl.BlockSpec(memory_space=pl.ANY)] * 8,
        out_specs=[whole()] * 2 + [pl.BlockSpec(memory_space=pl.ANY)] * 2,
        out_shape=[
            spec(512, 640, bf16),
            spec(512, 640, f32),
            spec(2, 3584, 128, bf16),
            spec(2, 3584, 128, bf16),
        ],
        scratch_shapes=[
            pltpu.VMEM((640, 1024), bf16),
            pltpu.VMEM((640, 512), bf16),
            pltpu.VMEM((4, 3584, 128), bf16),
            pltpu.SemaphoreType.DMA((12,)),
        ],
        compiler_params=params(40),
        cost_estimate=cost(3_400_000_000, 14_000_000),
    )(place, normed, back_q, back_kv, attended, back_attn, halo, own, gain_mid, gain_head, *shares)


def finish_kernel(own, back_own, returned, back_middle, gains, grad_in):
    x = own[...].astype(f32)
    e = back_own[...] + returned[...].astype(f32)
    grad_in[...] = (back_middle[...] + norm_back(x, inverse_rms(x), gains[0:1], e)).astype(bf16)


def finish(own, back_own, returned, back_middle, gains):
    row = lambda i: (i, 0)
    return pl.pallas_call(
        finish_kernel,
        name="finish",
        grid=(4,),
        in_specs=[pl.BlockSpec((128, 640), row)] * 4 + [pl.BlockSpec((8, 640), lambda i: (0, 0))],
        out_specs=pl.BlockSpec((128, 640), row),
        out_shape=spec(512, 640, bf16),
        compiler_params=params(10),
        cost_estimate=cost(4_000_000, 5_000_000),
    )(own, back_own, returned, back_middle, gains)


def rope_tables(offsets):
    powers = jnp.arange(128, dtype=f32) * (2.0 / 256)
    row = jnp.arange(512, dtype=jnp.int32)
    every = jnp.concatenate([offsets[0] - 512 + row, offsets])
    angles = every.astype(f32)[:, None] * (rope_base ** (-powers))[None, :]
    return jnp.cos(angles), jnp.sin(angles)


def unpack_kernel(spot, a0, a1, a2, a3, b0, b1, b2, b3, *rest):
    outs, gains, held, (ffn, attn, semaphores) = rest[:7], rest[7], rest[8:15], rest[15:]
    q, k, v, out, gate, up, down = held
    x, y = spot[0], spot[1]
    copies = []
    for half, pieces in enumerate(((a0, a1, a2, a3), (b0, b1, b2, b3))):
        for i in range(4):
            for j in range(4):
                first, second = (x, y) if half == 0 else (y, x)
                block = 16 * half + lax.rem(first - i + 4, 4) * 4 + lax.rem(second - j + 4, 4)
                n = (half * 4 + i) * 4 + j
                for m, (into, start, rows) in enumerate(((ffn, 0, 240), (attn, 240, 112))):
                    copies.append(
                        pltpu.make_async_copy(
                            pieces[i].at[j, pl.ds(start, rows), :],
                            into.at[pl.ds(pl.multiple_of(block * rows, 16), rows), :],
                            semaphores.at[2 * n + m],
                        )
                    )
    for copy in copies:
        copy.start()
    for copy in copies:
        copy.wait()
    outward = []

    def leave(n):
        copy = pltpu.make_async_copy(held[n], outs[n], semaphores.at[64 + n])
        copy.start()
        outward.append(copy)

    for n, into, flat, first, count in (
        (4, gate, ffn, 0, 16),
        (5, up, ffn, 2560, 16),
        (0, q, attn, 0, 8),
        (1, k, attn, 1280, 2),
        (2, v, attn, 1600, 2),
    ):
        for b in range(count):
            at = first + 160 * b
            into[:, 128 * b : 128 * b + 128] = flat[at : at + 160, :].astype(f32)
        leave(n)
    for n, into, flat, first, count in ((6, down, ffn, 5120, 4), (3, out, attn, 1920, 2)):
        for b in range(count):
            at = first + 640 * b
            into[128 * b : 128 * b + 128, :] = flat[at : at + 640, :].astype(f32).T
        leave(n)
    gains[...] = attn[3200:3216, :].astype(f32)
    for copy in outward:
        copy.wait()


def unpack(spot, pieces):
    shapes = [(160, 1024), (160, 256), (160, 256), (256, 640), (160, 2048), (160, 2048), (512, 640)]
    return pl.pallas_call(
        unpack_kernel,
        name="unpack",
        in_specs=[pl.BlockSpec(memory_space=pltpu.SMEM)] + [pl.BlockSpec(memory_space=pl.ANY)] * 8,
        out_specs=[pl.BlockSpec(memory_space=pl.ANY)] * 7 + [whole()],
        out_shape=[spec(*shape, f32) for shape in shapes] + [spec(16, 128, f32)],
        scratch_shapes=[pltpu.VMEM(shape, f32) for shape in shapes]
        + [
            pltpu.VMEM((7680, 128), bf16),
            pltpu.VMEM((3584, 128), bf16),
            pltpu.SemaphoreType.DMA((71,)),
        ],
        compiler_params=params(20),
        cost_estimate=cost(4_000_000, 11_000_000),
    )(spot, *pieces)


def sum_of(parts):
    whole = parts[0].astype(f32)
    for part in parts[1:]:
        whole = whole + part.astype(f32)
    return whole.astype(bf16)


def turn_around(position, d):
    return lax.rem(position + d, 4)


def first_kernel(spot, kept_ffn, got_ffn, kept_attn, got_attn, *outs):
    for half in range(2):
        for i, d in enumerate((0, 1, 3, 2)):
            at = turn_around(spot[half], d)
            out = outs[4 * half + i]
            for z in range(2):
                for j in range(4):
                    out[z, j, :240] = sum_of([r[z, half, at, j] for r in (kept_ffn, got_ffn)])
                    out[z, j, 240:] = sum_of([r[z, half, at, j] for r in (kept_attn, got_attn)])


def first_sums(spot, kept_ffn, got_ffn, kept_attn, got_attn):
    ins = [p.reshape(2, 2, 4, 4, p.shape[1] // 32, 128) for p in (kept_ffn, got_ffn, kept_attn, got_attn)]
    return pl.pallas_call(
        first_kernel,
        name="first_sums",
        in_specs=[pl.BlockSpec(memory_space=pltpu.SMEM)] + [whole()] * 4,
        out_specs=[whole()] * 8,
        out_shape=[spec(2, 4, 352, 128, bf16)] * 8,
        compiler_params=params(30),
        cost_estimate=cost(3_000_000, 17_000_000),
    )(spot, *ins)


def second_kernel(spot, *refs):
    ins, outs = refs[:8], refs[8:]
    for half in range(2):
        parts = ins[4 * half : 4 * half + 4]
        for i, d in enumerate((0, 1, 3, 2)):
            at = turn_around(spot[1 - half], d)
            for z in range(2):
                outs[4 * half + i][z] = sum_of([r[z, at] for r in parts])


def second_sums(spot, parts):
    return pl.pallas_call(
        second_kernel,
        name="second_sums",
        in_specs=[pl.BlockSpec(memory_space=pltpu.SMEM)] + [whole()] * 8,
        out_specs=[whole()] * 8,
        out_shape=[spec(2, 352, 128, bf16)] * 8,
        compiler_params=params(20),
        cost_estimate=cost(1_000_000, 7_200_000),
    )(spot, *parts)


def third_kernel(place, *refs):
    ins, (mine, other) = refs[:8], refs[8:]
    z = lax.div(place[0], 2)
    for half in range(2):
        parts = ins[4 * half : 4 * half + 4]
        mine[half] = sum_of([r[z] for r in parts])
        other[half] = sum_of([r[1 - z] for r in parts])


def third_sums(place, parts):
    return pl.pallas_call(
        third_kernel,
        name="third_sums",
        in_specs=[pl.BlockSpec(memory_space=pltpu.SMEM)] + [whole()] * 8,
        out_specs=[whole()] * 2,
        out_shape=[spec(2, 352, 128, bf16)] * 2,
        compiler_params=params(10),
        cost_estimate=cost(1_000_000, 1_800_000),
    )(place, *parts)


def fourth_kernel(p0, p1, p2, p3, a, b):
    for half, out in enumerate((a, b)):
        out[...] = sum_of([p0[half], p1[half], p2[half], p3[half]])


def fourth_sums(parts):
    return pl.pallas_call(
        fourth_kernel,
        name="fourth_sums",
        in_specs=[whole()] * 4,
        out_specs=[whole()] * 2,
        out_shape=[spec(352, 128, bf16)] * 2,
        compiler_params=params(10),
        cost_estimate=cost(1_000_000, 900_000),
    )(*parts)


def seq_index(z, x, y):
    return (z % 2 * 4 + x % 4) * 4 + y % 4


def along_xy(dx, dy):
    return [
        (seq_index(z, x, y), seq_index(z, x + dx, y + dy))
        for z in range(2)
        for x in range(4)
        for y in range(4)
    ]


def along_z(step):
    pairs = []
    for s in range(32):
        for f in range(4):
            z = s // 16 * 2 + f // 2
            t = step(z)
            pairs.append((s * 4 + f, (t // 2 * 16 + s % 16) * 4 + t % 2 * 2 + f % 2))
    return pairs


def swap_core(value):
    return lax.ppermute(value, "fsdp", [(0, 1), (1, 0), (2, 3), (3, 2)])


def swap_near(value):
    return lax.ppermute(value, "fsdp", [(0, 2), (1, 3), (2, 0), (3, 1)])


def swap_far(value):
    return lax.ppermute(value, ("seq", "fsdp"), along_z(lambda z: 3 - z))


def swap_hi(value):
    return lax.ppermute(value, "seq", [(s, (s + 16) % 32) for s in range(32)])


def move_x(value, d):
    return lax.ppermute(value, "seq", along_xy(d, 0))


def move_y(value, d):
    return lax.ppermute(value, "seq", along_xy(0, d))


def shifted(value, steps):
    first, last = (max(0, -steps), min(32, 32 - steps))
    return lax.ppermute(value, "seq", [(source, source + steps) for source in range(first, last)])


steps = (1, 3, 2)


def move_first(parts):
    return (
        [parts[0]]
        + [move_x(p, d) for p, d in zip(parts[1:4], steps)]
        + [parts[4]]
        + [move_y(p, d) for p, d in zip(parts[5:8], steps)]
    )


def move_second(parts):
    return (
        [parts[0]]
        + [move_y(p, d) for p, d in zip(parts[1:4], steps)]
        + [parts[4]]
        + [move_x(p, d) for p, d in zip(parts[5:8], steps)]
    )


def together(*groups):
    leaves, tree = jax.tree.flatten(groups)
    return jax.tree.unflatten(tree, lax.optimization_barrier(tuple(leaves)))


def body(
    hidden_in,
    cotangent,
    positions,
    query_weight,
    key_weight,
    value_weight,
    output_weight,
    gate_weight,
    up_weight,
    down_weight,
    norm_in,
    norm_attn,
    norm_ffn_in,
    norm_ffn_out,
    norm_query,
    norm_key,
):
    s = lax.axis_index("seq")
    f = lax.axis_index("fsdp")
    x, y, z_lo, core = s // 4 % 4, s % 4, f // 2, f % 2
    place = f.astype(jnp.int32).reshape(1)
    spot = jnp.stack([x, y]).astype(jnp.int32)
    own = hidden_in[0]
    upstream = cotangent[0]
    offsets = positions[0]

    q_partner = swap_near(query_weight)
    kv = pack(
        [norm_in, norm_attn, norm_ffn_in, norm_ffn_out, norm_query, norm_key],
        key_weight,
        value_weight,
    )
    kv_partner = swap_far(kv)
    q_sibling = swap_core(query_weight)
    kv_sibling = swap_core(kv)
    halo = shifted(own, 1)
    (q_sibling, kv_sibling), (wg, wu) = together(
        (q_sibling, kv_sibling), (gate_weight, up_weight)
    )
    wg_partner, wu_partner = swap_near(wg), swap_far(wu)
    q_diagonal = swap_core(q_partner)
    kv_diagonal = swap_core(kv_partner)
    (q_diagonal, kv_diagonal), (wo, wd) = together(
        (q_diagonal, kv_diagonal), (output_weight, down_weight)
    )
    wo_partner, wd_partner = swap_near(wo), swap_far(wd)
    q_shares = (query_weight, q_sibling, q_partner, q_diagonal)
    kv_shares = (kv, kv_sibling, kv_partner, kv_diagonal)
    tails = [share[160:168] for share in kv_shares]
    tails = [
        jnp.where(
            j // 2 == z_lo,
            jnp.where(j % 2 == core, tails[0], tails[1]),
            jnp.where(j % 2 == core, tails[2], tails[3]),
        )
        for j in range(4)
    ]
    gains = jnp.concatenate([tail[:, :160] for tail in tails], axis=1).astype(f32)
    head_gains = jnp.concatenate([tail[:, :64] for tail in tails], axis=1).astype(f32)

    cosine, sine = rope_tables(offsets)
    column = offsets[:, None]
    normed, q, k, v, q_proj, k_proj = project(
        place, halo, own, gains, head_gains, q_shares, kv_shares, cosine, sine
    )
    attended, level = attend(q, k, v, column)
    attended, (wo, wg, wu, wd) = together(attended, (wo, wg, wu, wd))
    siblings = [swap_core(w) for w in (wo, wg, wu, wd)]
    attended, wo_partner, wg_partner = together(attended, wo_partner, wg_partner)
    attended, wu_partner, wd_partner = together(attended, wu_partner, wd_partner)
    wo_shares = [wo, siblings[0], wo_partner, swap_core(wo_partner)]
    wg_shares = [wg, siblings[1], wg_partner, swap_core(wg_partner)]
    wu_shares = [wu, siblings[2], wu_partner, swap_core(wu_partner)]
    wd_shares = [wd, siblings[3], wd_partner, swap_core(wd_partner)]
    layer_out, back_middle, back_attn, back_attended, gain_mid, kept, sent = middle_part(
        place, own, attended, upstream, gains, wo_shares + wg_shares + wu_shares + wd_shares
    )
    got = swap_core(sent)
    back_q, back_kv, gain_head = attend_back(
        q, k, v, column, level, back_attended, q_proj, k_proj, head_gains, cosine, sine
    )
    back_halo, back_own, kept_attn, sent = weights_part(
        place,
        normed,
        back_q,
        back_kv,
        attended,
        back_attn,
        halo,
        own,
        gain_mid,
        gain_head,
        q_shares + kv_shares,
    )
    got_attn = swap_core(sent)
    first = move_first(first_sums(spot, kept, got, kept_attn, got_attn))
    returned = shifted(back_halo, -1)
    mine, other = third_sums(place, move_second(second_sums(spot, first)))
    a, b = fourth_sums([mine, swap_near(other), swap_far(other), swap_hi(mine)])
    a = jnp.stack([a] + [move_y(a, d) for d in (1, 2, 3)])
    b = jnp.stack([b] + [move_x(b, d) for d in (1, 2, 3)])
    a, b = together(a, b)
    pieces = [a] + [move_x(a, d) for d in (1, 2, 3)] + [b] + [move_y(b, d) for d in (1, 2, 3)]
    grad_q, grad_k, grad_v, grad_o, grad_g, grad_u, grad_d, tile = unpack(spot, pieces)
    grad_in = finish(own, back_own, returned, back_middle, gains)
    wide = jnp.concatenate([tile[0:4], tile[4:8, :32]], axis=1)
    return (
        layer_out[None],
        grad_in[None],
        grad_q,
        grad_k,
        grad_v,
        grad_o,
        grad_g,
        grad_u,
        grad_d,
        wide[0],
        wide[1],
        wide[2],
        wide[3],
        tile[8, :64],
        tile[9, :64],
    )


def solution(mesh):
    three = P("fsdp", "seq", None)
    two = P("fsdp", None)
    one = P("fsdp")
    return jax.shard_map(
        body,
        mesh=mesh,
        in_specs=(three, three, P("fsdp", "seq")) + (two,) * 7 + (one,) * 6,
        out_specs=(three, three) + (two,) * 7 + (one,) * 6,
        check_vma=False,
    )
```

profile of v0, /device:TPU:102, one launch (start us, length us, event | category | flops | bytes accessed | tf_op | source)
XLA Modules:
  0.0 278.6 jit_solution(7442220579807459436)
XLA Ops:
  8.3 3.5 %collective-permute-start = (bf16[512,640]{1,0:T(8,128)(2,1)}, bf16[512,640]{1,0:T(8,128)(2,1)S(1)}, u32[]{:S(2)}, u32[]{:S(2)}) collective-permute-start(bf16[512,640]{1,0:T(8,128)(2,1)} %bitcast.32), channel_id=1, source_target_pairs={{0,4},{4,8},{8,12},{12,16},{16,20},{20,24},{24,28},{28,32},{32,36}... | collective-permute-start | bytes 1966088 | tf_op jit(solution)/shard_map/ppermute | solution.py:868
  22.9 6.3 %collective-permute-done.halo = bf16[512,640]{1,0:T(8,128)(2,1)S(1)} collective-permute-done((bf16[512,640]{1,0:T(8,128)(2,1)}, bf16[512,640]{1,0:T(8,128)(2,1)S(1)}, u32[]{:S(2)}, u32[]{:S(2)}) %collective-permute-start) | collective-permute-done | bytes 655392 | tf_op jit(solution)/shard_map/ppermute | solution.py:868
  29.1 5.4 %project.1 = (bf16[1024,640]{1,0:T(8,128)(2,1)S(1)}, bf16[512,1024]{1,0:T(8,128)(2,1)S(1)}, bf16[1024,256]{1,0:T(8,128)(2,1)S(1)}, bf16[1024,256]{1,0:T(8,128)(2...) custom-call(s32[1]{0:T(128)} %bitcast.place, bf16[512,640]{1,0:T(8,128)(2,1)S(1)} %collective-permute-done.halo, ...), custom_call_target="tpu_custom_call" | custom-call | flops 1350000000 | bytes 9000000 | tf_op jit(solution)/shard_map/project/pallas_call | solution.py:186
  34.6 3.9 %attend.1 = (bf16[512,1024]{1,0:T(8,128)(2,1)S(1)}, f32[4,512,1]{2,1,0:T(8,128)S(1)}) custom-call(bf16[512,1024]{1,0:T(8,128)(2,1)S(1)} %get-tuple-element.90.q, bf16[1024,256]{1,0:T(8,128)(2,1)S(1)} %get-tuple-element.91.k, bf16[1024,256]{1,0:T(8,128)(2,1)S(1)} %get-tuple-element.92.v, s32[512,1]{1,0:T(8,128)S(1)} %copy.31.offsets), custom_call_target="tpu_custom_call" | custom-call | flops 1700000000 | bytes 4000000 | tf_op jit(solution)/shard_map/attend/pallas_call | solution.py:253
  42.3 8.3 %collective-permute-done.10.d2 = bf16[512,640]{1,0:T(8,128)(2,1)S(1)} collective-permute-done((bf16[512,640]{1,0:T(8,128)(2,1)}, bf16[512,640]{1,0:T(8,128)(2,1)S(1)}, u32[]{:S(2)}, u32[]{:S(2)}) %collective-permute-start.10) | collective-permute-done | bytes 655392 | tf_op jit(solution)/shard_map/ppermute | solution.py:851
  56.5 38.9 %middle_part.1 = (bf16[512,640]{1,0:T(8,128)(2,1)}, f32[512,640]{1,0:T(8,128)}, bf16[512,640]{1,0:T(8,128)(2,1)S(1)}, bf16[512,1024]{1,0:T(8,128)(2,1)}, f32[8,6...) custom-call(s32[1]{0:T(128)} %bitcast.place, bf16[512,640]{1,0:T(8,128)(2,1)S(1)} %bitcast.34, ...), custom_call_target="tpu_custom_call" | custom-call | flops 13400000512 | bytes 23000000 | tf_op jit(solution)/shard_map/middle_part/pallas_call | solution.py:396
  96.9 9.2 %attend_back.1 = (bf16[512,1024]{1,0:T(8,128)(2,1)S(1)}, bf16[1024,512]{1,0:T(8,128)(2,1)S(1)}, f32[8,256]{1,0:T(8,128)S(1)}) custom-call(bf16[512,1024]{1,0:T(8,128)(2,1)S(1)} %get-tuple-element.90.q, bf16[1024,256]{1,0:T(8,128)(2,1)S(1)} %get-tuple-element.91.k, bf16[1024,256]{1,0:T(8,128)(2,1)S(1)} %get-tuple-element.92.v, s32[512,1]{1,0:T(8,128)S(1)} %copy.31.offsets, ...), custom_call_target="tpu_custom_call" | custom-call | flops 4300000256 | bytes 10000000 | tf_op jit(solution)/shard_map/attend_back/pallas_call | solution.py:496
  107.2 7.5 %weights_part.1 = (bf16[512,640]{1,0:T(8,128)(2,1)S(1)}, f32[512,640]{1,0:T(8,128)S(1)}, bf16[2,3584,128]{2,1,0:T(8,128)(2,1)S(1)}, bf16[2,3584,128]{2,1,0:T(8,128)(2,1)}) custom-call(s32[1]{0:T(128)} %bitcast.place, bf16[1024,640]{1,0:T(8,128)(2,1)S(1)} %get-tuple-element.110.normed, bf16[512,1024]{1,0:T(8,128)(2,1)S(1)} %get-tuple-element.115.back_q, ...), custom_call_target="tpu_custom_call" | custom-call | flops 3400000000 | bytes 14000000 | tf_op jit(solution)/shard_map/weights_part/pallas_call | solution.py:602
  116.0 3.7 %collective-permute-done.21 = bf16[2,3584,128]{2,1,0:T(8,128)(2,1)} collective-permute-done((bf16[2,3584,128]{2,1,0:T(8,128)(2,1)}, bf16[2,3584,128]{2,1,0:T(8,128)(2,1)}, u32[]{:S(2)}, u32[]{:S(2)}) %collective-permute-start.21) | collective-permute-done | bytes 1835040 | tf_op jit(solution)/shard_map/ppermute | solution.py:843
  121.8 4.0 %first_sums.1 = (bf16[2,4,352,128]{3,2,1,0:T(8,128)(2,1)S(1)}, bf16[2,4,352,128]{3,2,1,0:T(8,128)(2,1)S(1)}, bf16[2,4,352,128]{3,2,1,0:T(8,128)(2,1)S(1)}, bf16[...) custom-call(s32[2]{0:T(128)S(1)} %pad_add_fusion.spot, ...), custom_call_target="tpu_custom_call" | custom-call | flops 3000000 | bytes 17000000 | tf_op jit(solution)/shard_map/first_sums/pallas_call | solution.py:748
  125.8 10.9 %collective-permute-start.22 = (bf16[2,4,352,128]{3,2,1,0:T(8,128)(2,1)S(1)}, bf16[2,4,352,128]{3,2,1,0:T(8,128)(2,1)S(1)}, u32[]{:S(2)}, u32[]{:S(2)}) collective-permute-start(bf16[2,4,352,128]{3,2,1,0:T(8,128)(2,1)S(1)} %get-tuple-element.128), channel_id=1, source_target_pairs={{0,16},{4,20},{8,24},{12,28},{16,32},{20,36},{24,40},{28,44},{32,4... | collective-permute-start | bytes 2162696 | tf_op jit(solution)/shard_map/ppermute | solution.py:859
  138.2 3.2 %collective-permute-start.26 = (bf16[2,4,352,128]{3,2,1,0:T(8,128)(2,1)S(1)}, bf16[2,4,352,128]{3,2,1,0:T(8,128)(2,1)S(1)}, u32[]{:S(2)}, u32[]{:S(2)}) collective-permute-start(bf16[2,4,352,128]{3,2,1,0:T(8,128)(2,1)S(1)} %get-tuple-element.133), channel_id=1, source_target_pairs={{0,12},{4,0},{8,4},{12,8},{16,28},{20,16},{24,20},{28,24},{32,44},... | collective-permute-start | bytes 2162696 | tf_op jit(solution)/shard_map/ppermute | solution.py:863
  141.4 26.6 %collective-permute-done.22.refs_1_ = bf16[2,4,352,128]{3,2,1,0:T(8,128)(2,1)S(1)} collective-permute-done((bf16[2,4,352,128]{3,2,1,0:T(8,128)(2,1)S(1)}, bf16[2,4,352,128]{3,2,1,0:T(8,128)(2,1)S(1)}, u32[]{:S(2)}, u32[]{:S(2)}) %collective-permute-start.22) | collective-permute-done | bytes 720928 | tf_op jit(solution)/shard_map/ppermute | solution.py:859
  172.0 15.4 %collective-permute-done.27.refs_7_ = bf16[2,4,352,128]{3,2,1,0:T(8,128)(2,1)S(1)} collective-permute-done((bf16[2,4,352,128]{3,2,1,0:T(8,128)(2,1)S(1)}, bf16[2,4,352,128]{3,2,1,0:T(8,128)(2,1)S(1)}, u32[]{:S(2)}, u32[]{:S(2)}) %collective-permute-start.27) | collective-permute-done | bytes 720928 | tf_op jit(solution)/shard_map/ppermute | solution.py:863
  191.9 3.7 %collective-permute-start.31 = (bf16[2,352,128]{2,1,0:T(8,128)(2,1)S(1)}, bf16[2,352,128]{2,1,0:T(8,128)(2,1)S(1)}, u32[]{:S(2)}, u32[]{:S(2)}) collective-permute-start(bf16[2,352,128]{2,1,0:T(8,128)(2,1)S(1)} %get-tuple-element.140), channel_id=1, source_target_pairs={{0,16},{4,20},{8,24},{12,28},{16,32},{20,36},{24,40},{28,44},{32,4... | collective-permute-start | bytes 540680 | tf_op jit(solution)/shard_map/ppermute | solution.py:859
  195.6 3.6 %collective-permute-done.28.refs_1_ = bf16[2,352,128]{2,1,0:T(8,128)(2,1)S(1)} collective-permute-done((bf16[2,352,128]{2,1,0:T(8,128)(2,1)S(1)}, bf16[2,352,128]{2,1,0:T(8,128)(2,1)S(1)}, u32[]{:S(2)}, u32[]{:S(2)}) %collective-permute-start.28) | collective-permute-done | bytes 180256 | tf_op jit(solution)/shard_map/ppermute | solution.py:863
  203.0 3.2 %collective-permute-done.33.refs_7_ = bf16[2,352,128]{2,1,0:T(8,128)(2,1)S(1)} collective-permute-done((bf16[2,352,128]{2,1,0:T(8,128)(2,1)S(1)}, bf16[2,352,128]{2,1,0:T(8,128)(2,1)S(1)}, u32[]{:S(2)}, u32[]{:S(2)}) %collective-permute-start.33) | collective-permute-done | bytes 180256 | tf_op jit(solution)/shard_map/ppermute | solution.py:859
  210.1 3.5 %collective-permute-done.36.p3 = bf16[2,352,128]{2,1,0:T(8,128)(2,1)S(1)} collective-permute-done((bf16[2,352,128]{2,1,0:T(8,128)(2,1)S(1)}, bf16[2,352,128]{2,1,0:T(8,128)(2,1)S(1)}, u32[]{:S(2)}, u32[]{:S(2)}) %collective-permute-start.36) | collective-permute-done | bytes 180256 | tf_op jit(solution)/shard_map/ppermute | solution.py:855
  219.1 3.7 %collective-permute-start.19 = (bf16[512,640]{1,0:T(8,128)(2,1)S(1)}, bf16[512,640]{1,0:T(8,128)(2,1)S(1)}, u32[]{:S(2)}, u32[]{:S(2)}) collective-permute-start(bf16[512,640]{1,0:T(8,128)(2,1)S(1)} %copy-done.19), channel_id=1, source_target_pairs={{4,0},{8,4},{12,8},{16,12},{20,16},{24,20},{28,24},{32,28},{36,32}... | collective-permute-start | bytes 1966088 | tf_op jit(solution)/shard_map/ppermute | solution.py:868
  223.0 6.2 %collective-permute-start.41 = (bf16[352,128]{1,0:T(8,128)(2,1)S(1)}, bf16[352,128]{1,0:T(8,128)(2,1)S(1)}, u32[]{:S(2)}, u32[]{:S(2)}) collective-permute-start(bf16[352,128]{1,0:T(8,128)(2,1)S(1)} %get-tuple-element.146), channel_id=1, source_target_pairs={{0,32},{4,36},{8,40},{12,44},{16,48},{20,52},{24,56},{28,60},{32,0... | collective-permute-start | bytes 270344 | tf_op jit(solution)/shard_map/ppermute | solution.py:859
  230.1 13.3 %collective-permute-done.42 = bf16[352,128]{1,0:T(8,128)(2,1)S(1)} collective-permute-done((bf16[352,128]{1,0:T(8,128)(2,1)S(1)}, bf16[352,128]{1,0:T(8,128)(2,1)S(1)}, u32[]{:S(2)}, u32[]{:S(2)}) %collective-permute-start.42) | collective-permute-done | bytes 90144 | tf_op jit(solution)/shard_map/ppermute | solution.py:859
  246.9 12.2 %collective-permute-done.45.a3 = bf16[4,352,128]{2,1,0:T(8,128)(2,1)S(1)} collective-permute-done((bf16[4,352,128]{2,1,0:T(8,128)(2,1)S(1)}, bf16[4,352,128]{2,1,0:T(8,128)(2,1)S(1)}, u32[]{:S(2)}, u32[]{:S(2)}) %collective-permute-start.45) | collective-permute-done | bytes 360480 | tf_op jit(solution)/shard_map/ppermute | solution.py:859
  261.0 7.6 %collective-permute-done.46.b1 = bf16[4,352,128]{2,1,0:T(8,128)(2,1)S(1)} collective-permute-done((bf16[4,352,128]{2,1,0:T(8,128)(2,1)S(1)}, bf16[4,352,128]{2,1,0:T(8,128)(2,1)S(1)}, u32[]{:S(2)}, u32[]{:S(2)}) %collective-permute-start.46) | collective-permute-done | bytes 360480 | tf_op jit(solution)/shard_map/ppermute | solution.py:863
  268.6 8.7 %unpack.1 = (f32[160,1024]{1,0:T(8,128)}, f32[160,256]{1,0:T(8,128)}, f32[160,256]{1,0:T(8,128)}, f32[256,640]{1,0:T(8,128)}, f32[160,2048]{1,0:T(8,128)}, /*ind...) custom-call(s32[2]{0:T(128)S(1)} %pad_add_fusion.spot, bf16[4,352,128]{2,1,0:T(8,128)(2,1)S(1)} %pad_maximum_fusion.a0, ...), custom_call_target="tpu_custom_call" | custom-call | flops 4000000 | bytes 11000000 | tf_op jit(solution)/shard_map/unpack/pallas_call | solution.py:707
  (193 shorter events, 64.1 us)
Async XLA Ops:
  0.7 14.5 %collective-permute-start.4 = (bf16[160,1024]{1,0:T(8,128)(2,1)}, bf16[160,1024]{1,0:T(8,128)(2,1)S(1)}, u32[]{:S(2)}, u32[]{:S(2)}) collective-permute-start(bf16[160,1024]{1,0:T(8,128)(2,1)} %q0.3), channel_id=1, source_target_pairs={{0,2},{1,3},{2,0},{3,1},{4,6},{5,7},{6,4},{7,5},{8,10},{9,11},{10,... | collective-permute-start | bytes 983048 | tf_op jit(solution)/shard_map/ppermute | solution.py:847
  8.3 20.8 %collective-permute-start = (bf16[512,640]{1,0:T(8,128)(2,1)}, bf16[512,640]{1,0:T(8,128)(2,1)S(1)}, u32[]{:S(2)}, u32[]{:S(2)}) collective-permute-start(bf16[512,640]{1,0:T(8,128)(2,1)} %bitcast.32), channel_id=1, source_target_pairs={{0,4},{4,8},{8,12},{12,16},{16,20},{20,24},{24,28},{28,32},{32,36}... | collective-permute-start | bytes 1966088 | tf_op jit(solution)/shard_map/ppermute | solution.py:868
  17.8 24.0 %collective-permute-start.8 = (bf16[160,2048]{1,0:T(8,128)(2,1)}, bf16[160,2048]{1,0:T(8,128)(2,1)S(1)}, u32[]{:S(2)}, u32[]{:S(2)}) collective-permute-start(bf16[160,2048]{1,0:T(8,128)(2,1)} %g0.2), channel_id=1, source_target_pairs={{0,2},{1,3},{2,0},{3,1},{4,6},{5,7},{6,4},{7,5},{8,10},{9,11},{10,... | collective-permute-start | bytes 1966088 | tf_op jit(solution)/shard_map/ppermute | solution.py:847
  18.8 23.4 %collective-permute-start.9 = (bf16[160,2048]{1,0:T(8,128)(2,1)}, bf16[160,2048]{1,0:T(8,128)(2,1)S(1)}, u32[]{:S(2)}, u32[]{:S(2)}) collective-permute-start(bf16[160,2048]{1,0:T(8,128)(2,1)} %u0), channel_id=1, source_target_pairs={{0,66},{1,67},{2,64},{3,65},{4,70},{5,71},{6,68},{7,69},{8,74},{9,... | collective-permute-start | bytes 1966088 | tf_op jit(solution)/shard_map/ppermute | solution.py:851
  21.5 20.2 %collective-permute-start.7 = (bf16[256,640]{1,0:T(8,128)(2,1)S(1)}, bf16[256,640]{1,0:T(8,128)(2,1)S(1)}, u32[]{:S(2)}, u32[]{:S(2)}) collective-permute-start(bf16[256,640]{1,0:T(8,128)(2,1)S(1)} %copy-done.22), channel_id=1, source_target_pairs={{0,2},{1,3},{2,0},{3,1},{4,6},{5,7},{6,4},{7,5},{8,10},{9,11},{10,... | collective-permute-start | bytes 983048 | tf_op jit(solution)/shard_map/ppermute | solution.py:847
  22.0 28.7 %collective-permute-start.10 = (bf16[512,640]{1,0:T(8,128)(2,1)}, bf16[512,640]{1,0:T(8,128)(2,1)S(1)}, u32[]{:S(2)}, u32[]{:S(2)}) collective-permute-start(bf16[512,640]{1,0:T(8,128)(2,1)} %d0), channel_id=1, source_target_pairs={{0,66},{1,67},{2,64},{3,65},{4,70},{5,71},{6,68},{7,69},{8,74},{9,... | collective-permute-start | bytes 1966088 | tf_op jit(solution)/shard_map/ppermute | solution.py:851
  95.4 24.3 %collective-permute-start.20 = (bf16[2,7680,128]{2,1,0:T(8,128)(2,1)}, bf16[2,7680,128]{2,1,0:T(8,128)(2,1)}, u32[]{:S(2)}, u32[]{:S(2)}) collective-permute-start(bf16[2,7680,128]{2,1,0:T(8,128)(2,1)} %get-tuple-element.124), channel_id=1, source_target_pairs={{0,1},{1,0},{2,3},{3,2},{4,5},{5,4},{6,7},{7,6},{8,9},{9,8},{10,11... | collective-permute-start | bytes 11796488 | tf_op jit(solution)/shard_map/ppermute | solution.py:843
  125.8 42.2 %collective-permute-start.22 = (bf16[2,4,352,128]{3,2,1,0:T(8,128)(2,1)S(1)}, bf16[2,4,352,128]{3,2,1,0:T(8,128)(2,1)S(1)}, u32[]{:S(2)}, u32[]{:S(2)}) collective-permute-start(bf16[2,4,352,128]{3,2,1,0:T(8,128)(2,1)S(1)} %get-tuple-element.128), channel_id=1, source_target_pairs={{0,16},{4,20},{8,24},{12,28},{16,32},{20,36},{24,40},{28,44},{32,4... | collective-permute-start | bytes 2162696 | tf_op jit(solution)/shard_map/ppermute | solution.py:859
  136.7 34.8 %collective-permute-start.23 = (bf16[2,4,352,128]{3,2,1,0:T(8,128)(2,1)S(1)}, bf16[2,4,352,128]{3,2,1,0:T(8,128)(2,1)S(1)}, u32[]{:S(2)}, u32[]{:S(2)}) collective-permute-start(bf16[2,4,352,128]{3,2,1,0:T(8,128)(2,1)S(1)} %get-tuple-element.129), channel_id=1, source_target_pairs={{0,48},{4,52},{8,56},{12,60},{16,0},{20,4},{24,8},{28,12},{32,16},... | collective-permute-start | bytes 2162696 | tf_op jit(solution)/shard_map/ppermute | solution.py:859
  136.7 34.8 %collective-permute-start.24 = (bf16[2,4,352,128]{3,2,1,0:T(8,128)(2,1)S(1)}, bf16[2,4,352,128]{3,2,1,0:T(8,128)(2,1)S(1)}, u32[]{:S(2)}, u32[]{:S(2)}) collective-permute-start(bf16[2,4,352,128]{3,2,1,0:T(8,128)(2,1)S(1)} %get-tuple-element.130), channel_id=1, source_target_pairs={{0,32},{4,36},{8,40},{12,44},{16,48},{20,52},{24,56},{28,60},{32,0... | collective-permute-start | bytes 2162696 | tf_op jit(solution)/shard_map/ppermute | solution.py:859
  138.2 33.2 %collective-permute-start.25 = (bf16[2,4,352,128]{3,2,1,0:T(8,128)(2,1)S(1)}, bf16[2,4,352,128]{3,2,1,0:T(8,128)(2,1)S(1)}, u32[]{:S(2)}, u32[]{:S(2)}) collective-permute-start(bf16[2,4,352,128]{3,2,1,0:T(8,128)(2,1)S(1)} %get-tuple-element.132), channel_id=1, source_target_pairs={{0,4},{4,8},{8,12},{12,0},{16,20},{20,24},{24,28},{28,16},{32,36},... | collective-permute-start | bytes 2162696 | tf_op jit(solution)/shard_map/ppermute | solution.py:863
  138.2 33.8 %collective-permute-start.26 = (bf16[2,4,352,128]{3,2,1,0:T(8,128)(2,1)S(1)}, bf16[2,4,352,128]{3,2,1,0:T(8,128)(2,1)S(1)}, u32[]{:S(2)}, u32[]{:S(2)}) collective-permute-start(bf16[2,4,352,128]{3,2,1,0:T(8,128)(2,1)S(1)} %get-tuple-element.133), channel_id=1, source_target_pairs={{0,12},{4,0},{8,4},{12,8},{16,28},{20,16},{24,20},{28,24},{32,44},... | collective-permute-start | bytes 2162696 | tf_op jit(solution)/shard_map/ppermute | solution.py:863
  168.0 19.3 %collective-permute-start.27 = (bf16[2,4,352,128]{3,2,1,0:T(8,128)(2,1)S(1)}, bf16[2,4,352,128]{3,2,1,0:T(8,128)(2,1)S(1)}, u32[]{:S(2)}, u32[]{:S(2)}) collective-permute-start(bf16[2,4,352,128]{3,2,1,0:T(8,128)(2,1)S(1)} %get-tuple-element.134), channel_id=1, source_target_pairs={{0,8},{4,12},{8,0},{12,4},{16,24},{20,28},{24,16},{28,20},{32,40},... | collective-permute-start | bytes 2162696 | tf_op jit(solution)/shard_map/ppermute | solution.py:863
  216.0 13.2 %collective-permute-start.38 = (bf16[352,128]{1,0:T(8,128)(2,1)S(1)}, bf16[352,128]{1,0:T(8,128)(2,1)S(1)}, u32[]{:S(2)}, u32[]{:S(2)}) collective-permute-start(bf16[352,128]{1,0:T(8,128)(2,1)S(1)} %get-tuple-element.145), channel_id=1, source_target_pairs={{0,8},{4,12},{8,0},{12,4},{16,24},{20,28},{24,16},{28,20},{32,40},... | collective-permute-start | bytes 270344 | tf_op jit(solution)/shard_map/ppermute | solution.py:863
  218.9 11.2 %collective-permute-start.37 = (bf16[352,128]{1,0:T(8,128)(2,1)S(1)}, bf16[352,128]{1,0:T(8,128)(2,1)S(1)}, u32[]{:S(2)}, u32[]{:S(2)}) collective-permute-start(bf16[352,128]{1,0:T(8,128)(2,1)S(1)} %get-tuple-element.145), channel_id=1, source_target_pairs={{0,4},{4,8},{8,12},{12,0},{16,20},{20,24},{24,28},{28,16},{32,36},... | collective-permute-start | bytes 270344 | tf_op jit(solution)/shard_map/ppermute | solution.py:863
  219.1 27.8 %collective-permute-start.19 = (bf16[512,640]{1,0:T(8,128)(2,1)S(1)}, bf16[512,640]{1,0:T(8,128)(2,1)S(1)}, u32[]{:S(2)}, u32[]{:S(2)}) collective-permute-start(bf16[512,640]{1,0:T(8,128)(2,1)S(1)} %copy-done.19), channel_id=1, source_target_pairs={{4,0},{8,4},{12,8},{16,12},{20,16},{24,20},{28,24},{32,28},{36,32}... | collective-permute-start | bytes 1966088 | tf_op jit(solution)/shard_map/ppermute | solution.py:868
  222.8 20.7 %collective-permute-start.42 = (bf16[352,128]{1,0:T(8,128)(2,1)S(1)}, bf16[352,128]{1,0:T(8,128)(2,1)S(1)}, u32[]{:S(2)}, u32[]{:S(2)}) collective-permute-start(bf16[352,128]{1,0:T(8,128)(2,1)S(1)} %get-tuple-element.146), channel_id=1, source_target_pairs={{0,48},{4,52},{8,56},{12,60},{16,0},{20,4},{24,8},{28,12},{32,16},... | collective-permute-start | bytes 270344 | tf_op jit(solution)/shard_map/ppermute | solution.py:859
  223.0 20.5 %collective-permute-start.41 = (bf16[352,128]{1,0:T(8,128)(2,1)S(1)}, bf16[352,128]{1,0:T(8,128)(2,1)S(1)}, u32[]{:S(2)}, u32[]{:S(2)}) collective-permute-start(bf16[352,128]{1,0:T(8,128)(2,1)S(1)} %get-tuple-element.146), channel_id=1, source_target_pairs={{0,32},{4,36},{8,40},{12,44},{16,48},{20,52},{24,56},{28,60},{32,0... | collective-permute-start | bytes 270344 | tf_op jit(solution)/shard_map/ppermute | solution.py:859
  229.2 14.3 %collective-permute-start.40 = (bf16[352,128]{1,0:T(8,128)(2,1)S(1)}, bf16[352,128]{1,0:T(8,128)(2,1)S(1)}, u32[]{:S(2)}, u32[]{:S(2)}) collective-permute-start(bf16[352,128]{1,0:T(8,128)(2,1)S(1)} %get-tuple-element.146), channel_id=1, source_target_pairs={{0,16},{4,20},{8,24},{12,28},{16,32},{20,36},{24,40},{28,44},{32,4... | collective-permute-start | bytes 270344 | tf_op jit(solution)/shard_map/ppermute | solution.py:859
  243.5 15.5 %collective-permute-start.45 = (bf16[4,352,128]{2,1,0:T(8,128)(2,1)S(1)}, bf16[4,352,128]{2,1,0:T(8,128)(2,1)S(1)}, u32[]{:S(2)}, u32[]{:S(2)}) collective-permute-start(bf16[4,352,128]{2,1,0:T(8,128)(2,1)S(1)} %pad_maximum_fusion.a0), channel_id=1, source_target_pairs={{0,48},{4,52},{8,56},{12,60},{16,0},{20,4},{24,8},{28,12},{32,16},... | collective-permute-start | bytes 1081352 | tf_op jit(solution)/shard_map/ppermute | solution.py:859
  243.6 17.4 %collective-permute-start.44 = (bf16[4,352,128]{2,1,0:T(8,128)(2,1)S(1)}, bf16[4,352,128]{2,1,0:T(8,128)(2,1)S(1)}, u32[]{:S(2)}, u32[]{:S(2)}) collective-permute-start(bf16[4,352,128]{2,1,0:T(8,128)(2,1)S(1)} %pad_maximum_fusion.a0), channel_id=1, source_target_pairs={{0,32},{4,36},{8,40},{12,44},{16,48},{20,52},{24,56},{28,60},{32,0... | collective-permute-start | bytes 1081352 | tf_op jit(solution)/shard_map/ppermute | solution.py:859
  244.6 16.4 %collective-permute-start.43 = (bf16[4,352,128]{2,1,0:T(8,128)(2,1)S(1)}, bf16[4,352,128]{2,1,0:T(8,128)(2,1)S(1)}, u32[]{:S(2)}, u32[]{:S(2)}) collective-permute-start(bf16[4,352,128]{2,1,0:T(8,128)(2,1)S(1)} %pad_maximum_fusion.a0), channel_id=1, source_target_pairs={{0,16},{4,20},{8,24},{12,28},{16,32},{20,36},{24,40},{28,44},{32,4... | collective-permute-start | bytes 1081352 | tf_op jit(solution)/shard_map/ppermute | solution.py:859
  246.9 14.2 %collective-permute-start.48 = (bf16[4,352,128]{2,1,0:T(8,128)(2,1)S(1)}, bf16[4,352,128]{2,1,0:T(8,128)(2,1)S(1)}, u32[]{:S(2)}, u32[]{:S(2)}) collective-permute-start(bf16[4,352,128]{2,1,0:T(8,128)(2,1)S(1)} %pad_maximum_fusion.1.b0), channel_id=1, source_target_pairs={{0,12},{4,0},{8,4},{12,8},{16,28},{20,16},{24,20},{28,24},{32,44},... | collective-permute-start | bytes 1081352 | tf_op jit(solution)/shard_map/ppermute | solution.py:863
  246.9 14.2 %collective-permute-start.47 = (bf16[4,352,128]{2,1,0:T(8,128)(2,1)S(1)}, bf16[4,352,128]{2,1,0:T(8,128)(2,1)S(1)}, u32[]{:S(2)}, u32[]{:S(2)}) collective-permute-start(bf16[4,352,128]{2,1,0:T(8,128)(2,1)S(1)} %pad_maximum_fusion.1.b0), channel_id=1, source_target_pairs={{0,8},{4,12},{8,0},{12,4},{16,24},{20,28},{24,16},{28,20},{32,40},... | collective-permute-start | bytes 1081352 | tf_op jit(solution)/shard_map/ppermute | solution.py:863
  (66 other events, 671.0 us)
where the time goes:
time: 281 us; the launch traced here: 279 us
  waiting for transfers between devices  118 us (42%)
  Pallas kernels  81.1 us (29%)
  starting transfers between devices  57.1 us (20%)
  local copies, waits for them, and re-layouts  16.4 us (6%)
  other arithmetic  3.5 us (1%)
    ppermute x12, waiting for transfers between devices, move_x(): return lax.ppermute(value, 'seq', along_xy(d, 0))  62.3 us
    pallas_call x1, Pallas kernels, middle_part(): pl.pallas_call(middle_kernel, name='middle_part', in_specs=[pl.BlockSpec(...  38.9 us
    ppermute x12, waiting for transfers between devices, move_y(): return lax.ppermute(value, 'seq', along_xy(0, d))  27.2 us
    ppermute x12, starting transfers between devices, move_x(): return lax.ppermute(value, 'seq', along_xy(d, 0))  26.6 us
    unnamed x82, local copies, waits for them, and re-layouts  13.9 us
    ppermute x12, starting transfers between devices, move_y(): return lax.ppermute(value, 'seq', along_xy(0, d))  10.2 us
    ppermute x4, waiting for transfers between devices, swap_far(): return lax.ppermute(value, ('seq', 'fsdp'), along_z(lambda z: 3 - z))  10.2 us
    pallas_call x1, Pallas kernels, attend_back(): pl.pallas_call(attend_back_kernel, name='attend_back', grid=(2,), in_spec...  9.18 us
  transfers between devices with their start and end apart: 49, of which 22 were waited for; matrix products, arithmetic and copies ran while one was open for 2% of the time, Pallas kernels for 10%

commit v1 on v0

--- a/solution.py
+++ b/solution.py
@@ -115,7 +115,7 @@
     return pl.pallas_call(
         pack_kernel,
         name="pack",
-        in_specs=[pl.BlockSpec(memory_space=pl.ANY)] * 6 + [whole()] * 2,
+        in_specs=[pl.BlockSpec(memory_space=pltpu.HBM)] * 6 + [whole()] * 2,
         out_specs=whole(),
         out_shape=spec(176, 512, bf16),
         scratch_shapes=[pltpu.VMEM(row.shape, bf16) for row in rows]
@@ -194,7 +194,7 @@
             pl.BlockSpec((8, 640), fixed),
             pl.BlockSpec((8, 256), fixed),
         ]
-        + [pl.BlockSpec(memory_space=pl.ANY)] * 8
+        + [pl.BlockSpec(memory_space=pltpu.HBM)] * 8
         + [pl.BlockSpec((256, 128), row)] * 2,
         out_specs=[
             pl.BlockSpec((256, 640), row),
@@ -398,8 +398,8 @@
         name="middle_part",
         in_specs=[pl.BlockSpec(memory_space=pltpu.SMEM)]
         + [whole()] * 4
-        + [pl.BlockSpec(memory_space=pl.ANY)] * 16,
-        out_specs=[whole()] * 5 + [pl.BlockSpec(memory_space=pl.ANY)] * 2,
+        + [pl.BlockSpec(memory_space=pltpu.HBM)] * 16,
+        out_specs=[whole()] * 5 + [pl.BlockSpec(memory_space=pltpu.HBM)] * 2,
         out_shape=[
             spec(512, 640, bf16),
             spec(512, 640, f32),
@@ -443,16 +443,26 @@
     head_gains,
     cosine,
     sine,
+    place,
+    kv0,
+    kv1,
+    kv2,
+    kv3,
     back_q,
     back_kv,
     gain_grads,
+    back_halo,
     sum_k,
     sum_v,
+    wkv,
+    semaphores,
 ):
     t = pl.program_id(0)
 
     @pl.when(t == 0)
     def _():
+        for copy in assemble((kv0, kv1, kv2, kv3), wkv, place[0], semaphores, 0):
+            copy.wait()
         sum_k[...] = jnp.zeros_like(sum_k)
         sum_v[...] = jnp.zeros_like(sum_v)
         gain_grads[...] = jnp.zeros_like(gain_grads)
@@ -486,10 +496,11 @@
         gain_grads[1:2] = jnp.sum(kp * r * e, axis=0, keepdims=True)
         back_kv[:, :256] = norm_back(kp, r, head_gains[5:6], e).astype(bf16)
         back_kv[:, 256:] = sum_v[...].astype(bf16)
+        back_halo[...] = dot(back_kv[:512, :], wkv[...], rows_both).astype(bf16)
 
 
 def attend_back(
-    q, k, v, offsets, level, back_attended, q_proj, k_proj, head_gains, cosine, sine
+    q, k, v, offsets, level, back_attended, q_proj, k_proj, head_gains, cosine, sine, place, shares
 ):
     row = lambda i: (i, 0)
     fixed = lambda i: (0, 0)
@@ -509,17 +520,32 @@
             pl.BlockSpec((8, 256), fixed),
             pl.BlockSpec((1024, 128), fixed),
             pl.BlockSpec((1024, 128), fixed),
-        ],
+            pl.BlockSpec(memory_space=pltpu.SMEM),
+        ]
+        + [pl.BlockSpec(memory_space=pltpu.HBM)] * 4,
         out_specs=[
             pl.BlockSpec((256, 1024), row),
             pl.BlockSpec((1024, 512), fixed),
             pl.BlockSpec((8, 256), fixed),
-        ],
-        out_shape=[spec(512, 1024, bf16), spec(1024, 512, bf16), spec(8, 256, f32)],
-        scratch_shapes=[pltpu.VMEM((1024, 256), f32), pltpu.VMEM((1024, 256), f32)],
+            pl.BlockSpec((512, 640), fixed),
+        ],
+        out_shape=[
+            spec(512, 1024, bf16),
+            spec(1024, 512, bf16),
+            spec(8, 256, f32),
+            spec(512, 640, bf16),
+        ],
+        scratch_shapes=[
+            pltpu.VMEM((1024, 256), f32),
+            pltpu.VMEM((1024, 256), f32),
+            pltpu.VMEM((640, 512), bf16),
+            pltpu.SemaphoreType.DMA((4,)),
+        ],
         compiler_params=params(30),
         cost_estimate=cost(4_300_000_000, 10_000_000, 2_000_000),
-    )(q, k, v, offsets, level, back_attended, q_proj, k_proj, head_gains, cosine, sine)
+    )(
+        q, k, v, offsets, level, back_attended, q_proj, k_proj, head_gains, cosine, sine, place, *shares
+    )
 
 
 def weights_kernel(
@@ -541,7 +567,6 @@
     kv1,
     kv2,
     kv3,
-    back_halo,
     back_own,
     kept,
     sent,
@@ -576,7 +601,6 @@
     for copy in copies:
         copy.wait()
     e = dot(bkv[:512], wkv[...], rows_both)
-    back_halo[...] = e.astype(bf16)
     x = halo[...].astype(f32)
     grad = jnp.sum(x * inverse_rms(x) * e, axis=0, keepdims=True)
     e = dot(bkv[512:], wkv[...], rows_both) + dot(bq, wq[...], rows_both)
@@ -604,10 +628,9 @@
         name="weights_part",
         in_specs=[pl.BlockSpec(memory_space=pltpu.SMEM)]
         + [whole()] * 9
-        + [pl.BlockSpec(memory_space=pl.ANY)] * 8,
-        out_specs=[whole()] * 2 + [pl.BlockSpec(memory_space=pl.ANY)] * 2,
+        + [pl.BlockSpec(memory_space=pltpu.HBM)] * 8,
+        out_specs=[whole()] + [pl.BlockSpec(memory_space=pltpu.HBM)] * 2,
         out_shape=[
-            spec(512, 640, bf16),
             spec(512, 640, f32),
             spec(2, 3584, 128, bf16),
             spec(2, 3584, 128, bf16),
@@ -707,8 +730,8 @@
     return pl.pallas_call(
         unpack_kernel,
         name="unpack",
-        in_specs=[pl.BlockSpec(memory_space=pltpu.SMEM)] + [pl.BlockSpec(memory_space=pl.ANY)] * 8,
-        out_specs=[pl.BlockSpec(memory_space=pl.ANY)] * 7 + [whole()],
+        in_specs=[pl.BlockSpec(memory_space=pltpu.SMEM)] + [pl.BlockSpec(memory_space=pltpu.HBM)] * 8,
+        out_specs=[pl.BlockSpec(memory_space=pltpu.HBM)] * 7 + [whole()],
         out_shape=[spec(*shape, f32) for shape in shapes] + [spec(16, 128, f32)],
         scratch_shapes=[pltpu.VMEM(shape, f32) for shape in shapes]
         + [
@@ -922,6 +945,7 @@
     offsets = positions[0]
 
     q_partner = swap_near(query_weight)
+    wg_partner, wu_partner = swap_near(gate_weight), swap_far(up_weight)
     kv = pack(
         [norm_in, norm_attn, norm_ffn_in, norm_ffn_out, norm_query, norm_key],
         key_weight,
@@ -931,14 +955,10 @@
     q_sibling = swap_core(query_weight)
     kv_sibling = swap_core(kv)
     halo = shifted(own, 1)
-    (q_sibling, kv_sibling), (wg, wu) = together(
-        (q_sibling, kv_sibling), (gate_weight, up_weight)
-    )
-    wg_partner, wu_partner = swap_near(wg), swap_far(wu)
     q_diagonal = swap_core(q_partner)
     kv_diagonal = swap_core(kv_partner)
-    (q_diagonal, kv_diagonal), (wo, wd) = together(
-        (q_diagonal, kv_diagonal), (output_weight, down_weight)
+    (q_diagonal, kv_diagonal, halo), (wg_partner, wu_partner), (wo, wd) = together(
+        (q_diagonal, kv_diagonal, halo), (wg_partner, wu_partner), (output_weight, down_weight)
     )
     wo_partner, wd_partner = swap_near(wo), swap_far(wd)
     q_shares = (query_weight, q_sibling, q_partner, q_diagonal)
@@ -961,7 +981,7 @@
         place, halo, own, gains, head_gains, q_shares, kv_shares, cosine, sine
     )
     attended, level = attend(q, k, v, column)
-    attended, (wo, wg, wu, wd) = together(attended, (wo, wg, wu, wd))
+    attended, (wo, wg, wu, wd) = together(attended, (wo, gate_weight, up_weight, wd))
     siblings = [swap_core(w) for w in (wo, wg, wu, wd)]
     attended, wo_partner, wg_partner = together(attended, wo_partner, wg_partner)
     attended, wu_partner, wd_partner = together(attended, wu_partner, wd_partner)
@@ -973,10 +993,22 @@
         place, own, attended, upstream, gains, wo_shares + wg_shares + wu_shares + wd_shares
     )
     got = swap_core(sent)
-    back_q, back_kv, gain_head = attend_back(
-        q, k, v, column, level, back_attended, q_proj, k_proj, head_gains, cosine, sine
-    )
-    back_halo, back_own, kept_attn, sent = weights_part(
+    back_q, back_kv, gain_head, back_halo = attend_back(
+        q,
+        k,
+        v,
+        column,
+        level,
+        back_attended,
+        q_proj,
+        k_proj,
+        head_gains,
+        cosine,
+        sine,
+        place,
+        kv_shares,
+    )
+    back_own, kept_attn, sent = weights_part(
         place,
         normed,
         back_q,
@@ -991,8 +1023,9 @@
     )
     got_attn = swap_core(sent)
     first = move_first(first_sums(spot, kept, got, kept_attn, got_attn))
+    mine, other = third_sums(place, move_second(second_sums(spot, first)))
+    mine, other, back_halo = together(mine, other, back_halo)
     returned = shifted(back_halo, -1)
-    mine, other = third_sums(place, move_second(second_sums(spot, first)))
     a, b = fourth_sums([mine, swap_near(other), swap_far(other), swap_hi(mine)])
     a = jnp.stack([a] + [move_y(a, d) for d in (1, 2, 3)])
     b = jnp.stack([b] + [move_x(b, d) for d in (1, 2, 3)])

time: 281 us -> 279 us (level)
  the two profiles are of different devices: /device:TPU:102 before, /device:TPU:28 now
where the time goes in v1:
time: 279 us; the launch traced here: 276 us
  waiting for transfers between devices  85.9 us (31%)
  starting transfers between devices  85.1 us (31%)
  Pallas kernels  82.3 us (29%)
  local copies, waits for them, and re-layouts  17.4 us (6%)
  other arithmetic  3.5 us (1%)
    pallas_call x1, Pallas kernels, middle_part(): pl.pallas_call(middle_kernel, name='middle_part', in_specs=[pl.BlockSpec(...  38.9 us
    ppermute x12, waiting for transfers between devices, move_y(): return lax.ppermute(value, 'seq', along_xy(0, d))  36.6 us
    ppermute x12, starting transfers between devices, move_x(): return lax.ppermute(value, 'seq', along_xy(d, 0))  36.5 us
    ppermute x12, starting transfers between devices, move_y(): return lax.ppermute(value, 'seq', along_xy(0, d))  28 us
    ppermute x12, waiting for transfers between devices, move_x(): return lax.ppermute(value, 'seq', along_xy(d, 0))  24.5 us
    unnamed x68, local copies, waits for them, and re-layouts  14.9 us
    pallas_call x1, Pallas kernels, attend_back(): pl.pallas_call(attend_back_kernel, name='attend_back', grid=(2,), in_spec...  9.91 us
    ppermute x14, waiting for transfers between devices, swap_core(): return lax.ppermute(value, 'fsdp', [(0, 1), (1, 0), (2, 3), (3, 2)])  9.03 us
  transfers between devices with their start and end apart: 49, of which 27 were waited for; matrix products, arithmetic and copies ran while one was open for 2% of the time, Pallas kernels for 13%

profile of v1, /device:TPU:28, one launch (start us, length us, event | category | flops | bytes accessed | tf_op | source)
XLA Modules:
  0.0 276.2 jit_solution(16402015407526202151)
XLA Ops:
  11.1 2.8 collective-permute-start.4
  22.2 6.9 %collective-permute-done.4.halo = bf16[512,640]{1,0:T(8,128)(2,1)S(1)} collective-permute-done((bf16[512,640]{1,0:T(8,128)(2,1)}, bf16[512,640]{1,0:T(8,128)(2,1)S(1)}, u32[]{:S(2)}, u32[]{:S(2)}) %collective-permute-start.4) | collective-permute-done | bytes 655392 | tf_op jit(solution)/shard_map/ppermute | solution.py:891
  34.1 6.0 %project.1 = (bf16[1024,640]{1,0:T(8,128)(2,1)S(1)}, bf16[512,1024]{1,0:T(8,128)(2,1)S(1)}, bf16[1024,256]{1,0:T(8,128)(2,1)S(1)}, bf16[1024,256]{1,0:T(8,128)(2...) custom-call(s32[1]{0:T(128)} %bitcast.place, bf16[512,640]{1,0:T(8,128)(2,1)S(1)} %collective-permute-done.4.halo, ...), custom_call_target="tpu_custom_call" | custom-call | flops 1350000000 | bytes 9000000 | tf_op jit(solution)/shard_map/project/pallas_call | solution.py:186
  40.2 3.9 %attend.1 = (bf16[512,1024]{1,0:T(8,128)(2,1)S(1)}, f32[4,512,1]{2,1,0:T(8,128)S(1)}) custom-call(bf16[512,1024]{1,0:T(8,128)(2,1)S(1)} %get-tuple-element.91.q, bf16[1024,256]{1,0:T(8,128)(2,1)S(1)} %get-tuple-element.92.k, bf16[1024,256]{1,0:T(8,128)(2,1)S(1)} %get-tuple-element.93.v, s32[512,1]{1,0:T(8,128)S(1)} %copy.31.offsets), custom_call_target="tpu_custom_call" | custom-call | flops 1700000000 | bytes 4000000 | tf_op jit(solution)/shard_map/attend/pallas_call | solution.py:253
  54.6 38.9 %middle_part.1 = (bf16[512,640]{1,0:T(8,128)(2,1)}, f32[512,640]{1,0:T(8,128)}, bf16[512,640]{1,0:T(8,128)(2,1)S(1)}, bf16[512,1024]{1,0:T(8,128)(2,1)}, f32[8,6...) custom-call(s32[1]{0:T(128)} %bitcast.place, bf16[512,640]{1,0:T(8,128)(2,1)S(1)} %bitcast.34, ...), custom_call_target="tpu_custom_call" | custom-call | flops 13400000512 | bytes 23000000 | tf_op jit(solution)/shard_map/middle_part/pallas_call | solution.py:396
  96.1 9.9 %attend_back.1 = (bf16[512,1024]{1,0:T(8,128)(2,1)S(1)}, bf16[1024,512]{1,0:T(8,128)(2,1)S(1)}, f32[8,256]{1,0:T(8,128)S(1)}, bf16[512,640]{1,0:T(8,128)(2,1)S(1)}) custom-call(bf16[512,1024]{1,0:T(8,128)(2,1)S(1)} %get-tuple-element.91.q, bf16[1024,256]{1,0:T(8,128)(2,1)S(1)} %copy-done.23, bf16[1024,256]{1,0:T(8,128)(2,1)S(1)} %get-tuple-element.93.v, ...), custom_call_target="tpu_custom_call" | custom-call | flops 4300000256 | bytes 10000000 | tf_op jit(solution)/shard_map/attend_back/pallas_call | solution.py:507
  106.9 7.4 %weights_part.1 = (f32[512,640]{1,0:T(8,128)S(1)}, bf16[2,3584,128]{2,1,0:T(8,128)(2,1)S(1)}, bf16[2,3584,128]{2,1,0:T(8,128)(2,1)}) custom-call(s32[1]{0:T(128)} %bitcast.place, bf16[1024,640]{1,0:T(8,128)(2,1)S(1)} %get-tuple-element.111.normed, bf16[512,1024]{1,0:T(8,128)(2,1)S(1)} %get-tuple-element.116.back_q, ...), custom_call_target="tpu_custom_call" | custom-call | flops 3400000000 | bytes 14000000 | tf_op jit(solution)/shard_map/weights_part/pallas_call | solution.py:626
  114.8 3.7 %collective-permute-done.20 = bf16[2,3584,128]{2,1,0:T(8,128)(2,1)} collective-permute-done((bf16[2,3584,128]{2,1,0:T(8,128)(2,1)}, bf16[2,3584,128]{2,1,0:T(8,128)(2,1)}, u32[]{:S(2)}, u32[]{:S(2)}) %collective-permute-start.20) | collective-permute-done | bytes 1835040 | tf_op jit(solution)/shard_map/ppermute | solution.py:866
  120.6 4.0 %first_sums.1 = (bf16[2,4,352,128]{3,2,1,0:T(8,128)(2,1)S(1)}, bf16[2,4,352,128]{3,2,1,0:T(8,128)(2,1)S(1)}, bf16[2,4,352,128]{3,2,1,0:T(8,128)(2,1)S(1)}, bf16[...) custom-call(s32[2]{0:T(128)S(1)} %pad_add_fusion.spot, ...), custom_call_target="tpu_custom_call" | custom-call | flops 3000000 | bytes 17000000 | tf_op jit(solution)/shard_map/first_sums/pallas_call | solution.py:771
  128.7 14.7 %collective-permute-start.24 = (bf16[2,4,352,128]{3,2,1,0:T(8,128)(2,1)S(1)}, bf16[2,4,352,128]{3,2,1,0:T(8,128)(2,1)S(1)}, u32[]{:S(2)}, u32[]{:S(2)}) collective-permute-start(bf16[2,4,352,128]{3,2,1,0:T(8,128)(2,1)S(1)} %get-tuple-element.131), channel_id=1, source_target_pairs={{0,4},{4,8},{8,12},{12,0},{16,20},{20,24},{24,28},{28,16},{32,36},... | collective-permute-start | bytes 2162696 | tf_op jit(solution)/shard_map/ppermute | solution.py:886
  145.6 13.2 %collective-permute-done.23.refs_3_ = bf16[2,4,352,128]{3,2,1,0:T(8,128)(2,1)S(1)} collective-permute-done((bf16[2,4,352,128]{3,2,1,0:T(8,128)(2,1)S(1)}, bf16[2,4,352,128]{3,2,1,0:T(8,128)(2,1)S(1)}, u32[]{:S(2)}, u32[]{:S(2)}) %collective-permute-start.23) | collective-permute-done | bytes 720928 | tf_op jit(solution)/shard_map/ppermute | solution.py:882
  158.8 15.1 %collective-permute-done.24.refs_5_ = bf16[2,4,352,128]{3,2,1,0:T(8,128)(2,1)S(1)} collective-permute-done((bf16[2,4,352,128]{3,2,1,0:T(8,128)(2,1)S(1)}, bf16[2,4,352,128]{3,2,1,0:T(8,128)(2,1)S(1)}, u32[]{:S(2)}, u32[]{:S(2)}) %collective-permute-start.24) | collective-permute-done | bytes 720928 | tf_op jit(solution)/shard_map/ppermute | solution.py:886
  174.0 3.6 %collective-permute-done.25.refs_6_ = bf16[2,4,352,128]{3,2,1,0:T(8,128)(2,1)S(1)} collective-permute-done((bf16[2,4,352,128]{3,2,1,0:T(8,128)(2,1)S(1)}, bf16[2,4,352,128]{3,2,1,0:T(8,128)(2,1)S(1)}, u32[]{:S(2)}, u32[]{:S(2)}) %collective-permute-start.25) | collective-permute-done | bytes 720928 | tf_op jit(solution)/shard_map/ppermute | solution.py:886
  181.5 13.3 %collective-permute-start.30 = (bf16[2,352,128]{2,1,0:T(8,128)(2,1)S(1)}, bf16[2,352,128]{2,1,0:T(8,128)(2,1)S(1)}, u32[]{:S(2)}, u32[]{:S(2)}) collective-permute-start(bf16[2,352,128]{2,1,0:T(8,128)(2,1)S(1)} %get-tuple-element.139), channel_id=1, source_target_pairs={{0,16},{4,20},{8,24},{12,28},{16,32},{20,36},{24,40},{28,44},{32,4... | collective-permute-start | bytes 540680 | tf_op jit(solution)/shard_map/ppermute | solution.py:882
  194.7 7.9 %collective-permute-start.32 = (bf16[2,352,128]{2,1,0:T(8,128)(2,1)S(1)}, bf16[2,352,128]{2,1,0:T(8,128)(2,1)S(1)}, u32[]{:S(2)}, u32[]{:S(2)}) collective-permute-start(bf16[2,352,128]{2,1,0:T(8,128)(2,1)S(1)} %get-tuple-element.141), channel_id=1, source_target_pairs={{0,32},{4,36},{8,40},{12,44},{16,48},{20,52},{24,56},{28,60},{32,0... | collective-permute-start | bytes 540680 | tf_op jit(solution)/shard_map/ppermute | solution.py:882
  202.8 3.2 %collective-permute-done.32.refs_7_ = bf16[2,352,128]{2,1,0:T(8,128)(2,1)S(1)} collective-permute-done((bf16[2,352,128]{2,1,0:T(8,128)(2,1)S(1)}, bf16[2,352,128]{2,1,0:T(8,128)(2,1)S(1)}, u32[]{:S(2)}, u32[]{:S(2)}) %collective-permute-start.32) | collective-permute-done | bytes 180256 | tf_op jit(solution)/shard_map/ppermute | solution.py:882
  210.3 3.1 %collective-permute-done.36.p3 = bf16[2,352,128]{2,1,0:T(8,128)(2,1)S(1)} collective-permute-done((bf16[2,352,128]{2,1,0:T(8,128)(2,1)S(1)}, bf16[2,352,128]{2,1,0:T(8,128)(2,1)S(1)}, u32[]{:S(2)}, u32[]{:S(2)}) %collective-permute-start.36) | collective-permute-done | bytes 180256 | tf_op jit(solution)/shard_map/ppermute | solution.py:878
  216.8 4.3 %collective-permute-start.38 = (bf16[352,128]{1,0:T(8,128)(2,1)S(1)}, bf16[352,128]{1,0:T(8,128)(2,1)S(1)}, u32[]{:S(2)}, u32[]{:S(2)}) collective-permute-start(bf16[352,128]{1,0:T(8,128)(2,1)S(1)} %get-tuple-element.149), channel_id=1, source_target_pairs={{0,8},{4,12},{8,0},{12,4},{16,24},{20,28},{24,16},{28,20},{32,40},... | collective-permute-start | bytes 270344 | tf_op jit(solution)/shard_map/ppermute | solution.py:886
  221.2 4.2 %collective-permute-start.41 = (bf16[352,128]{1,0:T(8,128)(2,1)S(1)}, bf16[352,128]{1,0:T(8,128)(2,1)S(1)}, u32[]{:S(2)}, u32[]{:S(2)}) collective-permute-start(bf16[352,128]{1,0:T(8,128)(2,1)S(1)} %get-tuple-element.150), channel_id=1, source_target_pairs={{0,32},{4,36},{8,40},{12,44},{16,48},{20,52},{24,56},{28,60},{32,0... | collective-permute-start | bytes 270344 | tf_op jit(solution)/shard_map/ppermute | solution.py:882
  235.2 2.7 collective-permute-start.48
  237.8 3.5 %collective-permute-done.45.a3 = bf16[4,352,128]{2,1,0:T(8,128)(2,1)S(1)} collective-permute-done((bf16[4,352,128]{2,1,0:T(8,128)(2,1)S(1)}, bf16[4,352,128]{2,1,0:T(8,128)(2,1)S(1)}, u32[]{:S(2)}, u32[]{:S(2)}) %collective-permute-start.45) | collective-permute-done | bytes 360480 | tf_op jit(solution)/shard_map/ppermute | solution.py:882
  242.7 2.7 collective-permute-start.33
  246.4 17.9 %collective-permute-done.48.b3 = bf16[4,352,128]{2,1,0:T(8,128)(2,1)S(1)} collective-permute-done((bf16[4,352,128]{2,1,0:T(8,128)(2,1)S(1)}, bf16[4,352,128]{2,1,0:T(8,128)(2,1)S(1)}, u32[]{:S(2)}, u32[]{:S(2)}) %collective-permute-start.48) | collective-permute-done | bytes 360480 | tf_op jit(solution)/shard_map/ppermute | solution.py:886
  264.3 8.7 %unpack.1 = (f32[160,1024]{1,0:T(8,128)}, f32[160,256]{1,0:T(8,128)}, f32[160,256]{1,0:T(8,128)}, f32[256,640]{1,0:T(8,128)}, f32[160,2048]{1,0:T(8,128)}, /*ind...) custom-call(s32[2]{0:T(128)S(1)} %pad_add_fusion.spot, bf16[4,352,128]{2,1,0:T(8,128)(2,1)S(1)} %pad_maximum_fusion.a0, ...), custom_call_target="tpu_custom_call" | custom-call | flops 4000000 | bytes 11000000 | tf_op jit(solution)/shard_map/unpack/pallas_call | solution.py:730
  (179 shorter events, 72.9 us)
Async XLA Ops:
  0.7 18.4 %collective-permute-start = (bf16[160,1024]{1,0:T(8,128)(2,1)}, bf16[160,1024]{1,0:T(8,128)(2,1)}, u32[]{:S(2)}, u32[]{:S(2)}) collective-permute-start(bf16[160,1024]{1,0:T(8,128)(2,1)} %q0.3), channel_id=1, source_target_pairs={{0,2},{1,3},{2,0},{3,1},{4,6},{5,7},{6,4},{7,5},{8,10},{9,11},{10,... | collective-permute-start | bytes 983048 | tf_op jit(solution)/shard_map/ppermute | solution.py:870
  11.1 18.0 %collective-permute-start.4 = (bf16[512,640]{1,0:T(8,128)(2,1)}, bf16[512,640]{1,0:T(8,128)(2,1)S(1)}, u32[]{:S(2)}, u32[]{:S(2)}) collective-permute-start(bf16[512,640]{1,0:T(8,128)(2,1)} %bitcast.32), channel_id=1, source_target_pairs={{0,4},{4,8},{8,12},{12,16},{16,20},{20,24},{24,28},{28,32},{32,36}... | collective-permute-start | bytes 1966088 | tf_op jit(solution)/shard_map/ppermute | solution.py:891
  13.8 15.9 %collective-permute-start.5 = (bf16[160,2048]{1,0:T(8,128)(2,1)}, bf16[160,2048]{1,0:T(8,128)(2,1)S(1)}, u32[]{:S(2)}, u32[]{:S(2)}) collective-permute-start(bf16[160,2048]{1,0:T(8,128)(2,1)} %g0.2), channel_id=1, source_target_pairs={{0,2},{1,3},{2,0},{3,1},{4,6},{5,7},{6,4},{7,5},{8,10},{9,11},{10,... | collective-permute-start | bytes 1966088 | tf_op jit(solution)/shard_map/ppermute | solution.py:870
  14.9 16.8 %collective-permute-start.6 = (bf16[160,2048]{1,0:T(8,128)(2,1)}, bf16[160,2048]{1,0:T(8,128)(2,1)S(1)}, u32[]{:S(2)}, u32[]{:S(2)}) collective-permute-start(bf16[160,2048]{1,0:T(8,128)(2,1)} %u0), channel_id=1, source_target_pairs={{0,66},{1,67},{2,64},{3,65},{4,70},{5,71},{6,68},{7,69},{8,74},{9,... | collective-permute-start | bytes 1966088 | tf_op jit(solution)/shard_map/ppermute | solution.py:874
  19.7 12.0 %collective-permute-start.7 = (bf16[176,512]{1,0:T(8,128)(2,1)S(1)}, bf16[176,512]{1,0:T(8,128)(2,1)S(1)}, u32[]{:S(2)}, u32[]{:S(2)}) collective-permute-start(bf16[176,512]{1,0:T(8,128)(2,1)S(1)} %pack.1.kv0), channel_id=1, source_target_pairs={{0,1},{1,0},{2,3},{3,2},{4,5},{5,4},{6,7},{7,6},{8,9},{9,8},{10,11... | collective-permute-start | bytes 540680 | tf_op jit(solution)/shard_map/ppermute | solution.py:866
  31.8 14.7 %collective-permute-start.9 = (bf16[256,640]{1,0:T(8,128)(2,1)}, bf16[256,640]{1,0:T(8,128)(2,1)S(1)}, u32[]{:S(2)}, u32[]{:S(2)}) collective-permute-start(bf16[256,640]{1,0:T(8,128)(2,1)} %o0), channel_id=1, source_target_pairs={{0,2},{1,3},{2,0},{3,1},{4,6},{5,7},{6,4},{7,5},{8,10},{9,11},{10,... | collective-permute-start | bytes 983048 | tf_op jit(solution)/shard_map/ppermute | solution.py:870
  31.9 15.9 %collective-permute-start.10 = (bf16[512,640]{1,0:T(8,128)(2,1)}, bf16[512,640]{1,0:T(8,128)(2,1)S(1)}, u32[]{:S(2)}, u32[]{:S(2)}) collective-permute-start(bf16[512,640]{1,0:T(8,128)(2,1)} %d0), channel_id=1, source_target_pairs={{0,66},{1,67},{2,64},{3,65},{4,70},{5,71},{6,68},{7,69},{8,74},{9,... | collective-permute-start | bytes 1966088 | tf_op jit(solution)/shard_map/ppermute | solution.py:874
  93.4 25.1 %collective-permute-start.19 = (bf16[2,7680,128]{2,1,0:T(8,128)(2,1)}, bf16[2,7680,128]{2,1,0:T(8,128)(2,1)}, u32[]{:S(2)}, u32[]{:S(2)}) collective-permute-start(bf16[2,7680,128]{2,1,0:T(8,128)(2,1)} %get-tuple-element.123), channel_id=1, source_target_pairs={{0,1},{1,0},{2,3},{3,2},{4,5},{5,4},{6,7},{7,6},{8,9},{9,8},{10,11... | collective-permute-start | bytes 11796488 | tf_op jit(solution)/shard_map/ppermute | solution.py:866
  124.6 18.9 %collective-permute-start.21 = (bf16[2,4,352,128]{3,2,1,0:T(8,128)(2,1)S(1)}, bf16[2,4,352,128]{3,2,1,0:T(8,128)(2,1)S(1)}, u32[]{:S(2)}, u32[]{:S(2)}) collective-permute-start(bf16[2,4,352,128]{3,2,1,0:T(8,128)(2,1)S(1)} %get-tuple-element.127), channel_id=1, source_target_pairs={{0,16},{4,20},{8,24},{12,28},{16,32},{20,36},{24,40},{28,44},{32,4... | collective-permute-start | bytes 2162696 | tf_op jit(solution)/shard_map/ppermute | solution.py:882
  125.9 19.7 %collective-permute-start.22 = (bf16[2,4,352,128]{3,2,1,0:T(8,128)(2,1)S(1)}, bf16[2,4,352,128]{3,2,1,0:T(8,128)(2,1)S(1)}, u32[]{:S(2)}, u32[]{:S(2)}) collective-permute-start(bf16[2,4,352,128]{3,2,1,0:T(8,128)(2,1)S(1)} %get-tuple-element.128), channel_id=1, source_target_pairs={{0,48},{4,52},{8,56},{12,60},{16,0},{20,4},{24,8},{28,12},{32,16},... | collective-permute-start | bytes 2162696 | tf_op jit(solution)/shard_map/ppermute | solution.py:882
  126.8 32.0 %collective-permute-start.23 = (bf16[2,4,352,128]{3,2,1,0:T(8,128)(2,1)S(1)}, bf16[2,4,352,128]{3,2,1,0:T(8,128)(2,1)S(1)}, u32[]{:S(2)}, u32[]{:S(2)}) collective-permute-start(bf16[2,4,352,128]{3,2,1,0:T(8,128)(2,1)S(1)} %get-tuple-element.129), channel_id=1, source_target_pairs={{0,32},{4,36},{8,40},{12,44},{16,48},{20,52},{24,56},{28,60},{32,0... | collective-permute-start | bytes 2162696 | tf_op jit(solution)/shard_map/ppermute | solution.py:882
  128.7 45.2 %collective-permute-start.24 = (bf16[2,4,352,128]{3,2,1,0:T(8,128)(2,1)S(1)}, bf16[2,4,352,128]{3,2,1,0:T(8,128)(2,1)S(1)}, u32[]{:S(2)}, u32[]{:S(2)}) collective-permute-start(bf16[2,4,352,128]{3,2,1,0:T(8,128)(2,1)S(1)} %get-tuple-element.131), channel_id=1, source_target_pairs={{0,4},{4,8},{8,12},{12,0},{16,20},{20,24},{24,28},{28,16},{32,36},... | collective-permute-start | bytes 2162696 | tf_op jit(solution)/shard_map/ppermute | solution.py:886
  143.4 34.1 %collective-permute-start.25 = (bf16[2,4,352,128]{3,2,1,0:T(8,128)(2,1)S(1)}, bf16[2,4,352,128]{3,2,1,0:T(8,128)(2,1)S(1)}, u32[]{:S(2)}, u32[]{:S(2)}) collective-permute-start(bf16[2,4,352,128]{3,2,1,0:T(8,128)(2,1)S(1)} %get-tuple-element.132), channel_id=1, source_target_pairs={{0,12},{4,0},{8,4},{12,8},{16,28},{20,16},{24,20},{28,24},{32,44},... | collective-permute-start | bytes 2162696 | tf_op jit(solution)/shard_map/ppermute | solution.py:886
  143.6 33.9 %collective-permute-start.26 = (bf16[2,4,352,128]{3,2,1,0:T(8,128)(2,1)S(1)}, bf16[2,4,352,128]{3,2,1,0:T(8,128)(2,1)S(1)}, u32[]{:S(2)}, u32[]{:S(2)}) collective-permute-start(bf16[2,4,352,128]{3,2,1,0:T(8,128)(2,1)S(1)} %get-tuple-element.133), channel_id=1, source_target_pairs={{0,8},{4,12},{8,0},{12,4},{16,24},{20,28},{24,16},{28,20},{32,40},... | collective-permute-start | bytes 2162696 | tf_op jit(solution)/shard_map/ppermute | solution.py:886
  178.8 15.9 %collective-permute-start.27 = (bf16[2,352,128]{2,1,0:T(8,128)(2,1)S(1)}, bf16[2,352,128]{2,1,0:T(8,128)(2,1)S(1)}, u32[]{:S(2)}, u32[]{:S(2)}) collective-permute-start(bf16[2,352,128]{2,1,0:T(8,128)(2,1)S(1)} %get-tuple-element.135), channel_id=1, source_target_pairs={{0,4},{4,8},{8,12},{12,0},{16,20},{20,24},{24,28},{28,16},{32,36},... | collective-permute-start | bytes 540680 | tf_op jit(solution)/shard_map/ppermute | solution.py:886
  179.0 23.6 %collective-permute-start.28 = (bf16[2,352,128]{2,1,0:T(8,128)(2,1)S(1)}, bf16[2,352,128]{2,1,0:T(8,128)(2,1)S(1)}, u32[]{:S(2)}, u32[]{:S(2)}) collective-permute-start(bf16[2,352,128]{2,1,0:T(8,128)(2,1)S(1)} %get-tuple-element.136), channel_id=1, source_target_pairs={{0,12},{4,0},{8,4},{12,8},{16,28},{20,16},{24,20},{28,24},{32,44},... | collective-permute-start | bytes 540680 | tf_op jit(solution)/shard_map/ppermute | solution.py:886
  180.9 21.7 %collective-permute-start.29 = (bf16[2,352,128]{2,1,0:T(8,128)(2,1)S(1)}, bf16[2,352,128]{2,1,0:T(8,128)(2,1)S(1)}, u32[]{:S(2)}, u32[]{:S(2)}) collective-permute-start(bf16[2,352,128]{2,1,0:T(8,128)(2,1)S(1)} %get-tuple-element.137), channel_id=1, source_target_pairs={{0,8},{4,12},{8,0},{12,4},{16,24},{20,28},{24,16},{28,20},{32,40},... | collective-permute-start | bytes 540680 | tf_op jit(solution)/shard_map/ppermute | solution.py:886
  181.5 21.1 %collective-permute-start.30 = (bf16[2,352,128]{2,1,0:T(8,128)(2,1)S(1)}, bf16[2,352,128]{2,1,0:T(8,128)(2,1)S(1)}, u32[]{:S(2)}, u32[]{:S(2)}) collective-permute-start(bf16[2,352,128]{2,1,0:T(8,128)(2,1)S(1)} %get-tuple-element.139), channel_id=1, source_target_pairs={{0,16},{4,20},{8,24},{12,28},{16,32},{20,36},{24,40},{28,44},{32,4... | collective-permute-start | bytes 540680 | tf_op jit(solution)/shard_map/ppermute | solution.py:882
  230.0 11.4 %collective-permute-start.45 = (bf16[4,352,128]{2,1,0:T(8,128)(2,1)S(1)}, bf16[4,352,128]{2,1,0:T(8,128)(2,1)S(1)}, u32[]{:S(2)}, u32[]{:S(2)}) collective-permute-start(bf16[4,352,128]{2,1,0:T(8,128)(2,1)S(1)} %pad_maximum_fusion.a0), channel_id=1, source_target_pairs={{0,48},{4,52},{8,56},{12,60},{16,0},{20,4},{24,8},{28,12},{32,16},... | collective-permute-start | bytes 1081352 | tf_op jit(solution)/shard_map/ppermute | solution.py:882
  234.0 12.4 %collective-permute-start.43 = (bf16[4,352,128]{2,1,0:T(8,128)(2,1)S(1)}, bf16[4,352,128]{2,1,0:T(8,128)(2,1)S(1)}, u32[]{:S(2)}, u32[]{:S(2)}) collective-permute-start(bf16[4,352,128]{2,1,0:T(8,128)(2,1)S(1)} %pad_maximum_fusion.a0), channel_id=1, source_target_pairs={{0,16},{4,20},{8,24},{12,28},{16,32},{20,36},{24,40},{28,44},{32,4... | collective-permute-start | bytes 1081352 | tf_op jit(solution)/shard_map/ppermute | solution.py:882
  235.2 29.1 %collective-permute-start.48 = (bf16[4,352,128]{2,1,0:T(8,128)(2,1)S(1)}, bf16[4,352,128]{2,1,0:T(8,128)(2,1)S(1)}, u32[]{:S(2)}, u32[]{:S(2)}) collective-permute-start(bf16[4,352,128]{2,1,0:T(8,128)(2,1)S(1)} %pad_maximum_fusion.1.b0), channel_id=1, source_target_pairs={{0,12},{4,0},{8,4},{12,8},{16,28},{20,16},{24,20},{28,24},{32,44},... | collective-permute-start | bytes 1081352 | tf_op jit(solution)/shard_map/ppermute | solution.py:886
  237.8 26.4 %collective-permute-start.47 = (bf16[4,352,128]{2,1,0:T(8,128)(2,1)S(1)}, bf16[4,352,128]{2,1,0:T(8,128)(2,1)S(1)}, u32[]{:S(2)}, u32[]{:S(2)}) collective-permute-start(bf16[4,352,128]{2,1,0:T(8,128)(2,1)S(1)} %pad_maximum_fusion.1.b0), channel_id=1, source_target_pairs={{0,8},{4,12},{8,0},{12,4},{16,24},{20,28},{24,16},{28,20},{32,40},... | collective-permute-start | bytes 1081352 | tf_op jit(solution)/shard_map/ppermute | solution.py:886
  241.4 22.9 %collective-permute-start.46 = (bf16[4,352,128]{2,1,0:T(8,128)(2,1)S(1)}, bf16[4,352,128]{2,1,0:T(8,128)(2,1)S(1)}, u32[]{:S(2)}, u32[]{:S(2)}) collective-permute-start(bf16[4,352,128]{2,1,0:T(8,128)(2,1)S(1)} %pad_maximum_fusion.1.b0), channel_id=1, source_target_pairs={{0,4},{4,8},{8,12},{12,0},{16,20},{20,24},{24,28},{28,16},{32,36},... | collective-permute-start | bytes 1081352 | tf_op jit(solution)/shard_map/ppermute | solution.py:886
  242.7 31.5 %collective-permute-start.33 = (bf16[512,640]{1,0:T(8,128)(2,1)S(1)}, bf16[512,640]{1,0:T(8,128)(2,1)S(1)}, u32[]{:S(2)}, u32[]{:S(2)}) collective-permute-start(bf16[512,640]{1,0:T(8,128)(2,1)S(1)} %copy-done.17), channel_id=1, source_target_pairs={{4,0},{8,4},{12,8},{16,12},{20,16},{24,20},{28,24},{32,28},{36,32}... | collective-permute-start | bytes 1966088 | tf_op jit(solution)/shard_map/ppermute | solution.py:891
  (59 other events, 491.0 us)

commit v2 on v1

--- a/solution.py
+++ b/solution.py
@@ -56,14 +56,16 @@
     return jnp.concatenate([a * cosine + b * sine, b * cosine - a * sine], axis=1)
 
 
-def assemble(pieces, into, place, semaphores, first):
+def assemble(pieces, into, place, semaphores, first, column=0):
     rows = into.shape[0] // 4
     copies = []
     for r in range(4):
         at = pl.ds(pl.multiple_of((place ^ r) * rows, rows), rows)
         copies.append(
             pltpu.make_async_copy(
-                pieces[r].at[pl.ds(0, rows), :], into.at[at, :], semaphores.at[first + r]
+                pieces[r].at[:, pl.ds(column, into.shape[1])],
+                into.at[at, :],
+                semaphores.at[first + r],
             )
         )
     for copy in copies:
@@ -90,7 +92,7 @@
     return copies
 
 
-def pack_kernel(g0, g1, g2, g3, g4, g5, k, v, kv, *rest):
+def pack_kernel(g0, g1, g2, g3, g4, g5, out, *rest):
     held, semaphores = rest[:6], rest[6]
     copies = [
         pltpu.make_async_copy(source, into, semaphores.at[i])
@@ -98,31 +100,26 @@
     ]
     for copy in copies:
         copy.start()
-    kv[:160, :256] = k[...]
-    kv[:160, 256:] = v[...]
-    tile = []
+    out[...] = jnp.zeros_like(out)
     for copy in copies:
         copy.wait()
     for i, ref in enumerate(held):
         n = ref.shape[0]
-        row = ref[...].astype(f32).reshape(1, n)
-        tile.append(jnp.concatenate([row, jnp.zeros((1, 512 - n), f32)], axis=1))
-    tile.append(jnp.zeros((10, 512), f32))
-    kv[160:, :] = jnp.concatenate(tile, axis=0).astype(bf16)
-
-
-def pack(rows, key_weight, value_weight):
+        out[i : i + 1, :n] = ref[...].astype(f32).reshape(1, n)
+
+
+def pack(rows):
     return pl.pallas_call(
         pack_kernel,
         name="pack",
-        in_specs=[pl.BlockSpec(memory_space=pltpu.HBM)] * 6 + [whole()] * 2,
+        in_specs=[pl.BlockSpec(memory_space=pltpu.HBM)] * 6,
         out_specs=whole(),
-        out_shape=spec(176, 512, bf16),
+        out_shape=spec(8, 256, f32),
         scratch_shapes=[pltpu.VMEM(row.shape, bf16) for row in rows]
         + [pltpu.SemaphoreType.DMA((6,))],
         compiler_params=params(4),
-        cost_estimate=cost(100_000, 400_000),
-    )(*rows, key_weight, value_weight)
+        cost_estimate=cost(100_000, 20_000),
+    )(*rows)
 
 
 def project_kernel(
@@ -316,8 +313,8 @@
     semaphores,
 ):
     output_copies = assemble((o0, o1, o2, o3), wo, place[0], semaphores, 0)
-    gate_copies = assemble((g0, g1, g2, g3), wg, place[0], semaphores, 4)
-    up_copies = assemble((u0, u1, u2, u3), wu, place[0], semaphores, 8)
+    gate_copies = assemble((g0, g1, g2, g3), wg, place[0], semaphores, 4, 1024)
+    up_copies = assemble((u0, u1, u2, u3), wu, place[0], semaphores, 8, 512)
     down_copies = assemble((d0, d1, d2, d3), wd, place[0], semaphores, 12)
     for copy in output_copies:
         copy.wait()
@@ -944,53 +941,29 @@
     upstream = cotangent[0]
     offsets = positions[0]
 
-    q_partner = swap_near(query_weight)
-    wg_partner, wu_partner = swap_near(gate_weight), swap_far(up_weight)
-    kv = pack(
-        [norm_in, norm_attn, norm_ffn_in, norm_ffn_out, norm_query, norm_key],
-        key_weight,
-        value_weight,
-    )
-    kv_partner = swap_far(kv)
-    q_sibling = swap_core(query_weight)
-    kv_sibling = swap_core(kv)
+    near = jnp.concatenate([query_weight, gate_weight], axis=1)
+    far = jnp.concatenate([key_weight, value_weight, up_weight], axis=1)
+    near_partner, far_partner = swap_near(near), swap_far(far)
     halo = shifted(own, 1)
-    q_diagonal = swap_core(q_partner)
-    kv_diagonal = swap_core(kv_partner)
-    (q_diagonal, kv_diagonal, halo), (wg_partner, wu_partner), (wo, wd) = together(
-        (q_diagonal, kv_diagonal, halo), (wg_partner, wu_partner), (output_weight, down_weight)
-    )
-    wo_partner, wd_partner = swap_near(wo), swap_far(wd)
-    q_shares = (query_weight, q_sibling, q_partner, q_diagonal)
-    kv_shares = (kv, kv_sibling, kv_partner, kv_diagonal)
-    tails = [share[160:168] for share in kv_shares]
-    tails = [
-        jnp.where(
-            j // 2 == z_lo,
-            jnp.where(j % 2 == core, tails[0], tails[1]),
-            jnp.where(j % 2 == core, tails[2], tails[3]),
-        )
-        for j in range(4)
-    ]
-    gains = jnp.concatenate([tail[:, :160] for tail in tails], axis=1).astype(f32)
-    head_gains = jnp.concatenate([tail[:, :64] for tail in tails], axis=1).astype(f32)
+    q_shares = (near, swap_core(near), near_partner, swap_core(near_partner))
+    kv_shares = (far, swap_core(far), far_partner, swap_core(far_partner))
+    wo_partner, wd_partner = swap_near(output_weight), swap_far(down_weight)
+    tile = pack([norm_in, norm_attn, norm_ffn_in, norm_ffn_out, norm_query, norm_key])
+    tiles = lax.all_gather(tile, "fsdp")
+    gains = jnp.concatenate([tiles[j, :, :160] for j in range(4)], axis=1)
+    head_gains = jnp.concatenate([tiles[j, :, :64] for j in range(4)], axis=1)
 
     cosine, sine = rope_tables(offsets)
     column = offsets[:, None]
     normed, q, k, v, q_proj, k_proj = project(
         place, halo, own, gains, head_gains, q_shares, kv_shares, cosine, sine
     )
+    (q, k, v), wo_partner, wd_partner = together((q, k, v), wo_partner, wd_partner)
+    wo_shares = (output_weight, swap_core(output_weight), wo_partner, swap_core(wo_partner))
+    wd_shares = (down_weight, swap_core(down_weight), wd_partner, swap_core(wd_partner))
     attended, level = attend(q, k, v, column)
-    attended, (wo, wg, wu, wd) = together(attended, (wo, gate_weight, up_weight, wd))
-    siblings = [swap_core(w) for w in (wo, wg, wu, wd)]
-    attended, wo_partner, wg_partner = together(attended, wo_partner, wg_partner)
-    attended, wu_partner, wd_partner = together(attended, wu_partner, wd_partner)
-    wo_shares = [wo, siblings[0], wo_partner, swap_core(wo_partner)]
-    wg_shares = [wg, siblings[1], wg_partner, swap_core(wg_partner)]
-    wu_shares = [wu, siblings[2], wu_partner, swap_core(wu_partner)]
-    wd_shares = [wd, siblings[3], wd_partner, swap_core(wd_partner)]
     layer_out, back_middle, back_attn, back_attended, gain_mid, kept, sent = middle_part(
-        place, own, attended, upstream, gains, wo_shares + wg_shares + wu_shares + wd_shares
+        place, own, attended, upstream, gains, wo_shares + q_shares + kv_shares + wd_shares
     )
     got = swap_core(sent)
     back_q, back_kv, gain_head, back_halo = attend_back(
@@ -1024,9 +997,9 @@
     got_attn = swap_core(sent)
     first = move_first(first_sums(spot, kept, got, kept_attn, got_attn))
     mine, other = third_sums(place, move_second(second_sums(spot, first)))
-    mine, other, back_halo = together(mine, other, back_halo)
     returned = shifted(back_halo, -1)
     a, b = fourth_sums([mine, swap_near(other), swap_far(other), swap_hi(mine)])
+    a, b, returned = together(a, b, returned)
     a = jnp.stack([a] + [move_y(a, d) for d in (1, 2, 3)])
     b = jnp.stack([b] + [move_x(b, d) for d in (1, 2, 3)])
     a, b = together(a, b)

time: 279 us -> 272 us (0.975)
  the two profiles are of different devices: /device:TPU:28 before, /device:TPU:0 now
where the time goes in v2:
time: 272 us; the launch traced here: 268 us
  waiting for transfers between devices  84.1 us (31%)
  Pallas kernels  81.2 us (30%)
  starting transfers between devices  46.2 us (17%)
  blocking collectives  30 us (11%)
  local copies, waits for them, and re-layouts  21.8 us (8%)
  other arithmetic  2.8 us (1%)
    ppermute x12, waiting for transfers between devices, move_x(): return lax.ppermute(value, 'seq', along_xy(d, 0))  43.6 us
    pallas_call x1, Pallas kernels, middle_part(): pl.pallas_call(middle_kernel, name='middle_part', in_specs=[pl.BlockSpec(...  37.4 us
    all_gather x1, blocking collectives, body(): tiles = lax.all_gather(tile, 'fsdp')  30 us
    ppermute x12, waiting for transfers between devices, move_y(): return lax.ppermute(value, 'seq', along_xy(0, d))  29 us
    unnamed x97, local copies, waits for them, and re-layouts  19.4 us
    ppermute x12, starting transfers between devices, move_y(): return lax.ppermute(value, 'seq', along_xy(0, d))  16.6 us
    ppermute x12, starting transfers between devices, move_x(): return lax.ppermute(value, 'seq', along_xy(d, 0))  12.4 us
    pallas_call x1, Pallas kernels, attend_back(): pl.pallas_call(attend_back_kernel, name='attend_back', grid=(2,), in_spec...  10.4 us
  transfers between devices with their start and end apart: 43, of which 19 were waited for; matrix products, arithmetic and copies ran while one was open for 1% of the time, Pallas kernels for 12%

profile of v2, /device:TPU:0, one launch (start us, length us, event | category | flops | bytes accessed | tf_op | source)
XLA Modules:
  0.0 268.4 jit_solution(5306628186441327143)
XLA Ops:
  5.2 2.6 collective-permute-start.5
  8.3 3.5 %collective-permute-start = (bf16[512,640]{1,0:T(8,128)(2,1)S(1)}, bf16[512,640]{1,0:T(8,128)(2,1)S(1)}, u32[]{:S(2)}, u32[]{:S(2)}) collective-permute-start(bf16[512,640]{1,0:T(8,128)(2,1)S(1)} %bitcast.47), channel_id=1, source_target_pairs={{0,4},{4,8},{8,12},{12,16},{16,20},{20,24},{24,28},{28,32},{32,36}... | collective-permute-start | bytes 1966088 | tf_op jit(solution)/shard_map/ppermute | solution.py:888
  12.0 30.0 %all-gather = f32[32,256]{1,0:T(8,128)S(1)} all-gather(f32[8,256]{1,0:T(8,128)S(1)} %pack.1), channel_id=2, replica_groups=mesh['seq'=32,'fsdp'=4] {'fsdp'}, dimensions={0}, use_global_device_ids=true | all-gather | bytes 40960 | tf_op jit(solution)/shard_map/all_gather | solution.py:952
  49.9 5.1 %project.1 = (bf16[1024,640]{1,0:T(8,128)(2,1)S(1)}, bf16[512,1024]{1,0:T(8,128)(2,1)S(1)}, bf16[1024,256]{1,0:T(8,128)(2,1)S(1)}, bf16[1024,256]{1,0:T(8,128)(2...) custom-call(s32[1]{0:T(128)} %bitcast.place, bf16[512,640]{1,0:T(8,128)(2,1)S(1)} %copy-done.7, ...), custom_call_target="tpu_custom_call" | custom-call | flops 1350000000 | bytes 9000000 | tf_op jit(solution)/shard_map/project/pallas_call | solution.py:183
  67.0 3.7 %attend.1 = (bf16[512,1024]{1,0:T(8,128)(2,1)S(1)}, f32[4,512,1]{2,1,0:T(8,128)S(1)}) custom-call(bf16[512,1024]{1,0:T(8,128)(2,1)S(1)} %copy-done.29, bf16[1024,256]{1,0:T(8,128)(2,1)S(1)} %copy-done.37, bf16[1024,256]{1,0:T(8,128)(2,1)S(1)} %copy-done.40, s32[512,1]{1,0:T(8,128)S(1)} %copy.31.offsets), custom_call_target="tpu_custom_call" | custom-call | flops 1700000000 | bytes 4000000 | tf_op jit(solution)/shard_map/attend/pallas_call | solution.py:250
  71.8 37.4 %middle_part.1 = (bf16[512,640]{1,0:T(8,128)(2,1)}, f32[512,640]{1,0:T(8,128)}, bf16[512,640]{1,0:T(8,128)(2,1)S(1)}, bf16[512,1024]{1,0:T(8,128)(2,1)}, f32[8,6...) custom-call(s32[1]{0:T(128)} %bitcast.place, bf16[512,640]{1,0:T(8,128)(2,1)S(1)} %bitcast.49, ...), custom_call_target="tpu_custom_call" | custom-call | flops 13400000512 | bytes 23000000 | tf_op jit(solution)/shard_map/middle_part/pallas_call | solution.py:393
  111.1 10.4 %attend_back.1 = (bf16[512,1024]{1,0:T(8,128)(2,1)S(1)}, bf16[1024,512]{1,0:T(8,128)(2,1)S(1)}, f32[8,256]{1,0:T(8,128)S(1)}, bf16[512,640]{1,0:T(8,128)(2,1)S(1)}) custom-call(bf16[512,1024]{1,0:T(8,128)(2,1)S(1)} %copy-done.30, bf16[1024,256]{1,0:T(8,128)(2,1)S(1)} %copy-done.38, bf16[1024,256]{1,0:T(8,128)(2,1)S(1)} %copy-done.41, ...), custom_call_target="tpu_custom_call" | custom-call | flops 4300000256 | bytes 10000000 | tf_op jit(solution)/shard_map/attend_back/pallas_call | solution.py:504
  121.6 9.0 %weights_part.1 = (f32[512,640]{1,0:T(8,128)S(1)}, bf16[2,3584,128]{2,1,0:T(8,128)(2,1)}, bf16[2,3584,128]{2,1,0:T(8,128)(2,1)}) custom-call(s32[1]{0:T(128)} %bitcast.place, bf16[1024,640]{1,0:T(8,128)(2,1)} %copy-done.17, bf16[512,1024]{1,0:T(8,128)(2,1)S(1)} %get-tuple-element.90.back_q, bf16[1024,512]{1,0:T(8,128)(2,1)S(1)} %get-tuple-element.91.back_kv, ...), custom_call_target="tpu_custom_call" | custom-call | flops 3400000000 | bytes 14000000 | tf_op jit(solution)/shard_map/weights_part/pallas_call | solution.py:623
  131.8 3.9 %collective-permute-done.14 = bf16[2,3584,128]{2,1,0:T(8,128)(2,1)S(1)} collective-permute-done((bf16[2,3584,128]{2,1,0:T(8,128)(2,1)}, bf16[2,3584,128]{2,1,0:T(8,128)(2,1)S(1)}, u32[]{:S(2)}, u32[]{:S(2)}) %collective-permute-start.14) | collective-permute-done | bytes 1835040 | tf_op jit(solution)/shard_map/ppermute | solution.py:863
  139.3 3.5 %first_sums.1 = (bf16[2,4,352,128]{3,2,1,0:T(8,128)(2,1)S(1)}, bf16[2,4,352,128]{3,2,1,0:T(8,128)(2,1)S(1)}, bf16[2,4,352,128]{3,2,1,0:T(8,128)(2,1)S(1)}, bf16[...) custom-call(s32[2]{0:T(128)S(1)} %pad_add_fusion.spot, ...), custom_call_target="tpu_custom_call" | custom-call | flops 3000000 | bytes 17000000 | tf_op jit(solution)/shard_map/first_sums/pallas_call | solution.py:768
  142.8 3.2 %collective-permute-start.16 = (bf16[2,4,352,128]{3,2,1,0:T(8,128)(2,1)S(1)}, bf16[2,4,352,128]{3,2,1,0:T(8,128)(2,1)S(1)}, u32[]{:S(2)}, u32[]{:S(2)}) collective-permute-start(bf16[2,4,352,128]{3,2,1,0:T(8,128)(2,1)S(1)} %get-tuple-element.102), channel_id=1, source_target_pairs={{0,48},{4,52},{8,56},{12,60},{16,0},{20,4},{24,8},{28,12},{32,16},... | collective-permute-start | bytes 2162696 | tf_op jit(solution)/shard_map/ppermute | solution.py:879
  146.1 3.2 %collective-permute-start.19 = (bf16[2,4,352,128]{3,2,1,0:T(8,128)(2,1)S(1)}, bf16[2,4,352,128]{3,2,1,0:T(8,128)(2,1)S(1)}, u32[]{:S(2)}, u32[]{:S(2)}) collective-permute-start(bf16[2,4,352,128]{3,2,1,0:T(8,128)(2,1)S(1)} %get-tuple-element.106), channel_id=1, source_target_pairs={{0,12},{4,0},{8,4},{12,8},{16,28},{20,16},{24,20},{28,24},{32,44},... | collective-permute-start | bytes 2162696 | tf_op jit(solution)/shard_map/ppermute | solution.py:883
  149.3 28.4 %collective-permute-done.15.refs_1_ = bf16[2,4,352,128]{3,2,1,0:T(8,128)(2,1)S(1)} collective-permute-done((bf16[2,4,352,128]{3,2,1,0:T(8,128)(2,1)S(1)}, bf16[2,4,352,128]{3,2,1,0:T(8,128)(2,1)S(1)}, u32[]{:S(2)}, u32[]{:S(2)}) %collective-permute-start.15) | collective-permute-done | bytes 720928 | tf_op jit(solution)/shard_map/ppermute | solution.py:879
  179.2 14.5 %collective-permute-done.19.refs_6_ = bf16[2,4,352,128]{3,2,1,0:T(8,128)(2,1)S(1)} collective-permute-done((bf16[2,4,352,128]{3,2,1,0:T(8,128)(2,1)S(1)}, bf16[2,4,352,128]{3,2,1,0:T(8,128)(2,1)S(1)}, u32[]{:S(2)}, u32[]{:S(2)}) %collective-permute-start.19) | collective-permute-done | bytes 720928 | tf_op jit(solution)/shard_map/ppermute | solution.py:883
  193.6 3.0 %collective-permute-done.20.refs_7_ = bf16[2,4,352,128]{3,2,1,0:T(8,128)(2,1)S(1)} collective-permute-done((bf16[2,4,352,128]{3,2,1,0:T(8,128)(2,1)S(1)}, bf16[2,4,352,128]{3,2,1,0:T(8,128)(2,1)S(1)}, u32[]{:S(2)}, u32[]{:S(2)}) %collective-permute-start.20) | collective-permute-done | bytes 720928 | tf_op jit(solution)/shard_map/ppermute | solution.py:883
  198.0 3.2 %collective-permute-start.22 = (bf16[2,352,128]{2,1,0:T(8,128)(2,1)S(1)}, bf16[2,352,128]{2,1,0:T(8,128)(2,1)S(1)}, u32[]{:S(2)}, u32[]{:S(2)}) collective-permute-start(bf16[2,352,128]{2,1,0:T(8,128)(2,1)S(1)} %get-tuple-element.110), channel_id=1, source_target_pairs={{0,12},{4,0},{8,4},{12,8},{16,28},{20,16},{24,20},{28,24},{32,44},... | collective-permute-start | bytes 540680 | tf_op jit(solution)/shard_map/ppermute | solution.py:883
  201.3 3.1 %collective-permute-start.24 = (bf16[2,352,128]{2,1,0:T(8,128)(2,1)S(1)}, bf16[2,352,128]{2,1,0:T(8,128)(2,1)S(1)}, u32[]{:S(2)}, u32[]{:S(2)}) collective-permute-start(bf16[2,352,128]{2,1,0:T(8,128)(2,1)S(1)} %get-tuple-element.113), channel_id=1, source_target_pairs={{0,16},{4,20},{8,24},{12,28},{16,32},{20,36},{24,40},{28,44},{32,4... | collective-permute-start | bytes 540680 | tf_op jit(solution)/shard_map/ppermute | solution.py:879
  204.4 4.2 %collective-permute-done.21.refs_1_ = bf16[2,352,128]{2,1,0:T(8,128)(2,1)S(1)} collective-permute-done((bf16[2,352,128]{2,1,0:T(8,128)(2,1)S(1)}, bf16[2,352,128]{2,1,0:T(8,128)(2,1)S(1)}, u32[]{:S(2)}, u32[]{:S(2)}) %collective-permute-start.21) | collective-permute-done | bytes 180256 | tf_op jit(solution)/shard_map/ppermute | solution.py:883
  208.6 5.5 %collective-permute-done.25.refs_6_ = bf16[2,352,128]{2,1,0:T(8,128)(2,1)S(1)} collective-permute-done((bf16[2,352,128]{2,1,0:T(8,128)(2,1)S(1)}, bf16[2,352,128]{2,1,0:T(8,128)(2,1)S(1)}, u32[]{:S(2)}, u32[]{:S(2)}) %collective-permute-start.25) | collective-permute-done | bytes 180256 | tf_op jit(solution)/shard_map/ppermute | solution.py:879
  219.3 3.6 %collective-permute-done.29.p3 = bf16[2,352,128]{2,1,0:T(8,128)(2,1)S(1)} collective-permute-done((bf16[2,352,128]{2,1,0:T(8,128)(2,1)S(1)}, bf16[2,352,128]{2,1,0:T(8,128)(2,1)S(1)}, u32[]{:S(2)}, u32[]{:S(2)}) %collective-permute-start.29) | collective-permute-done | bytes 180256 | tf_op jit(solution)/shard_map/ppermute | solution.py:875
  234.0 3.2 %collective-permute-done.35 = bf16[352,128]{1,0:T(8,128)(2,1)S(1)} collective-permute-done((bf16[352,128]{1,0:T(8,128)(2,1)S(1)}, bf16[352,128]{1,0:T(8,128)(2,1)S(1)}, u32[]{:S(2)}, u32[]{:S(2)}) %collective-permute-start.35) | collective-permute-done | bytes 90144 | tf_op jit(solution)/shard_map/ppermute | solution.py:879
  237.2 3.3 %collective-permute-done.34 = bf16[352,128]{1,0:T(8,128)(2,1)S(1)} collective-permute-done((bf16[352,128]{1,0:T(8,128)(2,1)S(1)}, bf16[352,128]{1,0:T(8,128)(2,1)S(1)}, u32[]{:S(2)}, u32[]{:S(2)}) %collective-permute-start.34) | collective-permute-done | bytes 90144 | tf_op jit(solution)/shard_map/ppermute | solution.py:879
  254.6 3.8 %collective-permute-done.40.b1 = bf16[4,352,128]{2,1,0:T(8,128)(2,1)S(1)} collective-permute-done((bf16[4,352,128]{2,1,0:T(8,128)(2,1)S(1)}, bf16[4,352,128]{2,1,0:T(8,128)(2,1)S(1)}, u32[]{:S(2)}, u32[]{:S(2)}) %collective-permute-start.40) | collective-permute-done | bytes 360480 | tf_op jit(solution)/shard_map/ppermute | solution.py:883
  258.4 8.7 %unpack.1 = (f32[160,1024]{1,0:T(8,128)}, f32[160,256]{1,0:T(8,128)}, f32[160,256]{1,0:T(8,128)}, f32[256,640]{1,0:T(8,128)}, f32[160,2048]{1,0:T(8,128)}, /*ind...) custom-call(s32[2]{0:T(128)S(1)} %pad_add_fusion.spot, bf16[4,352,128]{2,1,0:T(8,128)(2,1)S(1)} %pad_maximum_fusion.a0, ...), custom_call_target="tpu_custom_call" | custom-call | flops 4000000 | bytes 11000000 | tf_op jit(solution)/shard_map/unpack/pallas_call | solution.py:727
  (191 shorter events, 66.2 us)
Async XLA Ops:
  3.0 40.1 %collective-permute-start.2 = (bf16[160,3072]{1,0:T(8,128)(2,1)S(1)}, bf16[160,3072]{1,0:T(8,128)(2,1)S(1)}, u32[]{:S(2)}, u32[]{:S(2)}) collective-permute-start(bf16[160,3072]{1,0:T(8,128)(2,1)S(1)} %constant_dynamic-update-slice_fusion.q0.g0), channel_id=1, source_target_pairs={{0,2},{1,3},{2,0},{3,1},{4,6},{5,7},{6,4},{7,5},{8,10},{9,11},{10,... | collective-permute-start | bytes 2949128 | tf_op jit(solution)/shard_map/ppermute | solution.py:867
  5.2 38.3 %collective-permute-start.5 = (bf16[160,2560]{1,0:T(8,128)(2,1)S(1)}, bf16[160,2560]{1,0:T(8,128)(2,1)}, u32[]{:S(2)}, u32[]{:S(2)}) collective-permute-start(bf16[160,2560]{1,0:T(8,128)(2,1)S(1)} %constant_dynamic-update-slice_fusion.2.kv0.u0), channel_id=1, source_target_pairs={{0,66},{1,67},{2,64},{3,65},{4,70},{5,71},{6,68},{7,69},{8,74},{9,... | collective-permute-start | bytes 2457608 | tf_op jit(solution)/shard_map/ppermute | solution.py:871
  7.8 37.0 %collective-permute-start.4 = (bf16[160,2560]{1,0:T(8,128)(2,1)S(1)}, bf16[160,2560]{1,0:T(8,128)(2,1)}, u32[]{:S(2)}, u32[]{:S(2)}) collective-permute-start(bf16[160,2560]{1,0:T(8,128)(2,1)S(1)} %constant_dynamic-update-slice_fusion.2.kv0.u0), channel_id=1, source_target_pairs={{0,1},{1,0},{2,3},{3,2},{4,5},{5,4},{6,7},{7,6},{8,9},{9,8},{10,11... | collective-permute-start | bytes 2457608 | tf_op jit(solution)/shard_map/ppermute | solution.py:863
  7.8 40.7 %collective-permute-start.1 = (bf16[160,3072]{1,0:T(8,128)(2,1)S(1)}, bf16[160,3072]{1,0:T(8,128)(2,1)}, u32[]{:S(2)}, u32[]{:S(2)}) collective-permute-start(bf16[160,3072]{1,0:T(8,128)(2,1)S(1)} %constant_dynamic-update-slice_fusion.q0.g0), channel_id=1, source_target_pairs={{0,1},{1,0},{2,3},{3,2},{4,5},{5,4},{6,7},{7,6},{8,9},{9,8},{10,11... | collective-permute-start | bytes 2949128 | tf_op jit(solution)/shard_map/ppermute | solution.py:863
  8.3 35.4 %collective-permute-start = (bf16[512,640]{1,0:T(8,128)(2,1)S(1)}, bf16[512,640]{1,0:T(8,128)(2,1)S(1)}, u32[]{:S(2)}, u32[]{:S(2)}) collective-permute-start(bf16[512,640]{1,0:T(8,128)(2,1)S(1)} %bitcast.47), channel_id=1, source_target_pairs={{0,4},{4,8},{8,12},{12,16},{16,20},{20,24},{24,28},{28,32},{32,36}... | collective-permute-start | bytes 1966088 | tf_op jit(solution)/shard_map/ppermute | solution.py:888
  44.6 18.5 %collective-permute-start.8 = (bf16[512,640]{1,0:T(8,128)(2,1)}, bf16[512,640]{1,0:T(8,128)(2,1)}, u32[]{:S(2)}, u32[]{:S(2)}) collective-permute-start(bf16[512,640]{1,0:T(8,128)(2,1)} %d0.1), channel_id=1, source_target_pairs={{0,66},{1,67},{2,64},{3,65},{4,70},{5,71},{6,68},{7,69},{8,74},{9,... | collective-permute-start | bytes 1966088 | tf_op jit(solution)/shard_map/ppermute | solution.py:871
  44.8 16.2 %collective-permute-start.7 = (bf16[256,640]{1,0:T(8,128)(2,1)}, bf16[256,640]{1,0:T(8,128)(2,1)}, u32[]{:S(2)}, u32[]{:S(2)}) collective-permute-start(bf16[256,640]{1,0:T(8,128)(2,1)} %o0.1), channel_id=1, source_target_pairs={{0,2},{1,3},{2,0},{3,1},{4,6},{5,7},{6,4},{7,5},{8,10},{9,11},{10,... | collective-permute-start | bytes 983048 | tf_op jit(solution)/shard_map/ppermute | solution.py:867
  48.5 23.3 %collective-permute-start.11 = (bf16[512,640]{1,0:T(8,128)(2,1)}, bf16[512,640]{1,0:T(8,128)(2,1)}, u32[]{:S(2)}, u32[]{:S(2)}) collective-permute-start(bf16[512,640]{1,0:T(8,128)(2,1)} %d0.1), channel_id=1, source_target_pairs={{0,1},{1,0},{2,3},{3,2},{4,5},{5,4},{6,7},{7,6},{8,9},{9,8},{10,11... | collective-permute-start | bytes 1966088 | tf_op jit(solution)/shard_map/ppermute | solution.py:863
  109.2 26.4 %collective-permute-start.13 = (bf16[2,7680,128]{2,1,0:T(8,128)(2,1)}, bf16[2,7680,128]{2,1,0:T(8,128)(2,1)}, u32[]{:S(2)}, u32[]{:S(2)}) collective-permute-start(bf16[2,7680,128]{2,1,0:T(8,128)(2,1)} %get-tuple-element.97), channel_id=1, source_target_pairs={{0,1},{1,0},{2,3},{3,2},{4,5},{5,4},{6,7},{7,6},{8,9},{9,8},{10,11... | collective-permute-start | bytes 11796488 | tf_op jit(solution)/shard_map/ppermute | solution.py:863
  142.8 34.9 %collective-permute-start.15 = (bf16[2,4,352,128]{3,2,1,0:T(8,128)(2,1)S(1)}, bf16[2,4,352,128]{3,2,1,0:T(8,128)(2,1)S(1)}, u32[]{:S(2)}, u32[]{:S(2)}) collective-permute-start(bf16[2,4,352,128]{3,2,1,0:T(8,128)(2,1)S(1)} %get-tuple-element.101), channel_id=1, source_target_pairs={{0,16},{4,20},{8,24},{12,28},{16,32},{20,36},{24,40},{28,44},{32,4... | collective-permute-start | bytes 2162696 | tf_op jit(solution)/shard_map/ppermute | solution.py:879
  142.8 35.0 %collective-permute-start.16 = (bf16[2,4,352,128]{3,2,1,0:T(8,128)(2,1)S(1)}, bf16[2,4,352,128]{3,2,1,0:T(8,128)(2,1)S(1)}, u32[]{:S(2)}, u32[]{:S(2)}) collective-permute-start(bf16[2,4,352,128]{3,2,1,0:T(8,128)(2,1)S(1)} %get-tuple-element.102), channel_id=1, source_target_pairs={{0,48},{4,52},{8,56},{12,60},{16,0},{20,4},{24,8},{28,12},{32,16},... | collective-permute-start | bytes 2162696 | tf_op jit(solution)/shard_map/ppermute | solution.py:879
  146.1 33.1 %collective-permute-start.17 = (bf16[2,4,352,128]{3,2,1,0:T(8,128)(2,1)S(1)}, bf16[2,4,352,128]{3,2,1,0:T(8,128)(2,1)S(1)}, u32[]{:S(2)}, u32[]{:S(2)}) collective-permute-start(bf16[2,4,352,128]{3,2,1,0:T(8,128)(2,1)S(1)} %get-tuple-element.103), channel_id=1, source_target_pairs={{0,32},{4,36},{8,40},{12,44},{16,48},{20,52},{24,56},{28,60},{32,0... | collective-permute-start | bytes 2162696 | tf_op jit(solution)/shard_map/ppermute | solution.py:879
  146.1 33.1 %collective-permute-start.18 = (bf16[2,4,352,128]{3,2,1,0:T(8,128)(2,1)S(1)}, bf16[2,4,352,128]{3,2,1,0:T(8,128)(2,1)S(1)}, u32[]{:S(2)}, u32[]{:S(2)}) collective-permute-start(bf16[2,4,352,128]{3,2,1,0:T(8,128)(2,1)S(1)} %get-tuple-element.105), channel_id=1, source_target_pairs={{0,4},{4,8},{8,12},{12,0},{16,20},{20,24},{24,28},{28,16},{32,36},... | collective-permute-start | bytes 2162696 | tf_op jit(solution)/shard_map/ppermute | solution.py:883
  146.1 47.6 %collective-permute-start.19 = (bf16[2,4,352,128]{3,2,1,0:T(8,128)(2,1)S(1)}, bf16[2,4,352,128]{3,2,1,0:T(8,128)(2,1)S(1)}, u32[]{:S(2)}, u32[]{:S(2)}) collective-permute-start(bf16[2,4,352,128]{3,2,1,0:T(8,128)(2,1)S(1)} %get-tuple-element.106), channel_id=1, source_target_pairs={{0,12},{4,0},{8,4},{12,8},{16,28},{20,16},{24,20},{28,24},{32,44},... | collective-permute-start | bytes 2162696 | tf_op jit(solution)/shard_map/ppermute | solution.py:883
  177.7 19.0 %collective-permute-start.20 = (bf16[2,4,352,128]{3,2,1,0:T(8,128)(2,1)S(1)}, bf16[2,4,352,128]{3,2,1,0:T(8,128)(2,1)S(1)}, u32[]{:S(2)}, u32[]{:S(2)}) collective-permute-start(bf16[2,4,352,128]{3,2,1,0:T(8,128)(2,1)S(1)} %get-tuple-element.107), channel_id=1, source_target_pairs={{0,8},{4,12},{8,0},{12,4},{16,24},{20,28},{24,16},{28,20},{32,40},... | collective-permute-start | bytes 2162696 | tf_op jit(solution)/shard_map/ppermute | solution.py:883
  177.8 47.0 %collective-permute-start.30 = (bf16[512,640]{1,0:T(8,128)(2,1)S(1)}, bf16[512,640]{1,0:T(8,128)(2,1)S(1)}, u32[]{:S(2)}, u32[]{:S(2)}) collective-permute-start(bf16[512,640]{1,0:T(8,128)(2,1)S(1)} %copy-done.35), channel_id=1, source_target_pairs={{4,0},{8,4},{12,8},{16,12},{20,16},{24,20},{28,24},{32,28},{36,32}... | collective-permute-start | bytes 1966088 | tf_op jit(solution)/shard_map/ppermute | solution.py:888
  197.9 10.6 %collective-permute-start.21 = (bf16[2,352,128]{2,1,0:T(8,128)(2,1)S(1)}, bf16[2,352,128]{2,1,0:T(8,128)(2,1)S(1)}, u32[]{:S(2)}, u32[]{:S(2)}) collective-permute-start(bf16[2,352,128]{2,1,0:T(8,128)(2,1)S(1)} %get-tuple-element.109), channel_id=1, source_target_pairs={{0,4},{4,8},{8,12},{12,0},{16,20},{20,24},{24,28},{28,16},{32,36},... | collective-permute-start | bytes 540680 | tf_op jit(solution)/shard_map/ppermute | solution.py:883
  198.0 10.6 %collective-permute-start.22 = (bf16[2,352,128]{2,1,0:T(8,128)(2,1)S(1)}, bf16[2,352,128]{2,1,0:T(8,128)(2,1)S(1)}, u32[]{:S(2)}, u32[]{:S(2)}) collective-permute-start(bf16[2,352,128]{2,1,0:T(8,128)(2,1)S(1)} %get-tuple-element.110), channel_id=1, source_target_pairs={{0,12},{4,0},{8,4},{12,8},{16,28},{20,16},{24,20},{28,24},{32,44},... | collective-permute-start | bytes 540680 | tf_op jit(solution)/shard_map/ppermute | solution.py:883
  231.1 9.5 %collective-permute-start.34 = (bf16[352,128]{1,0:T(8,128)(2,1)S(1)}, bf16[352,128]{1,0:T(8,128)(2,1)S(1)}, u32[]{:S(2)}, u32[]{:S(2)}) collective-permute-start(bf16[352,128]{1,0:T(8,128)(2,1)S(1)} %get-tuple-element.124), channel_id=1, source_target_pairs={{0,16},{4,20},{8,24},{12,28},{16,32},{20,36},{24,40},{28,44},{32,4... | collective-permute-start | bytes 270344 | tf_op jit(solution)/shard_map/ppermute | solution.py:879
  240.7 11.6 %collective-permute-start.38 = (bf16[4,352,128]{2,1,0:T(8,128)(2,1)S(1)}, bf16[4,352,128]{2,1,0:T(8,128)(2,1)S(1)}, u32[]{:S(2)}, u32[]{:S(2)}) collective-permute-start(bf16[4,352,128]{2,1,0:T(8,128)(2,1)S(1)} %pad_maximum_fusion.a0), channel_id=1, source_target_pairs={{0,32},{4,36},{8,40},{12,44},{16,48},{20,52},{24,56},{28,60},{32,0... | collective-permute-start | bytes 1081352 | tf_op jit(solution)/shard_map/ppermute | solution.py:879
  241.9 11.6 %collective-permute-start.37 = (bf16[4,352,128]{2,1,0:T(8,128)(2,1)S(1)}, bf16[4,352,128]{2,1,0:T(8,128)(2,1)S(1)}, u32[]{:S(2)}, u32[]{:S(2)}) collective-permute-start(bf16[4,352,128]{2,1,0:T(8,128)(2,1)S(1)} %pad_maximum_fusion.a0), channel_id=1, source_target_pairs={{0,16},{4,20},{8,24},{12,28},{16,32},{20,36},{24,40},{28,44},{32,4... | collective-permute-start | bytes 1081352 | tf_op jit(solution)/shard_map/ppermute | solution.py:879
  243.3 11.2 %collective-permute-start.42 = (bf16[4,352,128]{2,1,0:T(8,128)(2,1)S(1)}, bf16[4,352,128]{2,1,0:T(8,128)(2,1)S(1)}, u32[]{:S(2)}, u32[]{:S(2)}) collective-permute-start(bf16[4,352,128]{2,1,0:T(8,128)(2,1)S(1)} %pad_maximum_fusion.1.b0), channel_id=1, source_target_pairs={{0,12},{4,0},{8,4},{12,8},{16,28},{20,16},{24,20},{28,24},{32,44},... | collective-permute-start | bytes 1081352 | tf_op jit(solution)/shard_map/ppermute | solution.py:883
  245.6 9.0 %collective-permute-start.41 = (bf16[4,352,128]{2,1,0:T(8,128)(2,1)S(1)}, bf16[4,352,128]{2,1,0:T(8,128)(2,1)S(1)}, u32[]{:S(2)}, u32[]{:S(2)}) collective-permute-start(bf16[4,352,128]{2,1,0:T(8,128)(2,1)S(1)} %pad_maximum_fusion.1.b0), channel_id=1, source_target_pairs={{0,8},{4,12},{8,0},{12,4},{16,24},{20,28},{24,16},{28,20},{32,40},... | collective-permute-start | bytes 1081352 | tf_op jit(solution)/shard_map/ppermute | solution.py:883
  248.1 10.3 %collective-permute-start.40 = (bf16[4,352,128]{2,1,0:T(8,128)(2,1)S(1)}, bf16[4,352,128]{2,1,0:T(8,128)(2,1)S(1)}, u32[]{:S(2)}, u32[]{:S(2)}) collective-permute-start(bf16[4,352,128]{2,1,0:T(8,128)(2,1)S(1)} %pad_maximum_fusion.1.b0), channel_id=1, source_target_pairs={{0,4},{4,8},{8,12},{12,0},{16,20},{20,24},{24,28},{28,16},{32,36},... | collective-permute-start | bytes 1081352 | tf_op jit(solution)/shard_map/ppermute | solution.py:883
  (66 other events, 817.2 us)

commit v3 on v2

--- a/solution.py
+++ b/solution.py
@@ -56,14 +56,14 @@
     return jnp.concatenate([a * cosine + b * sine, b * cosine - a * sine], axis=1)
 
 
-def assemble(pieces, into, place, semaphores, first, column=0):
+def assemble(pieces, into, place, semaphores, first):
     rows = into.shape[0] // 4
     copies = []
     for r in range(4):
         at = pl.ds(pl.multiple_of((place ^ r) * rows, rows), rows)
         copies.append(
             pltpu.make_async_copy(
-                pieces[r].at[:, pl.ds(column, into.shape[1])],
+                pieces[r],
                 into.at[at, :],
                 semaphores.at[first + r],
             )
@@ -214,7 +214,7 @@
             pltpu.VMEM((640, 512), bf16),
             pltpu.SemaphoreType.DMA((8,)),
         ],
-        compiler_params=params(20),
+        compiler_params=params(14),
         cost_estimate=cost(1_350_000_000, 9_000_000),
     )(place, halo, own, gains, head_gains, *q_shares, *kv_shares, cosine, sine)
 
@@ -262,7 +262,7 @@
             pl.BlockSpec((4, 256, 1), lambda i: (0, i, 0)),
         ],
         out_shape=[spec(512, 1024, bf16), spec(4, 512, 1, f32)],
-        compiler_params=params(20),
+        compiler_params=params(10),
         cost_estimate=cost(1_700_000_000, 4_000_000, 2_000_000),
     )(q, k, v, offsets)
 
@@ -313,8 +313,8 @@
     semaphores,
 ):
     output_copies = assemble((o0, o1, o2, o3), wo, place[0], semaphores, 0)
-    gate_copies = assemble((g0, g1, g2, g3), wg, place[0], semaphores, 4, 1024)
-    up_copies = assemble((u0, u1, u2, u3), wu, place[0], semaphores, 8, 512)
+    gate_copies = assemble((g0, g1, g2, g3), wg, place[0], semaphores, 4)
+    up_copies = assemble((u0, u1, u2, u3), wu, place[0], semaphores, 8)
     down_copies = assemble((d0, d1, d2, d3), wd, place[0], semaphores, 12)
     for copy in output_copies:
         copy.wait()
@@ -423,7 +423,7 @@
             pltpu.VMEM((4, 7680, 128), bf16),
             pltpu.SemaphoreType.DMA((20,)),
         ],
-        compiler_params=params(46),
+        compiler_params=params(44),
         cost_estimate=cost(13_400_000_000, 23_000_000, 1_000_000),
     )(place, x, attended, upstream, gains, *shares)
 
@@ -538,7 +538,7 @@
             pltpu.VMEM((640, 512), bf16),
             pltpu.SemaphoreType.DMA((4,)),
         ],
-        compiler_params=params(30),
+        compiler_params=params(16),
         cost_estimate=cost(4_300_000_000, 10_000_000, 2_000_000),
     )(
         q, k, v, offsets, level, back_attended, q_proj, k_proj, head_gains, cosine, sine, place, *shares
@@ -638,7 +638,7 @@
             pltpu.VMEM((4, 3584, 128), bf16),
             pltpu.SemaphoreType.DMA((12,)),
         ],
-        compiler_params=params(40),
+        compiler_params=params(24),
         cost_estimate=cost(3_400_000_000, 14_000_000),
     )(place, normed, back_q, back_kv, attended, back_attn, halo, own, gain_mid, gain_head, *shares)
 
@@ -736,7 +736,7 @@
             pltpu.VMEM((3584, 128), bf16),
             pltpu.SemaphoreType.DMA((71,)),
         ],
-        compiler_params=params(20),
+        compiler_params=params(14),
         cost_estimate=cost(4_000_000, 11_000_000),
     )(spot, *pieces)
 
@@ -771,7 +771,7 @@
         in_specs=[pl.BlockSpec(memory_space=pltpu.SMEM)] + [whole()] * 4,
         out_specs=[whole()] * 8,
         out_shape=[spec(2, 4, 352, 128, bf16)] * 8,
-        compiler_params=params(30),
+        compiler_params=params(24),
         cost_estimate=cost(3_000_000, 17_000_000),
     )(spot, *ins)
 
@@ -793,7 +793,7 @@
         in_specs=[pl.BlockSpec(memory_space=pltpu.SMEM)] + [whole()] * 8,
         out_specs=[whole()] * 8,
         out_shape=[spec(2, 352, 128, bf16)] * 8,
-        compiler_params=params(20),
+        compiler_params=params(12),
         cost_estimate=cost(1_000_000, 7_200_000),
     )(spot, *parts)
 
@@ -865,6 +865,10 @@
 
 def swap_near(value):
     return lax.ppermute(value, "fsdp", [(0, 2), (1, 3), (2, 0), (3, 1)])
+
+
+def swap_across(value):
+    return lax.ppermute(value, "fsdp", [(0, 3), (1, 2), (2, 1), (3, 0)])
 
 
 def swap_far(value):
@@ -941,29 +945,48 @@
     upstream = cotangent[0]
     offsets = positions[0]
 
-    near = jnp.concatenate([query_weight, gate_weight], axis=1)
-    far = jnp.concatenate([key_weight, value_weight, up_weight], axis=1)
-    near_partner, far_partner = swap_near(near), swap_far(far)
+    q_partner = swap_near(query_weight)
+    kv = jnp.concatenate([key_weight, value_weight], axis=1)
+    kv_partner = swap_far(kv)
+    wg_partner, wu_partner = swap_near(gate_weight), swap_far(up_weight)
     halo = shifted(own, 1)
-    q_shares = (near, swap_core(near), near_partner, swap_core(near_partner))
-    kv_shares = (far, swap_core(far), far_partner, swap_core(far_partner))
+    rows = (norm_in, norm_attn, norm_ffn_in, norm_ffn_out, norm_query, norm_key)
+    q_partner, rows = together(q_partner, rows)
+    tile = pack(rows)
+    tiles = [tile, swap_core(tile), swap_near(tile), swap_across(tile)]
+    tiles = [
+        jnp.where(
+            j // 2 == z_lo,
+            jnp.where(j % 2 == core, tiles[0], tiles[1]),
+            jnp.where(j % 2 == core, tiles[2], tiles[3]),
+        )
+        for j in range(4)
+    ]
+    gains = jnp.concatenate([t[:, :160] for t in tiles], axis=1)
+    head_gains = jnp.concatenate([t[:, :64] for t in tiles], axis=1)
+    q_shares = (query_weight, swap_core(query_weight), q_partner, swap_core(q_partner))
+    kv_shares = (kv, swap_core(kv), kv_partner, swap_core(kv_partner))
+    (q_shares, kv_shares, halo), (wg_partner, wu_partner) = together(
+        (q_shares, kv_shares, halo), (wg_partner, wu_partner)
+    )
     wo_partner, wd_partner = swap_near(output_weight), swap_far(down_weight)
-    tile = pack([norm_in, norm_attn, norm_ffn_in, norm_ffn_out, norm_query, norm_key])
-    tiles = lax.all_gather(tile, "fsdp")
-    gains = jnp.concatenate([tiles[j, :, :160] for j in range(4)], axis=1)
-    head_gains = jnp.concatenate([tiles[j, :, :64] for j in range(4)], axis=1)
 
     cosine, sine = rope_tables(offsets)
     column = offsets[:, None]
     normed, q, k, v, q_proj, k_proj = project(
         place, halo, own, gains, head_gains, q_shares, kv_shares, cosine, sine
     )
-    (q, k, v), wo_partner, wd_partner = together((q, k, v), wo_partner, wd_partner)
-    wo_shares = (output_weight, swap_core(output_weight), wo_partner, swap_core(wo_partner))
-    wd_shares = (down_weight, swap_core(down_weight), wd_partner, swap_core(wd_partner))
     attended, level = attend(q, k, v, column)
+    own_weights = (output_weight, gate_weight, up_weight, down_weight)
+    partners = (wo_partner, wg_partner, wu_partner, wd_partner)
+    attended, own_weights = together(attended, own_weights)
+    siblings = [swap_core(w) for w in own_weights]
+    shares = []
+    for share, sibling, partner in zip(own_weights, siblings, partners):
+        attended, partner = together(attended, partner)
+        shares += [share, sibling, partner, swap_core(partner)]
     layer_out, back_middle, back_attn, back_attended, gain_mid, kept, sent = middle_part(
-        place, own, attended, upstream, gains, wo_shares + q_shares + kv_shares + wd_shares
+        place, own, attended, upstream, gains, shares
     )
     got = swap_core(sent)
     back_q, back_kv, gain_head, back_halo = attend_back(

time: 272 us -> 274 us (level)
  blocking collectives: 30 us -> 0 us
  waiting for transfers between devices: 84.1 us -> 103 us
  starting transfers between devices: 46.2 us -> 56.3 us
    all_gather x1 -> x0, blocking collectives: 30 us -> none  [body(): tiles = lax.all_gather(tile, 'fsdp')]
    ppermute x3 -> x5, waiting for transfers between devices: 0.01 us -> 11.2 us  [swap_near(): return lax.ppermute(value, 'fsdp', [(0, 2), (1, 3), (2, 0), (3, 1)])]
    ppermute x10 -> x15, waiting for transfers between devices: 3.89 us -> 11.1 us  [swap_core(): return lax.ppermute(value, 'fsdp', [(0, 1), (1, 0), (2, 3), (3, 2)])]
    ppermute x10 -> x15, starting transfers between devices: 2.38 us -> 9.53 us  [swap_core(): return lax.ppermute(value, 'fsdp', [(0, 1), (1, 0), (2, 3), (3, 2)])]
    unnamed x97 -> x81, local copies, waits for them, and re-layouts: 19.4 us -> 18.3 us
  transfers between devices with their start and end apart: 43 -> 52, of which waited for: 19 -> 28; matrix products, arithmetic and copies ran while one was open for 1% -> 2% of each run, Pallas kernels for 12% -> 11%
where the time goes in v3:
time: 274 us; the launch traced here: 269 us
  waiting for transfers between devices  103 us (38%)
  Pallas kernels  82 us (30%)
  starting transfers between devices  56.3 us (21%)
  local copies, waits for them, and re-layouts  21.7 us (8%)
  other arithmetic  3.5 us (1%)
    ppermute x12, waiting for transfers between devices, move_x(): return lax.ppermute(value, 'seq', along_xy(d, 0))  43.5 us
    pallas_call x1, Pallas kernels, middle_part(): pl.pallas_call(middle_kernel, name='middle_part', in_specs=[pl.BlockSpec(...  39 us
    ppermute x12, waiting for transfers between devices, move_y(): return lax.ppermute(value, 'seq', along_xy(0, d))  29.5 us
    unnamed x81, local copies, waits for them, and re-layouts  18.3 us
    ppermute x12, starting transfers between devices, move_y(): return lax.ppermute(value, 'seq', along_xy(0, d))  16.8 us
    ppermute x12, starting transfers between devices, move_x(): return lax.ppermute(value, 'seq', along_xy(d, 0))  12.1 us
    ppermute x5, waiting for transfers between devices, swap_near(): return lax.ppermute(value, 'fsdp', [(0, 2), (1, 3), (2, 0), (3, 1)])  11.2 us
    ppermute x15, waiting for transfers between devices, swap_core(): return lax.ppermute(value, 'fsdp', [(0, 1), (1, 0), (2, 3), (3, 2)])  11.1 us
  transfers between devices with their start and end apart: 52, of which 28 were waited for; matrix products, arithmetic and copies ran while one was open for 2% of the time, Pallas kernels for 11%

profile of v3, /device:TPU:0, one launch (start us, length us, event | category | flops | bytes accessed | tf_op | source)
XLA Modules:
  0.0 269.0 jit_solution(15824059990634345304)
XLA Ops:
  7.6 3.5 %collective-permute-start.6 = (bf16[512,640]{1,0:T(8,128)(2,1)}, bf16[512,640]{1,0:T(8,128)(2,1)S(1)}, u32[]{:S(2)}, u32[]{:S(2)}) collective-permute-start(bf16[512,640]{1,0:T(8,128)(2,1)} %bitcast.36), channel_id=1, source_target_pairs={{0,4},{4,8},{8,12},{12,16},{16,20},{20,24},{24,28},{28,32},{32,36}... | collective-permute-start | bytes 1966088 | tf_op jit(solution)/shard_map/ppermute | solution.py:892
  24.3 6.4 %collective-permute-start.9 = (f32[8,256]{1,0:T(8,128)S(1)}, f32[8,256]{1,0:T(8,128)S(1)}, u32[]{:S(2)}, u32[]{:S(2)}) collective-permute-start(f32[8,256]{1,0:T(8,128)S(1)} %pack.1), channel_id=1, source_target_pairs={{0,1},{1,0},{2,3},{3,2},{4,5},{5,4},{6,7},{7,6},{8,9},{9,8},{10,11... | collective-permute-start | bytes 24584 | tf_op jit(solution)/shard_map/ppermute | solution.py:863
  33.4 11.2 %collective-permute-done.10 = f32[8,256]{1,0:T(8,128)S(1)} collective-permute-done((f32[8,256]{1,0:T(8,128)S(1)}, f32[8,256]{1,0:T(8,128)S(1)}, u32[]{:S(2)}, u32[]{:S(2)}) %collective-permute-start.10) | collective-permute-done | bytes 8224 | tf_op jit(solution)/shard_map/ppermute | solution.py:867
  52.0 5.3 %project.1 = (bf16[1024,640]{1,0:T(8,128)(2,1)S(1)}, bf16[512,1024]{1,0:T(8,128)(2,1)S(1)}, bf16[1024,256]{1,0:T(8,128)(2,1)S(1)}, bf16[1024,256]{1,0:T(8,128)(2...) custom-call(s32[1]{0:T(128)} %bitcast.place, bf16[512,640]{1,0:T(8,128)(2,1)S(1)} %collective-permute-done.6.halo, ...), custom_call_target="tpu_custom_call" | custom-call | flops 1350000000 | bytes 9000000 | tf_op jit(solution)/shard_map/project/pallas_call | solution.py:183
  57.3 3.9 %attend.1 = (bf16[512,1024]{1,0:T(8,128)(2,1)S(1)}, f32[4,512,1]{2,1,0:T(8,128)S(1)}) custom-call(bf16[512,1024]{1,0:T(8,128)(2,1)S(1)} %get-tuple-element.117.q, bf16[1024,256]{1,0:T(8,128)(2,1)S(1)} %get-tuple-element.118.k, bf16[1024,256]{1,0:T(8,128)(2,1)S(1)} %get-tuple-element.119.v, s32[512,1]{1,0:T(8,128)S(1)} %copy.31.offsets), custom_call_target="tpu_custom_call" | custom-call | flops 1700000000 | bytes 4000000 | tf_op jit(solution)/shard_map/attend/pallas_call | solution.py:250
  70.5 39.0 %middle_part.1 = (bf16[512,640]{1,0:T(8,128)(2,1)}, f32[512,640]{1,0:T(8,128)}, bf16[512,640]{1,0:T(8,128)(2,1)S(1)}, bf16[512,1024]{1,0:T(8,128)(2,1)}, f32[8,6...) custom-call(s32[1]{0:T(128)} %bitcast.place, bf16[512,640]{1,0:T(8,128)(2,1)S(1)} %bitcast.38, ...), custom_call_target="tpu_custom_call" | custom-call | flops 13400000512 | bytes 23000000 | tf_op jit(solution)/shard_map/middle_part/pallas_call | solution.py:393
  112.3 10.0 %attend_back.1 = (bf16[512,1024]{1,0:T(8,128)(2,1)S(1)}, bf16[1024,512]{1,0:T(8,128)(2,1)S(1)}, f32[8,256]{1,0:T(8,128)S(1)}, bf16[512,640]{1,0:T(8,128)(2,1)S(1)}) custom-call(bf16[512,1024]{1,0:T(8,128)(2,1)S(1)} %get-tuple-element.117.q, bf16[1024,256]{1,0:T(8,128)(2,1)S(1)} %get-tuple-element.118.k, bf16[1024,256]{1,0:T(8,128)(2,1)S(1)} %get-tuple-element.119.v, ...), custom_call_target="tpu_custom_call" | custom-call | flops 4300000256 | bytes 10000000 | tf_op jit(solution)/shard_map/attend_back/pallas_call | solution.py:504
  124.8 7.5 %weights_part.1 = (f32[512,640]{1,0:T(8,128)S(1)}, bf16[2,3584,128]{2,1,0:T(8,128)(2,1)S(1)}, bf16[2,3584,128]{2,1,0:T(8,128)(2,1)}) custom-call(s32[1]{0:T(128)} %bitcast.place, bf16[1024,640]{1,0:T(8,128)(2,1)S(1)} %get-tuple-element.137.normed, bf16[512,1024]{1,0:T(8,128)(2,1)S(1)} %get-tuple-element.142.back_q, ...), custom_call_target="tpu_custom_call" | custom-call | flops 3400000000 | bytes 14000000 | tf_op jit(solution)/shard_map/weights_part/pallas_call | solution.py:623
  132.8 3.7 %collective-permute-done.23 = bf16[2,3584,128]{2,1,0:T(8,128)(2,1)} collective-permute-done((bf16[2,3584,128]{2,1,0:T(8,128)(2,1)}, bf16[2,3584,128]{2,1,0:T(8,128)(2,1)}, u32[]{:S(2)}, u32[]{:S(2)}) %collective-permute-start.23) | collective-permute-done | bytes 1835040 | tf_op jit(solution)/shard_map/ppermute | solution.py:863
  138.6 4.1 %first_sums.1 = (bf16[2,4,352,128]{3,2,1,0:T(8,128)(2,1)S(1)}, bf16[2,4,352,128]{3,2,1,0:T(8,128)(2,1)S(1)}, bf16[2,4,352,128]{3,2,1,0:T(8,128)(2,1)S(1)}, bf16[...) custom-call(s32[2]{0:T(128)S(1)} %pad_add_fusion.spot, ...), custom_call_target="tpu_custom_call" | custom-call | flops 3000000 | bytes 17000000 | tf_op jit(solution)/shard_map/first_sums/pallas_call | solution.py:768
  142.8 3.2 %collective-permute-start.25 = (bf16[2,4,352,128]{3,2,1,0:T(8,128)(2,1)S(1)}, bf16[2,4,352,128]{3,2,1,0:T(8,128)(2,1)S(1)}, u32[]{:S(2)}, u32[]{:S(2)}) collective-permute-start(bf16[2,4,352,128]{3,2,1,0:T(8,128)(2,1)S(1)} %get-tuple-element.154), channel_id=1, source_target_pairs={{0,48},{4,52},{8,56},{12,60},{16,0},{20,4},{24,8},{28,12},{32,16},... | collective-permute-start | bytes 2162696 | tf_op jit(solution)/shard_map/ppermute | solution.py:883
  146.0 3.4 %collective-permute-start.28 = (bf16[2,4,352,128]{3,2,1,0:T(8,128)(2,1)S(1)}, bf16[2,4,352,128]{3,2,1,0:T(8,128)(2,1)S(1)}, u32[]{:S(2)}, u32[]{:S(2)}) collective-permute-start(bf16[2,4,352,128]{3,2,1,0:T(8,128)(2,1)S(1)} %get-tuple-element.158), channel_id=1, source_target_pairs={{0,12},{4,0},{8,4},{12,8},{16,28},{20,16},{24,20},{28,24},{32,44},... | collective-permute-start | bytes 2162696 | tf_op jit(solution)/shard_map/ppermute | solution.py:887
  149.4 28.4 %collective-permute-done.24.refs_1_ = bf16[2,4,352,128]{3,2,1,0:T(8,128)(2,1)S(1)} collective-permute-done((bf16[2,4,352,128]{3,2,1,0:T(8,128)(2,1)S(1)}, bf16[2,4,352,128]{3,2,1,0:T(8,128)(2,1)S(1)}, u32[]{:S(2)}, u32[]{:S(2)}) %collective-permute-start.24) | collective-permute-done | bytes 720928 | tf_op jit(solution)/shard_map/ppermute | solution.py:883
  179.1 14.8 %collective-permute-done.28.refs_6_ = bf16[2,4,352,128]{3,2,1,0:T(8,128)(2,1)S(1)} collective-permute-done((bf16[2,4,352,128]{3,2,1,0:T(8,128)(2,1)S(1)}, bf16[2,4,352,128]{3,2,1,0:T(8,128)(2,1)S(1)}, u32[]{:S(2)}, u32[]{:S(2)}) %collective-permute-start.28) | collective-permute-done | bytes 720928 | tf_op jit(solution)/shard_map/ppermute | solution.py:887
  193.9 3.0 %collective-permute-done.29.refs_7_ = bf16[2,4,352,128]{3,2,1,0:T(8,128)(2,1)S(1)} collective-permute-done((bf16[2,4,352,128]{3,2,1,0:T(8,128)(2,1)S(1)}, bf16[2,4,352,128]{3,2,1,0:T(8,128)(2,1)S(1)}, u32[]{:S(2)}, u32[]{:S(2)}) %collective-permute-start.29) | collective-permute-done | bytes 720928 | tf_op jit(solution)/shard_map/ppermute | solution.py:887
  198.3 3.2 %collective-permute-start.31 = (bf16[2,352,128]{2,1,0:T(8,128)(2,1)S(1)}, bf16[2,352,128]{2,1,0:T(8,128)(2,1)S(1)}, u32[]{:S(2)}, u32[]{:S(2)}) collective-permute-start(bf16[2,352,128]{2,1,0:T(8,128)(2,1)S(1)} %get-tuple-element.162), channel_id=1, source_target_pairs={{0,12},{4,0},{8,4},{12,8},{16,28},{20,16},{24,20},{28,24},{32,44},... | collective-permute-start | bytes 540680 | tf_op jit(solution)/shard_map/ppermute | solution.py:887
  201.5 3.1 %collective-permute-start.33 = (bf16[2,352,128]{2,1,0:T(8,128)(2,1)S(1)}, bf16[2,352,128]{2,1,0:T(8,128)(2,1)S(1)}, u32[]{:S(2)}, u32[]{:S(2)}) collective-permute-start(bf16[2,352,128]{2,1,0:T(8,128)(2,1)S(1)} %get-tuple-element.165), channel_id=1, source_target_pairs={{0,16},{4,20},{8,24},{12,28},{16,32},{20,36},{24,40},{28,44},{32,4... | collective-permute-start | bytes 540680 | tf_op jit(solution)/shard_map/ppermute | solution.py:883
  204.6 4.3 %collective-permute-done.30.refs_1_ = bf16[2,352,128]{2,1,0:T(8,128)(2,1)S(1)} collective-permute-done((bf16[2,352,128]{2,1,0:T(8,128)(2,1)S(1)}, bf16[2,352,128]{2,1,0:T(8,128)(2,1)S(1)}, u32[]{:S(2)}, u32[]{:S(2)}) %collective-permute-start.30) | collective-permute-done | bytes 180256 | tf_op jit(solution)/shard_map/ppermute | solution.py:887
  208.9 5.4 %collective-permute-done.34.refs_6_ = bf16[2,352,128]{2,1,0:T(8,128)(2,1)S(1)} collective-permute-done((bf16[2,352,128]{2,1,0:T(8,128)(2,1)S(1)}, bf16[2,352,128]{2,1,0:T(8,128)(2,1)S(1)}, u32[]{:S(2)}, u32[]{:S(2)}) %collective-permute-start.34) | collective-permute-done | bytes 180256 | tf_op jit(solution)/shard_map/ppermute | solution.py:883
  219.6 3.5 %collective-permute-done.38.p3 = bf16[2,352,128]{2,1,0:T(8,128)(2,1)S(1)} collective-permute-done((bf16[2,352,128]{2,1,0:T(8,128)(2,1)S(1)}, bf16[2,352,128]{2,1,0:T(8,128)(2,1)S(1)}, u32[]{:S(2)}, u32[]{:S(2)}) %collective-permute-start.38) | collective-permute-done | bytes 180256 | tf_op jit(solution)/shard_map/ppermute | solution.py:879
  235.0 3.0 %collective-permute-done.44 = bf16[352,128]{1,0:T(8,128)(2,1)S(1)} collective-permute-done((bf16[352,128]{1,0:T(8,128)(2,1)S(1)}, bf16[352,128]{1,0:T(8,128)(2,1)S(1)}, u32[]{:S(2)}, u32[]{:S(2)}) %collective-permute-start.44) | collective-permute-done | bytes 90144 | tf_op jit(solution)/shard_map/ppermute | solution.py:883
  237.9 3.3 %collective-permute-done.43 = bf16[352,128]{1,0:T(8,128)(2,1)S(1)} collective-permute-done((bf16[352,128]{1,0:T(8,128)(2,1)S(1)}, bf16[352,128]{1,0:T(8,128)(2,1)S(1)}, u32[]{:S(2)}, u32[]{:S(2)}) %collective-permute-start.43) | collective-permute-done | bytes 90144 | tf_op jit(solution)/shard_map/ppermute | solution.py:883
  255.3 3.8 %collective-permute-done.49.b1 = bf16[4,352,128]{2,1,0:T(8,128)(2,1)S(1)} collective-permute-done((bf16[4,352,128]{2,1,0:T(8,128)(2,1)S(1)}, bf16[4,352,128]{2,1,0:T(8,128)(2,1)S(1)}, u32[]{:S(2)}, u32[]{:S(2)}) %collective-permute-start.49) | collective-permute-done | bytes 360480 | tf_op jit(solution)/shard_map/ppermute | solution.py:887
  259.0 8.7 %unpack.1 = (f32[160,1024]{1,0:T(8,128)}, f32[160,256]{1,0:T(8,128)}, f32[160,256]{1,0:T(8,128)}, f32[256,640]{1,0:T(8,128)}, f32[160,2048]{1,0:T(8,128)}, /*ind...) custom-call(s32[2]{0:T(128)S(1)} %pad_add_fusion.spot, bf16[4,352,128]{2,1,0:T(8,128)(2,1)S(1)} %pad_maximum_fusion.a0, ...), custom_call_target="tpu_custom_call" | custom-call | flops 4000000 | bytes 11000000 | tf_op jit(solution)/shard_map/unpack/pallas_call | solution.py:727
  (194 shorter events, 81.4 us)
Async XLA Ops:
  0.7 13.1 %collective-permute-start.1 = (bf16[160,1024]{1,0:T(8,128)(2,1)}, bf16[160,1024]{1,0:T(8,128)(2,1)S(1)}, u32[]{:S(2)}, u32[]{:S(2)}) collective-permute-start(bf16[160,1024]{1,0:T(8,128)(2,1)} %q0.1), channel_id=1, source_target_pairs={{0,2},{1,3},{2,0},{3,1},{4,6},{5,7},{6,4},{7,5},{8,10},{9,11},{10,... | collective-permute-start | bytes 983048 | tf_op jit(solution)/shard_map/ppermute | solution.py:867
  7.0 11.9 %collective-permute-start.3 = (bf16[160,512]{1,0:T(8,128)(2,1)S(1)}, bf16[160,512]{1,0:T(8,128)(2,1)S(1)}, u32[]{:S(2)}, u32[]{:S(2)}) collective-permute-start(bf16[160,512]{1,0:T(8,128)(2,1)S(1)} %constant_dynamic-update-slice_fusion.kv0), channel_id=1, source_target_pairs={{0,1},{1,0},{2,3},{3,2},{4,5},{5,4},{6,7},{7,6},{8,9},{9,8},{10,11... | collective-permute-start | bytes 491528 | tf_op jit(solution)/shard_map/ppermute | solution.py:863
  7.0 14.6 %collective-permute-start = (bf16[160,1024]{1,0:T(8,128)(2,1)}, bf16[160,1024]{1,0:T(8,128)(2,1)S(1)}, u32[]{:S(2)}, u32[]{:S(2)}) collective-permute-start(bf16[160,1024]{1,0:T(8,128)(2,1)} %q0.1), channel_id=1, source_target_pairs={{0,1},{1,0},{2,3},{3,2},{4,5},{5,4},{6,7},{7,6},{8,9},{9,8},{10,11... | collective-permute-start | bytes 983048 | tf_op jit(solution)/shard_map/ppermute | solution.py:863
  7.6 40.3 %collective-permute-start.6 = (bf16[512,640]{1,0:T(8,128)(2,1)}, bf16[512,640]{1,0:T(8,128)(2,1)S(1)}, u32[]{:S(2)}, u32[]{:S(2)}) collective-permute-start(bf16[512,640]{1,0:T(8,128)(2,1)} %bitcast.36), channel_id=1, source_target_pairs={{0,4},{4,8},{8,12},{12,16},{16,20},{20,24},{24,28},{28,32},{32,36}... | collective-permute-start | bytes 1966088 | tf_op jit(solution)/shard_map/ppermute | solution.py:892
  18.9 28.9 %collective-permute-start.7 = (bf16[160,2048]{1,0:T(8,128)(2,1)}, bf16[160,2048]{1,0:T(8,128)(2,1)}, u32[]{:S(2)}, u32[]{:S(2)}) collective-permute-start(bf16[160,2048]{1,0:T(8,128)(2,1)} %g0.1), channel_id=1, source_target_pairs={{0,2},{1,3},{2,0},{3,1},{4,6},{5,7},{6,4},{7,5},{8,10},{9,11},{10,... | collective-permute-start | bytes 1966088 | tf_op jit(solution)/shard_map/ppermute | solution.py:867
  20.7 27.2 %collective-permute-start.8 = (bf16[160,2048]{1,0:T(8,128)(2,1)}, bf16[160,2048]{1,0:T(8,128)(2,1)}, u32[]{:S(2)}, u32[]{:S(2)}) collective-permute-start(bf16[160,2048]{1,0:T(8,128)(2,1)} %u0), channel_id=1, source_target_pairs={{0,66},{1,67},{2,64},{3,65},{4,70},{5,71},{6,68},{7,69},{8,74},{9,... | collective-permute-start | bytes 1966088 | tf_op jit(solution)/shard_map/ppermute | solution.py:875
  22.4 22.2 %collective-permute-start.10 = (f32[8,256]{1,0:T(8,128)S(1)}, f32[8,256]{1,0:T(8,128)S(1)}, u32[]{:S(2)}, u32[]{:S(2)}) collective-permute-start(f32[8,256]{1,0:T(8,128)S(1)} %pack.1), channel_id=1, source_target_pairs={{0,2},{1,3},{2,0},{3,1},{4,6},{5,7},{6,4},{7,5},{8,10},{9,11},{10,... | collective-permute-start | bytes 24584 | tf_op jit(solution)/shard_map/ppermute | solution.py:867
  24.3 20.4 %collective-permute-start.9 = (f32[8,256]{1,0:T(8,128)S(1)}, f32[8,256]{1,0:T(8,128)S(1)}, u32[]{:S(2)}, u32[]{:S(2)}) collective-permute-start(f32[8,256]{1,0:T(8,128)S(1)} %pack.1), channel_id=1, source_target_pairs={{0,1},{1,0},{2,3},{3,2},{4,5},{5,4},{6,7},{7,6},{8,9},{9,8},{10,11... | collective-permute-start | bytes 24584 | tf_op jit(solution)/shard_map/ppermute | solution.py:863
  44.6 18.2 %collective-permute-start.13 = (bf16[512,640]{1,0:T(8,128)(2,1)}, bf16[512,640]{1,0:T(8,128)(2,1)S(1)}, u32[]{:S(2)}, u32[]{:S(2)}) collective-permute-start(bf16[512,640]{1,0:T(8,128)(2,1)} %d0), channel_id=1, source_target_pairs={{0,66},{1,67},{2,64},{3,65},{4,70},{5,71},{6,68},{7,69},{8,74},{9,... | collective-permute-start | bytes 1966088 | tf_op jit(solution)/shard_map/ppermute | solution.py:875
  46.3 15.9 %collective-permute-start.12 = (bf16[256,640]{1,0:T(8,128)(2,1)}, bf16[256,640]{1,0:T(8,128)(2,1)S(1)}, u32[]{:S(2)}, u32[]{:S(2)}) collective-permute-start(bf16[256,640]{1,0:T(8,128)(2,1)} %o0), channel_id=1, source_target_pairs={{0,2},{1,3},{2,0},{3,1},{4,6},{5,7},{6,4},{7,5},{8,10},{9,11},{10,... | collective-permute-start | bytes 983048 | tf_op jit(solution)/shard_map/ppermute | solution.py:867
  109.6 26.9 %collective-permute-start.22 = (bf16[2,7680,128]{2,1,0:T(8,128)(2,1)}, bf16[2,7680,128]{2,1,0:T(8,128)(2,1)}, u32[]{:S(2)}, u32[]{:S(2)}) collective-permute-start(bf16[2,7680,128]{2,1,0:T(8,128)(2,1)} %get-tuple-element.149), channel_id=1, source_target_pairs={{0,1},{1,0},{2,3},{3,2},{4,5},{5,4},{6,7},{7,6},{8,9},{9,8},{10,11... | collective-permute-start | bytes 11796488 | tf_op jit(solution)/shard_map/ppermute | solution.py:863
  142.7 35.1 %collective-permute-start.24 = (bf16[2,4,352,128]{3,2,1,0:T(8,128)(2,1)S(1)}, bf16[2,4,352,128]{3,2,1,0:T(8,128)(2,1)S(1)}, u32[]{:S(2)}, u32[]{:S(2)}) collective-permute-start(bf16[2,4,352,128]{3,2,1,0:T(8,128)(2,1)S(1)} %get-tuple-element.153), channel_id=1, source_target_pairs={{0,16},{4,20},{8,24},{12,28},{16,32},{20,36},{24,40},{28,44},{32,4... | collective-permute-start | bytes 2162696 | tf_op jit(solution)/shard_map/ppermute | solution.py:883
  142.8 35.1 %collective-permute-start.25 = (bf16[2,4,352,128]{3,2,1,0:T(8,128)(2,1)S(1)}, bf16[2,4,352,128]{3,2,1,0:T(8,128)(2,1)S(1)}, u32[]{:S(2)}, u32[]{:S(2)}) collective-permute-start(bf16[2,4,352,128]{3,2,1,0:T(8,128)(2,1)S(1)} %get-tuple-element.154), channel_id=1, source_target_pairs={{0,48},{4,52},{8,56},{12,60},{16,0},{20,4},{24,8},{28,12},{32,16},... | collective-permute-start | bytes 2162696 | tf_op jit(solution)/shard_map/ppermute | solution.py:883
  146.0 33.1 %collective-permute-start.26 = (bf16[2,4,352,128]{3,2,1,0:T(8,128)(2,1)S(1)}, bf16[2,4,352,128]{3,2,1,0:T(8,128)(2,1)S(1)}, u32[]{:S(2)}, u32[]{:S(2)}) collective-permute-start(bf16[2,4,352,128]{3,2,1,0:T(8,128)(2,1)S(1)} %get-tuple-element.155), channel_id=1, source_target_pairs={{0,32},{4,36},{8,40},{12,44},{16,48},{20,52},{24,56},{28,60},{32,0... | collective-permute-start | bytes 2162696 | tf_op jit(solution)/shard_map/ppermute | solution.py:883
  146.0 33.1 %collective-permute-start.27 = (bf16[2,4,352,128]{3,2,1,0:T(8,128)(2,1)S(1)}, bf16[2,4,352,128]{3,2,1,0:T(8,128)(2,1)S(1)}, u32[]{:S(2)}, u32[]{:S(2)}) collective-permute-start(bf16[2,4,352,128]{3,2,1,0:T(8,128)(2,1)S(1)} %get-tuple-element.157), channel_id=1, source_target_pairs={{0,4},{4,8},{8,12},{12,0},{16,20},{20,24},{24,28},{28,16},{32,36},... | collective-permute-start | bytes 2162696 | tf_op jit(solution)/shard_map/ppermute | solution.py:887
  146.0 48.0 %collective-permute-start.28 = (bf16[2,4,352,128]{3,2,1,0:T(8,128)(2,1)S(1)}, bf16[2,4,352,128]{3,2,1,0:T(8,128)(2,1)S(1)}, u32[]{:S(2)}, u32[]{:S(2)}) collective-permute-start(bf16[2,4,352,128]{3,2,1,0:T(8,128)(2,1)S(1)} %get-tuple-element.158), channel_id=1, source_target_pairs={{0,12},{4,0},{8,4},{12,8},{16,28},{20,16},{24,20},{28,24},{32,44},... | collective-permute-start | bytes 2162696 | tf_op jit(solution)/shard_map/ppermute | solution.py:887
  177.8 19.1 %collective-permute-start.29 = (bf16[2,4,352,128]{3,2,1,0:T(8,128)(2,1)S(1)}, bf16[2,4,352,128]{3,2,1,0:T(8,128)(2,1)S(1)}, u32[]{:S(2)}, u32[]{:S(2)}) collective-permute-start(bf16[2,4,352,128]{3,2,1,0:T(8,128)(2,1)S(1)} %get-tuple-element.159), channel_id=1, source_target_pairs={{0,8},{4,12},{8,0},{12,4},{16,24},{20,28},{24,16},{28,20},{32,40},... | collective-permute-start | bytes 2162696 | tf_op jit(solution)/shard_map/ppermute | solution.py:887
  177.8 47.8 %collective-permute-start.39 = (bf16[512,640]{1,0:T(8,128)(2,1)S(1)}, bf16[512,640]{1,0:T(8,128)(2,1)S(1)}, u32[]{:S(2)}, u32[]{:S(2)}) collective-permute-start(bf16[512,640]{1,0:T(8,128)(2,1)S(1)} %copy-done.16), channel_id=1, source_target_pairs={{4,0},{8,4},{12,8},{16,12},{20,16},{24,20},{28,24},{32,28},{36,32}... | collective-permute-start | bytes 1966088 | tf_op jit(solution)/shard_map/ppermute | solution.py:892
  198.2 10.6 %collective-permute-start.30 = (bf16[2,352,128]{2,1,0:T(8,128)(2,1)S(1)}, bf16[2,352,128]{2,1,0:T(8,128)(2,1)S(1)}, u32[]{:S(2)}, u32[]{:S(2)}) collective-permute-start(bf16[2,352,128]{2,1,0:T(8,128)(2,1)S(1)} %get-tuple-element.161), channel_id=1, source_target_pairs={{0,4},{4,8},{8,12},{12,0},{16,20},{20,24},{24,28},{28,16},{32,36},... | collective-permute-start | bytes 540680 | tf_op jit(solution)/shard_map/ppermute | solution.py:887
  198.3 10.6 %collective-permute-start.31 = (bf16[2,352,128]{2,1,0:T(8,128)(2,1)S(1)}, bf16[2,352,128]{2,1,0:T(8,128)(2,1)S(1)}, u32[]{:S(2)}, u32[]{:S(2)}) collective-permute-start(bf16[2,352,128]{2,1,0:T(8,128)(2,1)S(1)} %get-tuple-element.162), channel_id=1, source_target_pairs={{0,12},{4,0},{8,4},{12,8},{16,28},{20,16},{24,20},{28,24},{32,44},... | collective-permute-start | bytes 540680 | tf_op jit(solution)/shard_map/ppermute | solution.py:887
  241.3 11.6 %collective-permute-start.47 = (bf16[4,352,128]{2,1,0:T(8,128)(2,1)S(1)}, bf16[4,352,128]{2,1,0:T(8,128)(2,1)S(1)}, u32[]{:S(2)}, u32[]{:S(2)}) collective-permute-start(bf16[4,352,128]{2,1,0:T(8,128)(2,1)S(1)} %pad_maximum_fusion.a0), channel_id=1, source_target_pairs={{0,32},{4,36},{8,40},{12,44},{16,48},{20,52},{24,56},{28,60},{32,0... | collective-permute-start | bytes 1081352 | tf_op jit(solution)/shard_map/ppermute | solution.py:883
  242.6 11.6 %collective-permute-start.46 = (bf16[4,352,128]{2,1,0:T(8,128)(2,1)S(1)}, bf16[4,352,128]{2,1,0:T(8,128)(2,1)S(1)}, u32[]{:S(2)}, u32[]{:S(2)}) collective-permute-start(bf16[4,352,128]{2,1,0:T(8,128)(2,1)S(1)} %pad_maximum_fusion.a0), channel_id=1, source_target_pairs={{0,16},{4,20},{8,24},{12,28},{16,32},{20,36},{24,40},{28,44},{32,4... | collective-permute-start | bytes 1081352 | tf_op jit(solution)/shard_map/ppermute | solution.py:883
  243.9 11.1 %collective-permute-start.51 = (bf16[4,352,128]{2,1,0:T(8,128)(2,1)S(1)}, bf16[4,352,128]{2,1,0:T(8,128)(2,1)S(1)}, u32[]{:S(2)}, u32[]{:S(2)}) collective-permute-start(bf16[4,352,128]{2,1,0:T(8,128)(2,1)S(1)} %pad_maximum_fusion.1.b0), channel_id=1, source_target_pairs={{0,12},{4,0},{8,4},{12,8},{16,28},{20,16},{24,20},{28,24},{32,44},... | collective-permute-start | bytes 1081352 | tf_op jit(solution)/shard_map/ppermute | solution.py:887
  248.8 10.3 %collective-permute-start.49 = (bf16[4,352,128]{2,1,0:T(8,128)(2,1)S(1)}, bf16[4,352,128]{2,1,0:T(8,128)(2,1)S(1)}, u32[]{:S(2)}, u32[]{:S(2)}) collective-permute-start(bf16[4,352,128]{2,1,0:T(8,128)(2,1)S(1)} %pad_maximum_fusion.1.b0), channel_id=1, source_target_pairs={{0,4},{4,8},{8,12},{12,0},{16,20},{20,24},{24,28},{28,16},{32,36},... | collective-permute-start | bytes 1081352 | tf_op jit(solution)/shard_map/ppermute | solution.py:887
  (68 other events, 624.8 us)

commit v4 on v1

--- a/solution.py
+++ b/solution.py
@@ -63,7 +63,9 @@
         at = pl.ds(pl.multiple_of((place ^ r) * rows, rows), rows)
         copies.append(
             pltpu.make_async_copy(
-                pieces[r].at[pl.ds(0, rows), :], into.at[at, :], semaphores.at[first + r]
+                pieces[r].at[pl.ds(0, rows), :],
+                into.at[at, :],
+                semaphores.at[first + r],
             )
         )
     for copy in copies:
@@ -103,7 +105,7 @@
     tile = []
     for copy in copies:
         copy.wait()
-    for i, ref in enumerate(held):
+    for ref in held:
         n = ref.shape[0]
         row = ref[...].astype(f32).reshape(1, n)
         tile.append(jnp.concatenate([row, jnp.zeros((1, 512 - n), f32)], axis=1))
@@ -217,7 +219,7 @@
             pltpu.VMEM((640, 512), bf16),
             pltpu.SemaphoreType.DMA((8,)),
         ],
-        compiler_params=params(20),
+        compiler_params=params(14),
         cost_estimate=cost(1_350_000_000, 9_000_000),
     )(place, halo, own, gains, head_gains, *q_shares, *kv_shares, cosine, sine)
 
@@ -265,7 +267,7 @@
             pl.BlockSpec((4, 256, 1), lambda i: (0, i, 0)),
         ],
         out_shape=[spec(512, 1024, bf16), spec(4, 512, 1, f32)],
-        compiler_params=params(20),
+        compiler_params=params(10),
         cost_estimate=cost(1_700_000_000, 4_000_000, 2_000_000),
     )(q, k, v, offsets)
 
@@ -426,7 +428,7 @@
             pltpu.VMEM((4, 7680, 128), bf16),
             pltpu.SemaphoreType.DMA((20,)),
         ],
-        compiler_params=params(46),
+        compiler_params=params(44),
         cost_estimate=cost(13_400_000_000, 23_000_000, 1_000_000),
     )(place, x, attended, upstream, gains, *shares)
 
@@ -541,7 +543,7 @@
             pltpu.VMEM((640, 512), bf16),
             pltpu.SemaphoreType.DMA((4,)),
         ],
-        compiler_params=params(30),
+        compiler_params=params(16),
         cost_estimate=cost(4_300_000_000, 10_000_000, 2_000_000),
     )(
         q, k, v, offsets, level, back_attended, q_proj, k_proj, head_gains, cosine, sine, place, *shares
@@ -641,7 +643,7 @@
             pltpu.VMEM((4, 3584, 128), bf16),
             pltpu.SemaphoreType.DMA((12,)),
         ],
-        compiler_params=params(40),
+        compiler_params=params(24),
         cost_estimate=cost(3_400_000_000, 14_000_000),
     )(place, normed, back_q, back_kv, attended, back_attn, halo, own, gain_mid, gain_head, *shares)
 
@@ -739,7 +741,7 @@
             pltpu.VMEM((3584, 128), bf16),
             pltpu.SemaphoreType.DMA((71,)),
         ],
-        compiler_params=params(20),
+        compiler_params=params(14),
         cost_estimate=cost(4_000_000, 11_000_000),
     )(spot, *pieces)
 
@@ -774,7 +776,7 @@
         in_specs=[pl.BlockSpec(memory_space=pltpu.SMEM)] + [whole()] * 4,
         out_specs=[whole()] * 8,
         out_shape=[spec(2, 4, 352, 128, bf16)] * 8,
-        compiler_params=params(30),
+        compiler_params=params(24),
         cost_estimate=cost(3_000_000, 17_000_000),
     )(spot, *ins)
 
@@ -796,7 +798,7 @@
         in_specs=[pl.BlockSpec(memory_space=pltpu.SMEM)] + [whole()] * 8,
         out_specs=[whole()] * 8,
         out_shape=[spec(2, 352, 128, bf16)] * 8,
-        compiler_params=params(20),
+        compiler_params=params(12),
         cost_estimate=cost(1_000_000, 7_200_000),
     )(spot, *parts)
 
@@ -868,6 +870,10 @@
 
 def swap_near(value):
     return lax.ppermute(value, "fsdp", [(0, 2), (1, 3), (2, 0), (3, 1)])
+
+
+def swap_across(value):
+    return lax.ppermute(value, "fsdp", [(0, 3), (1, 2), (2, 1), (3, 0)])
 
 
 def swap_far(value):
@@ -952,28 +958,28 @@
         value_weight,
     )
     kv_partner = swap_far(kv)
-    q_sibling = swap_core(query_weight)
-    kv_sibling = swap_core(kv)
     halo = shifted(own, 1)
-    q_diagonal = swap_core(q_partner)
-    kv_diagonal = swap_core(kv_partner)
-    (q_diagonal, kv_diagonal, halo), (wg_partner, wu_partner), (wo, wd) = together(
-        (q_diagonal, kv_diagonal, halo), (wg_partner, wu_partner), (output_weight, down_weight)
+    q_shares = (query_weight, swap_core(query_weight), q_partner, swap_core(q_partner))
+    kv_shares = (kv, swap_core(kv), kv_partner, swap_core(kv_partner))
+    wg_diagonal, wu_diagonal = swap_core(wg_partner), swap_core(wu_partner)
+    q_shares, kv_shares, halo, wg_diagonal, wu_diagonal = together(
+        q_shares, kv_shares, halo, wg_diagonal, wu_diagonal
+    )
+    wo, wd, wg_partner, wu_partner = together(
+        output_weight, down_weight, wg_partner, wu_partner
     )
     wo_partner, wd_partner = swap_near(wo), swap_far(wd)
-    q_shares = (query_weight, q_sibling, q_partner, q_diagonal)
-    kv_shares = (kv, kv_sibling, kv_partner, kv_diagonal)
-    tails = [share[160:168] for share in kv_shares]
-    tails = [
+    tiles = [share[160:168] for share in kv_shares]
+    tiles = [
         jnp.where(
             j // 2 == z_lo,
-            jnp.where(j % 2 == core, tails[0], tails[1]),
-            jnp.where(j % 2 == core, tails[2], tails[3]),
+            jnp.where(j % 2 == core, tiles[0], tiles[1]),
+            jnp.where(j % 2 == core, tiles[2], tiles[3]),
         )
         for j in range(4)
     ]
-    gains = jnp.concatenate([tail[:, :160] for tail in tails], axis=1).astype(f32)
-    head_gains = jnp.concatenate([tail[:, :64] for tail in tails], axis=1).astype(f32)
+    gains = jnp.concatenate([t[:, :160] for t in tiles], axis=1).astype(f32)
+    head_gains = jnp.concatenate([t[:, :64] for t in tiles], axis=1).astype(f32)
 
     cosine, sine = rope_tables(offsets)
     column = offsets[:, None]
@@ -981,14 +987,13 @@
         place, halo, own, gains, head_gains, q_shares, kv_shares, cosine, sine
     )
     attended, level = attend(q, k, v, column)
-    attended, (wo, wg, wu, wd) = together(attended, (wo, gate_weight, up_weight, wd))
-    siblings = [swap_core(w) for w in (wo, wg, wu, wd)]
-    attended, wo_partner, wg_partner = together(attended, wo_partner, wg_partner)
-    attended, wu_partner, wd_partner = together(attended, wu_partner, wd_partner)
-    wo_shares = [wo, siblings[0], wo_partner, swap_core(wo_partner)]
-    wg_shares = [wg, siblings[1], wg_partner, swap_core(wg_partner)]
-    wu_shares = [wu, siblings[2], wu_partner, swap_core(wu_partner)]
-    wd_shares = [wd, siblings[3], wd_partner, swap_core(wd_partner)]
+    attended, wo, wg, wu, wd = together(attended, wo, gate_weight, up_weight, wd)
+    wg_shares = [wg, swap_core(wg), wg_partner, wg_diagonal]
+    wu_shares = [wu, swap_core(wu), wu_partner, wu_diagonal]
+    attended, wo_partner = together(attended, wo_partner)
+    wo_shares = [wo, swap_core(wo), wo_partner, swap_core(wo_partner)]
+    attended, wd_partner = together(attended, wd_partner)
+    wd_shares = [wd, swap_core(wd), wd_partner, swap_core(wd_partner)]
     layer_out, back_middle, back_attn, back_attended, gain_mid, kept, sent = middle_part(
         place, own, attended, upstream, gains, wo_shares + wg_shares + wu_shares + wd_shares
     )
@@ -1027,6 +1032,7 @@
     mine, other, back_halo = together(mine, other, back_halo)
     returned = shifted(back_halo, -1)
     a, b = fourth_sums([mine, swap_near(other), swap_far(other), swap_hi(mine)])
+    a, b, returned = together(a, b, returned)
     a = jnp.stack([a] + [move_y(a, d) for d in (1, 2, 3)])
     b = jnp.stack([b] + [move_x(b, d) for d in (1, 2, 3)])
     a, b = together(a, b)

time: 279 us -> 283 us (1.014)
  the two profiles are of different devices: /device:TPU:28 before, /device:TPU:0 now
where the time goes in v4:
time: 283 us; the launch traced here: 280 us
  waiting for transfers between devices  115 us (41%)
  Pallas kernels  82.6 us (29%)
  starting transfers between devices  58.8 us (21%)
  local copies, waits for them, and re-layouts  18.3 us (6%)
  other arithmetic  3.5 us (1%)
    ppermute x12, waiting for transfers between devices, move_x(): return lax.ppermute(value, 'seq', along_xy(d, 0))  49.4 us
    pallas_call x1, Pallas kernels, middle_part(): pl.pallas_call(middle_kernel, name='middle_part', in_specs=[pl.BlockSpec(...  39 us
    ppermute x12, waiting for transfers between devices, move_y(): return lax.ppermute(value, 'seq', along_xy(0, d))  27.9 us
    ppermute x4, waiting for transfers between devices, swap_far(): return lax.ppermute(value, ('seq', 'fsdp'), along_z(lambda z: 3 - z))  21 us
    ppermute x12, starting transfers between devices, move_x(): return lax.ppermute(value, 'seq', along_xy(d, 0))  20.1 us
    ppermute x12, starting transfers between devices, move_y(): return lax.ppermute(value, 'seq', along_xy(0, d))  16.6 us
    unnamed x66, local copies, waits for them, and re-layouts  15.8 us
    pallas_call x1, Pallas kernels, attend_back(): pl.pallas_call(attend_back_kernel, name='attend_back', grid=(2,), in_spec...  10.2 us
  transfers between devices with their start and end apart: 49, of which 24 were waited for; matrix products, arithmetic and copies ran while one was open for 2% of the time, Pallas kernels for 11%

profile of v4, /device:TPU:0, one launch (start us, length us, event | category | flops | bytes accessed | tf_op | source)
XLA Modules:
  0.0 280.4 jit_solution(10142022189375741930)
XLA Ops:
  12.4 11.9 %collective-permute-done.4.kv2 = bf16[176,512]{1,0:T(8,128)(2,1)S(1)} collective-permute-done((bf16[176,512]{1,0:T(8,128)(2,1)S(1)}, bf16[176,512]{1,0:T(8,128)(2,1)S(1)}, u32[]{:S(2)}, u32[]{:S(2)}) %collective-permute-start.4) | collective-permute-done | bytes 180256 | tf_op jit(solution)/shard_map/ppermute | solution.py:880
  24.2 3.5 %collective-permute-start.6 = (bf16[512,640]{1,0:T(8,128)(2,1)}, bf16[512,640]{1,0:T(8,128)(2,1)S(1)}, u32[]{:S(2)}, u32[]{:S(2)}) collective-permute-start(bf16[512,640]{1,0:T(8,128)(2,1)} %bitcast.32), channel_id=1, source_target_pairs={{0,4},{4,8},{8,12},{12,16},{16,20},{20,24},{24,28},{28,32},{32,36}... | collective-permute-start | bytes 1966088 | tf_op jit(solution)/shard_map/ppermute | solution.py:897
  42.1 6.0 %project.1 = (bf16[1024,640]{1,0:T(8,128)(2,1)S(1)}, bf16[512,1024]{1,0:T(8,128)(2,1)S(1)}, bf16[1024,256]{1,0:T(8,128)(2,1)S(1)}, bf16[1024,256]{1,0:T(8,128)(2...) custom-call(s32[1]{0:T(128)} %bitcast.place, bf16[512,640]{1,0:T(8,128)(2,1)S(1)} %collective-permute-done.6.halo, ...), custom_call_target="tpu_custom_call" | custom-call | flops 1350000000 | bytes 9000000 | tf_op jit(solution)/shard_map/project/pallas_call | solution.py:188
  48.1 3.9 %attend.1 = (bf16[512,1024]{1,0:T(8,128)(2,1)S(1)}, f32[4,512,1]{2,1,0:T(8,128)S(1)}) custom-call(bf16[512,1024]{1,0:T(8,128)(2,1)S(1)} %get-tuple-element.106.q, bf16[1024,256]{1,0:T(8,128)(2,1)S(1)} %get-tuple-element.107.k, bf16[1024,256]{1,0:T(8,128)(2,1)S(1)} %get-tuple-element.108.v, s32[512,1]{1,0:T(8,128)S(1)} %copy.31.offsets), custom_call_target="tpu_custom_call" | custom-call | flops 1700000000 | bytes 4000000 | tf_op jit(solution)/shard_map/attend/pallas_call | solution.py:255
  54.2 6.2 %collective-permute-done.12.d2 = bf16[512,640]{1,0:T(8,128)(2,1)S(1)} collective-permute-done((bf16[512,640]{1,0:T(8,128)(2,1)}, bf16[512,640]{1,0:T(8,128)(2,1)S(1)}, u32[]{:S(2)}, u32[]{:S(2)}) %collective-permute-start.12) | collective-permute-done | bytes 655392 | tf_op jit(solution)/shard_map/ppermute | solution.py:880
  62.2 4.1 %collective-permute-done.13.o1 = bf16[256,640]{1,0:T(8,128)(2,1)S(1)} collective-permute-done((bf16[256,640]{1,0:T(8,128)(2,1)S(1)}, bf16[256,640]{1,0:T(8,128)(2,1)S(1)}, u32[]{:S(2)}, u32[]{:S(2)}) %collective-permute-start.13) | collective-permute-done | bytes 327712 | tf_op jit(solution)/shard_map/ppermute | solution.py:868
  67.1 39.0 %middle_part.1 = (bf16[512,640]{1,0:T(8,128)(2,1)}, f32[512,640]{1,0:T(8,128)}, bf16[512,640]{1,0:T(8,128)(2,1)S(1)}, bf16[512,1024]{1,0:T(8,128)(2,1)}, f32[8,6...) custom-call(s32[1]{0:T(128)} %bitcast.place, bf16[512,640]{1,0:T(8,128)(2,1)S(1)} %bitcast.34, ...), custom_call_target="tpu_custom_call" | custom-call | flops 13400000512 | bytes 23000000 | tf_op jit(solution)/shard_map/middle_part/pallas_call | solution.py:398
  108.8 10.2 %attend_back.1 = (bf16[512,1024]{1,0:T(8,128)(2,1)S(1)}, bf16[1024,512]{1,0:T(8,128)(2,1)S(1)}, f32[8,256]{1,0:T(8,128)S(1)}, bf16[512,640]{1,0:T(8,128)(2,1)S(1)}) custom-call(bf16[512,1024]{1,0:T(8,128)(2,1)S(1)} %get-tuple-element.106.q, bf16[1024,256]{1,0:T(8,128)(2,1)S(1)} %get-tuple-element.107.k, bf16[1024,256]{1,0:T(8,128)(2,1)S(1)} %get-tuple-element.108.v, ...), custom_call_target="tpu_custom_call" | custom-call | flops 4300000256 | bytes 10000000 | tf_op jit(solution)/shard_map/attend_back/pallas_call | solution.py:509
  120.8 7.3 %weights_part.1 = (f32[512,640]{1,0:T(8,128)S(1)}, bf16[2,3584,128]{2,1,0:T(8,128)(2,1)S(1)}, bf16[2,3584,128]{2,1,0:T(8,128)(2,1)}) custom-call(s32[1]{0:T(128)} %bitcast.place, bf16[1024,640]{1,0:T(8,128)(2,1)S(1)} %get-tuple-element.126.normed, bf16[512,1024]{1,0:T(8,128)(2,1)S(1)} %get-tuple-element.131.back_q, ...), custom_call_target="tpu_custom_call" | custom-call | flops 3400000000 | bytes 14000000 | tf_op jit(solution)/shard_map/weights_part/pallas_call | solution.py:628
  128.6 3.7 %collective-permute-done.20 = bf16[2,3584,128]{2,1,0:T(8,128)(2,1)} collective-permute-done((bf16[2,3584,128]{2,1,0:T(8,128)(2,1)}, bf16[2,3584,128]{2,1,0:T(8,128)(2,1)}, u32[]{:S(2)}, u32[]{:S(2)}) %collective-permute-start.20) | collective-permute-done | bytes 1835040 | tf_op jit(solution)/shard_map/ppermute | solution.py:868
  134.4 4.0 %first_sums.1 = (bf16[2,4,352,128]{3,2,1,0:T(8,128)(2,1)S(1)}, bf16[2,4,352,128]{3,2,1,0:T(8,128)(2,1)S(1)}, bf16[2,4,352,128]{3,2,1,0:T(8,128)(2,1)S(1)}, bf16[...) custom-call(s32[2]{0:T(128)S(1)} %pad_add_fusion.spot, ...), custom_call_target="tpu_custom_call" | custom-call | flops 3000000 | bytes 17000000 | tf_op jit(solution)/shard_map/first_sums/pallas_call | solution.py:773
  138.5 3.2 %collective-permute-start.22 = (bf16[2,4,352,128]{3,2,1,0:T(8,128)(2,1)S(1)}, bf16[2,4,352,128]{3,2,1,0:T(8,128)(2,1)S(1)}, u32[]{:S(2)}, u32[]{:S(2)}) collective-permute-start(bf16[2,4,352,128]{3,2,1,0:T(8,128)(2,1)S(1)} %get-tuple-element.143), channel_id=1, source_target_pairs={{0,48},{4,52},{8,56},{12,60},{16,0},{20,4},{24,8},{28,12},{32,16},... | collective-permute-start | bytes 2162696 | tf_op jit(solution)/shard_map/ppermute | solution.py:888
  141.8 3.4 %collective-permute-start.25 = (bf16[2,4,352,128]{3,2,1,0:T(8,128)(2,1)S(1)}, bf16[2,4,352,128]{3,2,1,0:T(8,128)(2,1)S(1)}, u32[]{:S(2)}, u32[]{:S(2)}) collective-permute-start(bf16[2,4,352,128]{3,2,1,0:T(8,128)(2,1)S(1)} %get-tuple-element.147), channel_id=1, source_target_pairs={{0,12},{4,0},{8,4},{12,8},{16,28},{20,16},{24,20},{28,24},{32,44},... | collective-permute-start | bytes 2162696 | tf_op jit(solution)/shard_map/ppermute | solution.py:892
  145.2 28.4 %collective-permute-done.21.refs_1_ = bf16[2,4,352,128]{3,2,1,0:T(8,128)(2,1)S(1)} collective-permute-done((bf16[2,4,352,128]{3,2,1,0:T(8,128)(2,1)S(1)}, bf16[2,4,352,128]{3,2,1,0:T(8,128)(2,1)S(1)}, u32[]{:S(2)}, u32[]{:S(2)}) %collective-permute-start.21) | collective-permute-done | bytes 720928 | tf_op jit(solution)/shard_map/ppermute | solution.py:888
  175.7 17.0 %collective-permute-done.26.refs_7_ = bf16[2,4,352,128]{3,2,1,0:T(8,128)(2,1)S(1)} collective-permute-done((bf16[2,4,352,128]{3,2,1,0:T(8,128)(2,1)S(1)}, bf16[2,4,352,128]{3,2,1,0:T(8,128)(2,1)S(1)}, u32[]{:S(2)}, u32[]{:S(2)}) %collective-permute-start.26) | collective-permute-done | bytes 720928 | tf_op jit(solution)/shard_map/ppermute | solution.py:892
  197.3 3.2 %collective-permute-start.31 = (bf16[2,352,128]{2,1,0:T(8,128)(2,1)S(1)}, bf16[2,352,128]{2,1,0:T(8,128)(2,1)S(1)}, u32[]{:S(2)}, u32[]{:S(2)}) collective-permute-start(bf16[2,352,128]{2,1,0:T(8,128)(2,1)S(1)} %get-tuple-element.155), channel_id=1, source_target_pairs={{0,48},{4,52},{8,56},{12,60},{16,0},{20,4},{24,8},{28,12},{32,16},... | collective-permute-start | bytes 540680 | tf_op jit(solution)/shard_map/ppermute | solution.py:888
  200.5 4.1 %collective-permute-done.27.refs_1_ = bf16[2,352,128]{2,1,0:T(8,128)(2,1)S(1)} collective-permute-done((bf16[2,352,128]{2,1,0:T(8,128)(2,1)S(1)}, bf16[2,352,128]{2,1,0:T(8,128)(2,1)S(1)}, u32[]{:S(2)}, u32[]{:S(2)}) %collective-permute-start.27) | collective-permute-done | bytes 180256 | tf_op jit(solution)/shard_map/ppermute | solution.py:892
  205.9 5.7 %collective-permute-done.32.refs_7_ = bf16[2,352,128]{2,1,0:T(8,128)(2,1)S(1)} collective-permute-done((bf16[2,352,128]{2,1,0:T(8,128)(2,1)S(1)}, bf16[2,352,128]{2,1,0:T(8,128)(2,1)S(1)}, u32[]{:S(2)}, u32[]{:S(2)}) %collective-permute-start.32) | collective-permute-done | bytes 180256 | tf_op jit(solution)/shard_map/ppermute | solution.py:888
  213.1 4.2 %collective-permute-start.35 = (bf16[2,352,128]{2,1,0:T(8,128)(2,1)S(1)}, bf16[2,352,128]{2,1,0:T(8,128)(2,1)S(1)}, u32[]{:S(2)}, u32[]{:S(2)}) collective-permute-start(bf16[2,352,128]{2,1,0:T(8,128)(2,1)S(1)} %get-tuple-element.160.p0), channel_id=1, source_target_pairs={{0,64},{4,68},{8,72},{12,76},{16,80},{20,84},{24,88},{28,92},{32,9... | collective-permute-start | bytes 540680 | tf_op jit(solution)/shard_map/ppermute | solution.py:884
  229.3 10.2 %collective-permute-start.42 = (bf16[352,128]{1,0:T(8,128)(2,1)S(1)}, bf16[352,128]{1,0:T(8,128)(2,1)S(1)}, u32[]{:S(2)}, u32[]{:S(2)}) collective-permute-start(bf16[352,128]{1,0:T(8,128)(2,1)S(1)} %get-tuple-element.168), channel_id=1, source_target_pairs={{0,48},{4,52},{8,56},{12,60},{16,0},{20,4},{24,8},{28,12},{32,16},... | collective-permute-start | bytes 270344 | tf_op jit(solution)/shard_map/ppermute | solution.py:888
  253.8 4.4 %collective-permute-done.45.a3 = bf16[4,352,128]{2,1,0:T(8,128)(2,1)S(1)} collective-permute-done((bf16[4,352,128]{2,1,0:T(8,128)(2,1)S(1)}, bf16[4,352,128]{2,1,0:T(8,128)(2,1)S(1)}, u32[]{:S(2)}, u32[]{:S(2)}) %collective-permute-start.45) | collective-permute-done | bytes 360480 | tf_op jit(solution)/shard_map/ppermute | solution.py:888
  262.2 3.4 %collective-permute-done.43.a1 = bf16[4,352,128]{2,1,0:T(8,128)(2,1)S(1)} collective-permute-done((bf16[4,352,128]{2,1,0:T(8,128)(2,1)S(1)}, bf16[4,352,128]{2,1,0:T(8,128)(2,1)S(1)}, u32[]{:S(2)}, u32[]{:S(2)}) %collective-permute-start.43) | collective-permute-done | bytes 360480 | tf_op jit(solution)/shard_map/ppermute | solution.py:888
  266.7 3.7 %collective-permute-done.46.b1 = bf16[4,352,128]{2,1,0:T(8,128)(2,1)S(1)} collective-permute-done((bf16[4,352,128]{2,1,0:T(8,128)(2,1)S(1)}, bf16[4,352,128]{2,1,0:T(8,128)(2,1)S(1)}, u32[]{:S(2)}, u32[]{:S(2)}) %collective-permute-start.46) | collective-permute-done | bytes 360480 | tf_op jit(solution)/shard_map/ppermute | solution.py:892
  270.4 8.7 %unpack.1 = (f32[160,1024]{1,0:T(8,128)}, f32[160,256]{1,0:T(8,128)}, f32[160,256]{1,0:T(8,128)}, f32[256,640]{1,0:T(8,128)}, f32[160,2048]{1,0:T(8,128)}, /*ind...) custom-call(s32[2]{0:T(128)S(1)} %pad_add_fusion.spot, bf16[4,352,128]{2,1,0:T(8,128)(2,1)S(1)} %pad_maximum_fusion.a0, ...), custom_call_target="tpu_custom_call" | custom-call | flops 4000000 | bytes 11000000 | tf_op jit(solution)/shard_map/unpack/pallas_call | solution.py:732
  (177 shorter events, 78.9 us)
Async XLA Ops:
  0.7 27.1 %collective-permute-start.7 = (bf16[160,2048]{1,0:T(8,128)(2,1)}, bf16[160,2048]{1,0:T(8,128)(2,1)S(1)}, u32[]{:S(2)}, u32[]{:S(2)}) collective-permute-start(bf16[160,2048]{1,0:T(8,128)(2,1)} %g0.2), channel_id=1, source_target_pairs={{0,2},{1,3},{2,0},{3,1},{4,6},{5,7},{6,4},{7,5},{8,10},{9,11},{10,... | collective-permute-start | bytes 1966088 | tf_op jit(solution)/shard_map/ppermute | solution.py:872
  2.7 25.1 %collective-permute-start.9 = (bf16[160,2048]{1,0:T(8,128)(2,1)}, bf16[160,2048]{1,0:T(8,128)(2,1)S(1)}, u32[]{:S(2)}, u32[]{:S(2)}) collective-permute-start(bf16[160,2048]{1,0:T(8,128)(2,1)} %u0), channel_id=1, source_target_pairs={{0,66},{1,67},{2,64},{3,65},{4,70},{5,71},{6,68},{7,69},{8,74},{9,... | collective-permute-start | bytes 1966088 | tf_op jit(solution)/shard_map/ppermute | solution.py:880
  11.1 13.1 %collective-permute-start.4 = (bf16[176,512]{1,0:T(8,128)(2,1)S(1)}, bf16[176,512]{1,0:T(8,128)(2,1)S(1)}, u32[]{:S(2)}, u32[]{:S(2)}) collective-permute-start(bf16[176,512]{1,0:T(8,128)(2,1)S(1)} %pack.1.kv0), channel_id=1, source_target_pairs={{0,66},{1,67},{2,64},{3,65},{4,70},{5,71},{6,68},{7,69},{8,74},{9,... | collective-permute-start | bytes 540680 | tf_op jit(solution)/shard_map/ppermute | solution.py:880
  11.9 19.1 %collective-permute-start.3 = (bf16[176,512]{1,0:T(8,128)(2,1)S(1)}, bf16[176,512]{1,0:T(8,128)(2,1)S(1)}, u32[]{:S(2)}, u32[]{:S(2)}) collective-permute-start(bf16[176,512]{1,0:T(8,128)(2,1)S(1)} %pack.1.kv0), channel_id=1, source_target_pairs={{0,1},{1,0},{2,3},{3,2},{4,5},{5,4},{6,7},{7,6},{8,9},{9,8},{10,11... | collective-permute-start | bytes 540680 | tf_op jit(solution)/shard_map/ppermute | solution.py:868
  11.9 20.0 %collective-permute-start.1 = (bf16[160,1024]{1,0:T(8,128)(2,1)}, bf16[160,1024]{1,0:T(8,128)(2,1)}, u32[]{:S(2)}, u32[]{:S(2)}) collective-permute-start(bf16[160,1024]{1,0:T(8,128)(2,1)} %q0.1), channel_id=1, source_target_pairs={{0,2},{1,3},{2,0},{3,1},{4,6},{5,7},{6,4},{7,5},{8,10},{9,11},{10,... | collective-permute-start | bytes 983048 | tf_op jit(solution)/shard_map/ppermute | solution.py:872
  24.2 16.6 %collective-permute-start.6 = (bf16[512,640]{1,0:T(8,128)(2,1)}, bf16[512,640]{1,0:T(8,128)(2,1)S(1)}, u32[]{:S(2)}, u32[]{:S(2)}) collective-permute-start(bf16[512,640]{1,0:T(8,128)(2,1)} %bitcast.32), channel_id=1, source_target_pairs={{0,4},{4,8},{8,12},{12,16},{16,20},{20,24},{24,28},{28,32},{32,36}... | collective-permute-start | bytes 1966088 | tf_op jit(solution)/shard_map/ppermute | solution.py:897
  27.7 13.1 %collective-permute-start.8 = (bf16[160,2048]{1,0:T(8,128)(2,1)S(1)}, bf16[160,2048]{1,0:T(8,128)(2,1)}, u32[]{:S(2)}, u32[]{:S(2)}) collective-permute-start(bf16[160,2048]{1,0:T(8,128)(2,1)S(1)} %collective-permute-done.7.g2), channel_id=1, source_target_pairs={{0,1},{1,0},{2,3},{3,2},{4,5},{5,4},{6,7},{7,6},{8,9},{9,8},{10,11... | collective-permute-start | bytes 1966088 | tf_op jit(solution)/shard_map/ppermute | solution.py:868
  35.0 19.2 %collective-permute-start.11 = (bf16[256,640]{1,0:T(8,128)(2,1)}, bf16[256,640]{1,0:T(8,128)(2,1)S(1)}, u32[]{:S(2)}, u32[]{:S(2)}) collective-permute-start(bf16[256,640]{1,0:T(8,128)(2,1)} %o0), channel_id=1, source_target_pairs={{0,2},{1,3},{2,0},{3,1},{4,6},{5,7},{6,4},{7,5},{8,10},{9,11},{10,... | collective-permute-start | bytes 983048 | tf_op jit(solution)/shard_map/ppermute | solution.py:872
  35.7 24.7 %collective-permute-start.12 = (bf16[512,640]{1,0:T(8,128)(2,1)}, bf16[512,640]{1,0:T(8,128)(2,1)S(1)}, u32[]{:S(2)}, u32[]{:S(2)}) collective-permute-start(bf16[512,640]{1,0:T(8,128)(2,1)} %d0), channel_id=1, source_target_pairs={{0,66},{1,67},{2,64},{3,65},{4,70},{5,71},{6,68},{7,69},{8,74},{9,... | collective-permute-start | bytes 1966088 | tf_op jit(solution)/shard_map/ppermute | solution.py:880
  106.1 26.2 %collective-permute-start.19 = (bf16[2,7680,128]{2,1,0:T(8,128)(2,1)}, bf16[2,7680,128]{2,1,0:T(8,128)(2,1)}, u32[]{:S(2)}, u32[]{:S(2)}) collective-permute-start(bf16[2,7680,128]{2,1,0:T(8,128)(2,1)} %get-tuple-element.138), channel_id=1, source_target_pairs={{0,1},{1,0},{2,3},{3,2},{4,5},{5,4},{6,7},{7,6},{8,9},{9,8},{10,11... | collective-permute-start | bytes 11796488 | tf_op jit(solution)/shard_map/ppermute | solution.py:868
  138.4 35.1 %collective-permute-start.21 = (bf16[2,4,352,128]{3,2,1,0:T(8,128)(2,1)S(1)}, bf16[2,4,352,128]{3,2,1,0:T(8,128)(2,1)S(1)}, u32[]{:S(2)}, u32[]{:S(2)}) collective-permute-start(bf16[2,4,352,128]{3,2,1,0:T(8,128)(2,1)S(1)} %get-tuple-element.142), channel_id=1, source_target_pairs={{0,16},{4,20},{8,24},{12,28},{16,32},{20,36},{24,40},{28,44},{32,4... | collective-permute-start | bytes 2162696 | tf_op jit(solution)/shard_map/ppermute | solution.py:888
  138.5 35.1 %collective-permute-start.22 = (bf16[2,4,352,128]{3,2,1,0:T(8,128)(2,1)S(1)}, bf16[2,4,352,128]{3,2,1,0:T(8,128)(2,1)S(1)}, u32[]{:S(2)}, u32[]{:S(2)}) collective-permute-start(bf16[2,4,352,128]{3,2,1,0:T(8,128)(2,1)S(1)} %get-tuple-element.143), channel_id=1, source_target_pairs={{0,48},{4,52},{8,56},{12,60},{16,0},{20,4},{24,8},{28,12},{32,16},... | collective-permute-start | bytes 2162696 | tf_op jit(solution)/shard_map/ppermute | solution.py:888
  141.8 31.8 %collective-permute-start.23 = (bf16[2,4,352,128]{3,2,1,0:T(8,128)(2,1)S(1)}, bf16[2,4,352,128]{3,2,1,0:T(8,128)(2,1)S(1)}, u32[]{:S(2)}, u32[]{:S(2)}) collective-permute-start(bf16[2,4,352,128]{3,2,1,0:T(8,128)(2,1)S(1)} %get-tuple-element.144), channel_id=1, source_target_pairs={{0,32},{4,36},{8,40},{12,44},{16,48},{20,52},{24,56},{28,60},{32,0... | collective-permute-start | bytes 2162696 | tf_op jit(solution)/shard_map/ppermute | solution.py:888
  141.8 31.8 %collective-permute-start.24 = (bf16[2,4,352,128]{3,2,1,0:T(8,128)(2,1)S(1)}, bf16[2,4,352,128]{3,2,1,0:T(8,128)(2,1)S(1)}, u32[]{:S(2)}, u32[]{:S(2)}) collective-permute-start(bf16[2,4,352,128]{3,2,1,0:T(8,128)(2,1)S(1)} %get-tuple-element.146), channel_id=1, source_target_pairs={{0,4},{4,8},{8,12},{12,0},{16,20},{20,24},{24,28},{28,16},{32,36},... | collective-permute-start | bytes 2162696 | tf_op jit(solution)/shard_map/ppermute | solution.py:892
  141.8 33.9 %collective-permute-start.25 = (bf16[2,4,352,128]{3,2,1,0:T(8,128)(2,1)S(1)}, bf16[2,4,352,128]{3,2,1,0:T(8,128)(2,1)S(1)}, u32[]{:S(2)}, u32[]{:S(2)}) collective-permute-start(bf16[2,4,352,128]{3,2,1,0:T(8,128)(2,1)S(1)} %get-tuple-element.147), channel_id=1, source_target_pairs={{0,12},{4,0},{8,4},{12,8},{16,28},{20,16},{24,20},{28,24},{32,44},... | collective-permute-start | bytes 2162696 | tf_op jit(solution)/shard_map/ppermute | solution.py:892
  173.6 19.1 %collective-permute-start.26 = (bf16[2,4,352,128]{3,2,1,0:T(8,128)(2,1)S(1)}, bf16[2,4,352,128]{3,2,1,0:T(8,128)(2,1)S(1)}, u32[]{:S(2)}, u32[]{:S(2)}) collective-permute-start(bf16[2,4,352,128]{3,2,1,0:T(8,128)(2,1)S(1)} %get-tuple-element.148), channel_id=1, source_target_pairs={{0,8},{4,12},{8,0},{12,4},{16,24},{20,28},{24,16},{28,20},{32,40},... | collective-permute-start | bytes 2162696 | tf_op jit(solution)/shard_map/ppermute | solution.py:892
  211.8 14.4 %collective-permute-start.36 = (bf16[512,640]{1,0:T(8,128)(2,1)S(1)}, bf16[512,640]{1,0:T(8,128)(2,1)S(1)}, u32[]{:S(2)}, u32[]{:S(2)}) collective-permute-start(bf16[512,640]{1,0:T(8,128)(2,1)S(1)} %copy-done.20), channel_id=1, source_target_pairs={{4,0},{8,4},{12,8},{16,12},{20,16},{24,20},{28,24},{32,28},{36,32}... | collective-permute-start | bytes 1966088 | tf_op jit(solution)/shard_map/ppermute | solution.py:897
  226.2 13.4 %collective-permute-start.39 = (bf16[352,128]{1,0:T(8,128)(2,1)S(1)}, bf16[352,128]{1,0:T(8,128)(2,1)S(1)}, u32[]{:S(2)}, u32[]{:S(2)}) collective-permute-start(bf16[352,128]{1,0:T(8,128)(2,1)S(1)} %get-tuple-element.167), channel_id=1, source_target_pairs={{0,12},{4,0},{8,4},{12,8},{16,28},{20,16},{24,20},{28,24},{32,44},... | collective-permute-start | bytes 270344 | tf_op jit(solution)/shard_map/ppermute | solution.py:892
  227.2 13.2 %collective-permute-start.38 = (bf16[352,128]{1,0:T(8,128)(2,1)S(1)}, bf16[352,128]{1,0:T(8,128)(2,1)S(1)}, u32[]{:S(2)}, u32[]{:S(2)}) collective-permute-start(bf16[352,128]{1,0:T(8,128)(2,1)S(1)} %get-tuple-element.167), channel_id=1, source_target_pairs={{0,8},{4,12},{8,0},{12,4},{16,24},{20,28},{24,16},{28,20},{32,40},... | collective-permute-start | bytes 270344 | tf_op jit(solution)/shard_map/ppermute | solution.py:892
  229.3 13.7 %collective-permute-start.42 = (bf16[352,128]{1,0:T(8,128)(2,1)S(1)}, bf16[352,128]{1,0:T(8,128)(2,1)S(1)}, u32[]{:S(2)}, u32[]{:S(2)}) collective-permute-start(bf16[352,128]{1,0:T(8,128)(2,1)S(1)} %get-tuple-element.168), channel_id=1, source_target_pairs={{0,48},{4,52},{8,56},{12,60},{16,0},{20,4},{24,8},{28,12},{32,16},... | collective-permute-start | bytes 270344 | tf_op jit(solution)/shard_map/ppermute | solution.py:888
  247.7 14.5 %collective-permute-start.44 = (bf16[4,352,128]{2,1,0:T(8,128)(2,1)S(1)}, bf16[4,352,128]{2,1,0:T(8,128)(2,1)S(1)}, u32[]{:S(2)}, u32[]{:S(2)}) collective-permute-start(bf16[4,352,128]{2,1,0:T(8,128)(2,1)S(1)} %pad_maximum_fusion.a0), channel_id=1, source_target_pairs={{0,32},{4,36},{8,40},{12,44},{16,48},{20,52},{24,56},{28,60},{32,0... | collective-permute-start | bytes 1081352 | tf_op jit(solution)/shard_map/ppermute | solution.py:888
  247.8 17.8 %collective-permute-start.43 = (bf16[4,352,128]{2,1,0:T(8,128)(2,1)S(1)}, bf16[4,352,128]{2,1,0:T(8,128)(2,1)S(1)}, u32[]{:S(2)}, u32[]{:S(2)}) collective-permute-start(bf16[4,352,128]{2,1,0:T(8,128)(2,1)S(1)} %pad_maximum_fusion.a0), channel_id=1, source_target_pairs={{0,16},{4,20},{8,24},{12,28},{16,32},{20,36},{24,40},{28,44},{32,4... | collective-permute-start | bytes 1081352 | tf_op jit(solution)/shard_map/ppermute | solution.py:888
  249.2 17.5 %collective-permute-start.48 = (bf16[4,352,128]{2,1,0:T(8,128)(2,1)S(1)}, bf16[4,352,128]{2,1,0:T(8,128)(2,1)S(1)}, u32[]{:S(2)}, u32[]{:S(2)}) collective-permute-start(bf16[4,352,128]{2,1,0:T(8,128)(2,1)S(1)} %pad_maximum_fusion.1.b0), channel_id=1, source_target_pairs={{0,12},{4,0},{8,4},{12,8},{16,28},{20,16},{24,20},{28,24},{32,44},... | collective-permute-start | bytes 1081352 | tf_op jit(solution)/shard_map/ppermute | solution.py:892
  251.9 14.8 %collective-permute-start.47 = (bf16[4,352,128]{2,1,0:T(8,128)(2,1)S(1)}, bf16[4,352,128]{2,1,0:T(8,128)(2,1)S(1)}, u32[]{:S(2)}, u32[]{:S(2)}) collective-permute-start(bf16[4,352,128]{2,1,0:T(8,128)(2,1)S(1)} %pad_maximum_fusion.1.b0), channel_id=1, source_target_pairs={{0,8},{4,12},{8,0},{12,4},{16,24},{20,28},{24,16},{28,20},{32,40},... | collective-permute-start | bytes 1081352 | tf_op jit(solution)/shard_map/ppermute | solution.py:892
  (58 other events, 589.1 us)

commit v5 on v3

--- a/solution.py
+++ b/solution.py
@@ -948,12 +948,13 @@
     q_partner = swap_near(query_weight)
     kv = jnp.concatenate([key_weight, value_weight], axis=1)
     kv_partner = swap_far(kv)
-    wg_partner, wu_partner = swap_near(gate_weight), swap_far(up_weight)
     halo = shifted(own, 1)
     rows = (norm_in, norm_attn, norm_ffn_in, norm_ffn_out, norm_query, norm_key)
     q_partner, rows = together(q_partner, rows)
     tile = pack(rows)
     tiles = [tile, swap_core(tile), swap_near(tile), swap_across(tile)]
+    tiles, wg, wu = together(tiles, gate_weight, up_weight)
+    wg_partner, wu_partner = swap_near(wg), swap_far(wu)
     tiles = [
         jnp.where(
             j // 2 == z_lo,
@@ -966,18 +967,19 @@
     head_gains = jnp.concatenate([t[:, :64] for t in tiles], axis=1)
     q_shares = (query_weight, swap_core(query_weight), q_partner, swap_core(q_partner))
     kv_shares = (kv, swap_core(kv), kv_partner, swap_core(kv_partner))
-    (q_shares, kv_shares, halo), (wg_partner, wu_partner) = together(
-        (q_shares, kv_shares, halo), (wg_partner, wu_partner)
+    q_shares, kv_shares, halo, wo, wd = together(
+        q_shares, kv_shares, halo, output_weight, down_weight
     )
-    wo_partner, wd_partner = swap_near(output_weight), swap_far(down_weight)
+    wo_partner, wd_partner = swap_near(wo), swap_far(wd)
 
     cosine, sine = rope_tables(offsets)
     column = offsets[:, None]
     normed, q, k, v, q_proj, k_proj = project(
         place, halo, own, gains, head_gains, q_shares, kv_shares, cosine, sine
     )
+    (q, k, v), wg_partner, wu_partner = together((q, k, v), wg_partner, wu_partner)
     attended, level = attend(q, k, v, column)
-    own_weights = (output_weight, gate_weight, up_weight, down_weight)
+    own_weights = (wo, wg, wu, wd)
     partners = (wo_partner, wg_partner, wu_partner, wd_partner)
     attended, own_weights = together(attended, own_weights)
     siblings = [swap_core(w) for w in own_weights]

time: 274 us -> 271 us (0.989)
  waiting for transfers between devices: 103 us -> 108 us
  starting transfers between devices: 56.3 us -> 52.1 us
  local copies, waits for them, and re-layouts: 21.7 us -> 18.4 us
    ppermute x5, waiting for transfers between devices: 11.2 us -> 0.53 us  [swap_near(): return lax.ppermute(value, 'fsdp', [(0, 2), (1, 3), (2, 0), (3, 1)])]
    ppermute x4, waiting for transfers between devices: 2.98 us -> 11.8 us  [swap_far(): return lax.ppermute(value, ('seq', 'fsdp'), along_z(lambda z: 3 - z))]
    ppermute x1, waiting for transfers between devices: 1.72 us -> 10 us  [swap_across(): return lax.ppermute(value, 'fsdp', [(0, 3), (1, 2), (2, 1), (3, 0)])]
    ppermute x15, starting transfers between devices: 9.53 us -> 4.16 us  [swap_core(): return lax.ppermute(value, 'fsdp', [(0, 1), (1, 0), (2, 3), (3, 2)])]
    ppermute x4, starting transfers between devices: 3.75 us -> 7.23 us  [swap_far(): return lax.ppermute(value, ('seq', 'fsdp'), along_z(lambda z: 3 - z))]
    unnamed x81 -> x69, local copies, waits for them, and re-layouts: 18.3 us -> 15 us
  transfers between devices with their start and end apart: 52 -> 52, of which waited for: 28 -> 29; matrix products, arithmetic and copies ran while one was open for 2% -> 2% of each run, Pallas kernels for 11% -> 12%
where the time goes in v5:
time: 271 us; the launch traced here: 267 us
  waiting for transfers between devices  108 us (40%)
  Pallas kernels  82.5 us (30%)
  starting transfers between devices  52.1 us (19%)
  local copies, waits for them, and re-layouts  18.4 us (7%)
  other arithmetic  3.5 us (1%)
    ppermute x12, waiting for transfers between devices, move_x(): return lax.ppermute(value, 'seq', along_xy(d, 0))  43.8 us
    pallas_call x1, Pallas kernels, middle_part(): pl.pallas_call(middle_kernel, name='middle_part', in_specs=[pl.BlockSpec(...  39 us
    ppermute x12, waiting for transfers between devices, move_y(): return lax.ppermute(value, 'seq', along_xy(0, d))  29.5 us
    ppermute x12, starting transfers between devices, move_y(): return lax.ppermute(value, 'seq', along_xy(0, d))  16.8 us
    unnamed x69, local copies, waits for them, and re-layouts  15 us
    ppermute x12, starting transfers between devices, move_x(): return lax.ppermute(value, 'seq', along_xy(d, 0))  12.1 us
    ppermute x4, waiting for transfers between devices, swap_far(): return lax.ppermute(value, ('seq', 'fsdp'), along_z(lambda z: 3 - z))  11.8 us
    pallas_call x1, Pallas kernels, attend_back(): pl.pallas_call(attend_back_kernel, name='attend_back', grid=(2,), in_spec...  10.7 us
  transfers between devices with their start and end apart: 52, of which 29 were waited for; matrix products, arithmetic and copies ran while one was open for 2% of the time, Pallas kernels for 12%

profile of v5, /device:TPU:0, one launch (start us, length us, event | category | flops | bytes accessed | tf_op | source)
XLA Modules:
  0.0 266.8 jit_solution(13796903182885865304)
XLA Ops:
  7.0 3.5 %collective-permute-start.6 = (bf16[512,640]{1,0:T(8,128)(2,1)}, bf16[512,640]{1,0:T(8,128)(2,1)S(1)}, u32[]{:S(2)}, u32[]{:S(2)}) collective-permute-start(bf16[512,640]{1,0:T(8,128)(2,1)} %bitcast.36), channel_id=1, source_target_pairs={{0,4},{4,8},{8,12},{12,16},{16,20},{20,24},{24,28},{28,32},{32,36}... | collective-permute-start | bytes 1966088 | tf_op jit(solution)/shard_map/ppermute | solution.py:892
  19.2 10.0 %collective-permute-done.9 = f32[8,256]{1,0:T(8,128)S(1)} collective-permute-done((f32[8,256]{1,0:T(8,128)S(1)}, f32[8,256]{1,0:T(8,128)S(1)}, u32[]{:S(2)}, u32[]{:S(2)}) %collective-permute-start.9) | collective-permute-done | bytes 8224 | tf_op jit(solution)/shard_map/ppermute | solution.py:871
  41.2 5.5 %project.1 = (bf16[1024,640]{1,0:T(8,128)(2,1)S(1)}, bf16[512,1024]{1,0:T(8,128)(2,1)S(1)}, bf16[1024,256]{1,0:T(8,128)(2,1)S(1)}, bf16[1024,256]{1,0:T(8,128)(2...) custom-call(s32[1]{0:T(128)} %bitcast.place, bf16[512,640]{1,0:T(8,128)(2,1)S(1)} %collective-permute-done.6.halo, ...), custom_call_target="tpu_custom_call" | custom-call | flops 1350000000 | bytes 9000000 | tf_op jit(solution)/shard_map/project/pallas_call | solution.py:183
  50.1 3.9 %attend.1 = (bf16[512,1024]{1,0:T(8,128)(2,1)S(1)}, f32[4,512,1]{2,1,0:T(8,128)S(1)}) custom-call(bf16[512,1024]{1,0:T(8,128)(2,1)S(1)} %get-tuple-element.137.q, bf16[1024,256]{1,0:T(8,128)(2,1)S(1)} %get-tuple-element.138.k, bf16[1024,256]{1,0:T(8,128)(2,1)S(1)} %get-tuple-element.139.v, s32[512,1]{1,0:T(8,128)S(1)} %copy.31.offsets), custom_call_target="tpu_custom_call" | custom-call | flops 1700000000 | bytes 4000000 | tf_op jit(solution)/shard_map/attend/pallas_call | solution.py:250
  56.0 7.2 %collective-permute-done.13.d2 = bf16[512,640]{1,0:T(8,128)(2,1)S(1)} collective-permute-done((bf16[512,640]{1,0:T(8,128)(2,1)}, bf16[512,640]{1,0:T(8,128)(2,1)S(1)}, u32[]{:S(2)}, u32[]{:S(2)}) %collective-permute-start.13) | collective-permute-done | bytes 655392 | tf_op jit(solution)/shard_map/ppermute | solution.py:875
  69.0 39.0 %middle_part.1 = (bf16[512,640]{1,0:T(8,128)(2,1)}, f32[512,640]{1,0:T(8,128)}, bf16[512,640]{1,0:T(8,128)(2,1)S(1)}, bf16[512,1024]{1,0:T(8,128)(2,1)}, f32[8,6...) custom-call(s32[1]{0:T(128)} %bitcast.place, bf16[512,640]{1,0:T(8,128)(2,1)S(1)} %bitcast.38, ...), custom_call_target="tpu_custom_call" | custom-call | flops 13400000512 | bytes 23000000 | tf_op jit(solution)/shard_map/middle_part/pallas_call | solution.py:393
  110.6 10.7 %attend_back.1 = (bf16[512,1024]{1,0:T(8,128)(2,1)S(1)}, bf16[1024,512]{1,0:T(8,128)(2,1)S(1)}, f32[8,256]{1,0:T(8,128)S(1)}, bf16[512,640]{1,0:T(8,128)(2,1)S(1)}) custom-call(bf16[512,1024]{1,0:T(8,128)(2,1)S(1)} %get-tuple-element.137.q, bf16[1024,256]{1,0:T(8,128)(2,1)S(1)} %get-tuple-element.138.k, bf16[1024,256]{1,0:T(8,128)(2,1)S(1)} %get-tuple-element.139.v, ...), custom_call_target="tpu_custom_call" | custom-call | flops 4300000256 | bytes 10000000 | tf_op jit(solution)/shard_map/attend_back/pallas_call | solution.py:504
  123.2 7.2 %weights_part.1 = (f32[512,640]{1,0:T(8,128)S(1)}, bf16[2,3584,128]{2,1,0:T(8,128)(2,1)S(1)}, bf16[2,3584,128]{2,1,0:T(8,128)(2,1)}) custom-call(s32[1]{0:T(128)} %bitcast.place, bf16[1024,640]{1,0:T(8,128)(2,1)S(1)} %get-tuple-element.159.normed, bf16[512,1024]{1,0:T(8,128)(2,1)S(1)} %get-tuple-element.164.back_q, ...), custom_call_target="tpu_custom_call" | custom-call | flops 3400000000 | bytes 14000000 | tf_op jit(solution)/shard_map/weights_part/pallas_call | solution.py:623
  130.9 3.7 %collective-permute-done.23 = bf16[2,3584,128]{2,1,0:T(8,128)(2,1)} collective-permute-done((bf16[2,3584,128]{2,1,0:T(8,128)(2,1)}, bf16[2,3584,128]{2,1,0:T(8,128)(2,1)}, u32[]{:S(2)}, u32[]{:S(2)}) %collective-permute-start.23) | collective-permute-done | bytes 1835040 | tf_op jit(solution)/shard_map/ppermute | solution.py:863
  136.7 4.1 %first_sums.1 = (bf16[2,4,352,128]{3,2,1,0:T(8,128)(2,1)S(1)}, bf16[2,4,352,128]{3,2,1,0:T(8,128)(2,1)S(1)}, bf16[2,4,352,128]{3,2,1,0:T(8,128)(2,1)S(1)}, bf16[...) custom-call(s32[2]{0:T(128)S(1)} %pad_add_fusion.spot, ...), custom_call_target="tpu_custom_call" | custom-call | flops 3000000 | bytes 17000000 | tf_op jit(solution)/shard_map/first_sums/pallas_call | solution.py:768
  140.9 3.2 %collective-permute-start.25 = (bf16[2,4,352,128]{3,2,1,0:T(8,128)(2,1)S(1)}, bf16[2,4,352,128]{3,2,1,0:T(8,128)(2,1)S(1)}, u32[]{:S(2)}, u32[]{:S(2)}) collective-permute-start(bf16[2,4,352,128]{3,2,1,0:T(8,128)(2,1)S(1)} %get-tuple-element.176), channel_id=1, source_target_pairs={{0,48},{4,52},{8,56},{12,60},{16,0},{20,4},{24,8},{28,12},{32,16},... | collective-permute-start | bytes 2162696 | tf_op jit(solution)/shard_map/ppermute | solution.py:883
  144.1 3.4 %collective-permute-start.28 = (bf16[2,4,352,128]{3,2,1,0:T(8,128)(2,1)S(1)}, bf16[2,4,352,128]{3,2,1,0:T(8,128)(2,1)S(1)}, u32[]{:S(2)}, u32[]{:S(2)}) collective-permute-start(bf16[2,4,352,128]{3,2,1,0:T(8,128)(2,1)S(1)} %get-tuple-element.180), channel_id=1, source_target_pairs={{0,12},{4,0},{8,4},{12,8},{16,28},{20,16},{24,20},{28,24},{32,44},... | collective-permute-start | bytes 2162696 | tf_op jit(solution)/shard_map/ppermute | solution.py:887
  147.5 28.4 %collective-permute-done.24.refs_1_ = bf16[2,4,352,128]{3,2,1,0:T(8,128)(2,1)S(1)} collective-permute-done((bf16[2,4,352,128]{3,2,1,0:T(8,128)(2,1)S(1)}, bf16[2,4,352,128]{3,2,1,0:T(8,128)(2,1)S(1)}, u32[]{:S(2)}, u32[]{:S(2)}) %collective-permute-start.24) | collective-permute-done | bytes 720928 | tf_op jit(solution)/shard_map/ppermute | solution.py:883
  177.2 14.8 %collective-permute-done.28.refs_6_ = bf16[2,4,352,128]{3,2,1,0:T(8,128)(2,1)S(1)} collective-permute-done((bf16[2,4,352,128]{3,2,1,0:T(8,128)(2,1)S(1)}, bf16[2,4,352,128]{3,2,1,0:T(8,128)(2,1)S(1)}, u32[]{:S(2)}, u32[]{:S(2)}) %collective-permute-start.28) | collective-permute-done | bytes 720928 | tf_op jit(solution)/shard_map/ppermute | solution.py:887
  192.1 2.9 %collective-permute-done.29.refs_7_ = bf16[2,4,352,128]{3,2,1,0:T(8,128)(2,1)S(1)} collective-permute-done((bf16[2,4,352,128]{3,2,1,0:T(8,128)(2,1)S(1)}, bf16[2,4,352,128]{3,2,1,0:T(8,128)(2,1)S(1)}, u32[]{:S(2)}, u32[]{:S(2)}) %collective-permute-start.29) | collective-permute-done | bytes 720928 | tf_op jit(solution)/shard_map/ppermute | solution.py:887
  196.4 3.2 %collective-permute-start.31 = (bf16[2,352,128]{2,1,0:T(8,128)(2,1)S(1)}, bf16[2,352,128]{2,1,0:T(8,128)(2,1)S(1)}, u32[]{:S(2)}, u32[]{:S(2)}) collective-permute-start(bf16[2,352,128]{2,1,0:T(8,128)(2,1)S(1)} %get-tuple-element.184), channel_id=1, source_target_pairs={{0,12},{4,0},{8,4},{12,8},{16,28},{20,16},{24,20},{28,24},{32,44},... | collective-permute-start | bytes 540680 | tf_op jit(solution)/shard_map/ppermute | solution.py:887
  199.6 3.1 %collective-permute-start.33 = (bf16[2,352,128]{2,1,0:T(8,128)(2,1)S(1)}, bf16[2,352,128]{2,1,0:T(8,128)(2,1)S(1)}, u32[]{:S(2)}, u32[]{:S(2)}) collective-permute-start(bf16[2,352,128]{2,1,0:T(8,128)(2,1)S(1)} %get-tuple-element.187), channel_id=1, source_target_pairs={{0,16},{4,20},{8,24},{12,28},{16,32},{20,36},{24,40},{28,44},{32,4... | collective-permute-start | bytes 540680 | tf_op jit(solution)/shard_map/ppermute | solution.py:883
  202.7 4.2 %collective-permute-done.30.refs_1_ = bf16[2,352,128]{2,1,0:T(8,128)(2,1)S(1)} collective-permute-done((bf16[2,352,128]{2,1,0:T(8,128)(2,1)S(1)}, bf16[2,352,128]{2,1,0:T(8,128)(2,1)S(1)}, u32[]{:S(2)}, u32[]{:S(2)}) %collective-permute-start.30) | collective-permute-done | bytes 180256 | tf_op jit(solution)/shard_map/ppermute | solution.py:887
  207.0 5.4 %collective-permute-done.34.refs_6_ = bf16[2,352,128]{2,1,0:T(8,128)(2,1)S(1)} collective-permute-done((bf16[2,352,128]{2,1,0:T(8,128)(2,1)S(1)}, bf16[2,352,128]{2,1,0:T(8,128)(2,1)S(1)}, u32[]{:S(2)}, u32[]{:S(2)}) %collective-permute-start.34) | collective-permute-done | bytes 180256 | tf_op jit(solution)/shard_map/ppermute | solution.py:883
  217.7 3.6 %collective-permute-done.38.p3 = bf16[2,352,128]{2,1,0:T(8,128)(2,1)S(1)} collective-permute-done((bf16[2,352,128]{2,1,0:T(8,128)(2,1)S(1)}, bf16[2,352,128]{2,1,0:T(8,128)(2,1)S(1)}, u32[]{:S(2)}, u32[]{:S(2)}) %collective-permute-start.38) | collective-permute-done | bytes 180256 | tf_op jit(solution)/shard_map/ppermute | solution.py:879
  232.4 2.9 %collective-permute-done.44 = bf16[352,128]{1,0:T(8,128)(2,1)S(1)} collective-permute-done((bf16[352,128]{1,0:T(8,128)(2,1)S(1)}, bf16[352,128]{1,0:T(8,128)(2,1)S(1)}, u32[]{:S(2)}, u32[]{:S(2)}) %collective-permute-start.44) | collective-permute-done | bytes 90144 | tf_op jit(solution)/shard_map/ppermute | solution.py:883
  235.3 3.6 %collective-permute-done.43 = bf16[352,128]{1,0:T(8,128)(2,1)S(1)} collective-permute-done((bf16[352,128]{1,0:T(8,128)(2,1)S(1)}, bf16[352,128]{1,0:T(8,128)(2,1)S(1)}, u32[]{:S(2)}, u32[]{:S(2)}) %collective-permute-start.43) | collective-permute-done | bytes 90144 | tf_op jit(solution)/shard_map/ppermute | solution.py:883
  253.0 3.8 %collective-permute-done.49.b1 = bf16[4,352,128]{2,1,0:T(8,128)(2,1)S(1)} collective-permute-done((bf16[4,352,128]{2,1,0:T(8,128)(2,1)S(1)}, bf16[4,352,128]{2,1,0:T(8,128)(2,1)S(1)}, u32[]{:S(2)}, u32[]{:S(2)}) %collective-permute-start.49) | collective-permute-done | bytes 360480 | tf_op jit(solution)/shard_map/ppermute | solution.py:887
  256.8 8.7 %unpack.1 = (f32[160,1024]{1,0:T(8,128)}, f32[160,256]{1,0:T(8,128)}, f32[160,256]{1,0:T(8,128)}, f32[256,640]{1,0:T(8,128)}, f32[160,2048]{1,0:T(8,128)}, /*ind...) custom-call(s32[2]{0:T(128)S(1)} %pad_add_fusion.spot, bf16[4,352,128]{2,1,0:T(8,128)(2,1)S(1)} %pad_maximum_fusion.a0, ...), custom_call_target="tpu_custom_call" | custom-call | flops 4000000 | bytes 11000000 | tf_op jit(solution)/shard_map/unpack/pallas_call | solution.py:727
  (182 shorter events, 78.6 us)
Async XLA Ops:
  0.7 12.4 %collective-permute-start.1 = (bf16[160,1024]{1,0:T(8,128)(2,1)}, bf16[160,1024]{1,0:T(8,128)(2,1)S(1)}, u32[]{:S(2)}, u32[]{:S(2)}) collective-permute-start(bf16[160,1024]{1,0:T(8,128)(2,1)} %q0.1), channel_id=1, source_target_pairs={{0,2},{1,3},{2,0},{3,1},{4,6},{5,7},{6,4},{7,5},{8,10},{9,11},{10,... | collective-permute-start | bytes 983048 | tf_op jit(solution)/shard_map/ppermute | solution.py:867
  4.5 14.6 %collective-permute-start.4 = (bf16[160,512]{1,0:T(8,128)(2,1)S(1)}, bf16[160,512]{1,0:T(8,128)(2,1)S(1)}, u32[]{:S(2)}, u32[]{:S(2)}) collective-permute-start(bf16[160,512]{1,0:T(8,128)(2,1)S(1)} %constant_dynamic-update-slice_fusion.kv0), channel_id=1, source_target_pairs={{0,66},{1,67},{2,64},{3,65},{4,70},{5,71},{6,68},{7,69},{8,74},{9,... | collective-permute-start | bytes 491528 | tf_op jit(solution)/shard_map/ppermute | solution.py:875
  7.0 28.9 %collective-permute-start.6 = (bf16[512,640]{1,0:T(8,128)(2,1)}, bf16[512,640]{1,0:T(8,128)(2,1)S(1)}, u32[]{:S(2)}, u32[]{:S(2)}) collective-permute-start(bf16[512,640]{1,0:T(8,128)(2,1)} %bitcast.36), channel_id=1, source_target_pairs={{0,4},{4,8},{8,12},{12,16},{16,20},{20,24},{24,28},{28,32},{32,36}... | collective-permute-start | bytes 1966088 | tf_op jit(solution)/shard_map/ppermute | solution.py:892
  17.1 12.1 %collective-permute-start.9 = (f32[8,256]{1,0:T(8,128)S(1)}, f32[8,256]{1,0:T(8,128)S(1)}, u32[]{:S(2)}, u32[]{:S(2)}) collective-permute-start(f32[8,256]{1,0:T(8,128)S(1)} %pack.1), channel_id=1, source_target_pairs={{0,3},{1,2},{2,1},{3,0},{4,7},{5,6},{6,5},{7,4},{8,11},{9,10},{10,... | collective-permute-start | bytes 24584 | tf_op jit(solution)/shard_map/ppermute | solution.py:871
  17.2 12.1 %collective-permute-start.8 = (f32[8,256]{1,0:T(8,128)S(1)}, f32[8,256]{1,0:T(8,128)S(1)}, u32[]{:S(2)}, u32[]{:S(2)}) collective-permute-start(f32[8,256]{1,0:T(8,128)S(1)} %pack.1), channel_id=1, source_target_pairs={{0,2},{1,3},{2,0},{3,1},{4,6},{5,7},{6,4},{7,5},{8,10},{9,11},{10,... | collective-permute-start | bytes 24584 | tf_op jit(solution)/shard_map/ppermute | solution.py:867
  18.3 11.0 %collective-permute-start.7 = (f32[8,256]{1,0:T(8,128)S(1)}, f32[8,256]{1,0:T(8,128)S(1)}, u32[]{:S(2)}, u32[]{:S(2)}) collective-permute-start(f32[8,256]{1,0:T(8,128)S(1)} %pack.1), channel_id=1, source_target_pairs={{0,1},{1,0},{2,3},{3,2},{4,5},{5,4},{6,7},{7,6},{8,9},{9,8},{10,11... | collective-permute-start | bytes 24584 | tf_op jit(solution)/shard_map/ppermute | solution.py:863
  19.1 14.6 %collective-permute-start.3 = (bf16[160,512]{1,0:T(8,128)(2,1)S(1)}, bf16[160,512]{1,0:T(8,128)(2,1)S(1)}, u32[]{:S(2)}, u32[]{:S(2)}) collective-permute-start(bf16[160,512]{1,0:T(8,128)(2,1)S(1)} %constant_dynamic-update-slice_fusion.kv0), channel_id=1, source_target_pairs={{0,1},{1,0},{2,3},{3,2},{4,5},{5,4},{6,7},{7,6},{8,9},{9,8},{10,11... | collective-permute-start | bytes 491528 | tf_op jit(solution)/shard_map/ppermute | solution.py:863
  29.3 17.9 %collective-permute-start.10 = (bf16[160,2048]{1,0:T(8,128)(2,1)}, bf16[160,2048]{1,0:T(8,128)(2,1)}, u32[]{:S(2)}, u32[]{:S(2)}) collective-permute-start(bf16[160,2048]{1,0:T(8,128)(2,1)} %g0.1), channel_id=1, source_target_pairs={{0,2},{1,3},{2,0},{3,1},{4,6},{5,7},{6,4},{7,5},{8,10},{9,11},{10,... | collective-permute-start | bytes 1966088 | tf_op jit(solution)/shard_map/ppermute | solution.py:867
  30.9 19.1 %collective-permute-start.11 = (bf16[160,2048]{1,0:T(8,128)(2,1)}, bf16[160,2048]{1,0:T(8,128)(2,1)}, u32[]{:S(2)}, u32[]{:S(2)}) collective-permute-start(bf16[160,2048]{1,0:T(8,128)(2,1)} %u0), channel_id=1, source_target_pairs={{0,66},{1,67},{2,64},{3,65},{4,70},{5,71},{6,68},{7,69},{8,74},{9,... | collective-permute-start | bytes 1966088 | tf_op jit(solution)/shard_map/ppermute | solution.py:875
  35.9 19.0 %collective-permute-start.12 = (bf16[256,640]{1,0:T(8,128)(2,1)}, bf16[256,640]{1,0:T(8,128)(2,1)S(1)}, u32[]{:S(2)}, u32[]{:S(2)}) collective-permute-start(bf16[256,640]{1,0:T(8,128)(2,1)} %o0), channel_id=1, source_target_pairs={{0,2},{1,3},{2,0},{3,1},{4,6},{5,7},{6,4},{7,5},{8,10},{9,11},{10,... | collective-permute-start | bytes 983048 | tf_op jit(solution)/shard_map/ppermute | solution.py:867
  36.4 26.8 %collective-permute-start.13 = (bf16[512,640]{1,0:T(8,128)(2,1)}, bf16[512,640]{1,0:T(8,128)(2,1)S(1)}, u32[]{:S(2)}, u32[]{:S(2)}) collective-permute-start(bf16[512,640]{1,0:T(8,128)(2,1)} %d0), channel_id=1, source_target_pairs={{0,66},{1,67},{2,64},{3,65},{4,70},{5,71},{6,68},{7,69},{8,74},{9,... | collective-permute-start | bytes 1966088 | tf_op jit(solution)/shard_map/ppermute | solution.py:875
  107.9 26.7 %collective-permute-start.22 = (bf16[2,7680,128]{2,1,0:T(8,128)(2,1)}, bf16[2,7680,128]{2,1,0:T(8,128)(2,1)}, u32[]{:S(2)}, u32[]{:S(2)}) collective-permute-start(bf16[2,7680,128]{2,1,0:T(8,128)(2,1)} %get-tuple-element.171), channel_id=1, source_target_pairs={{0,1},{1,0},{2,3},{3,2},{4,5},{5,4},{6,7},{7,6},{8,9},{9,8},{10,11... | collective-permute-start | bytes 11796488 | tf_op jit(solution)/shard_map/ppermute | solution.py:863
  140.8 35.1 %collective-permute-start.24 = (bf16[2,4,352,128]{3,2,1,0:T(8,128)(2,1)S(1)}, bf16[2,4,352,128]{3,2,1,0:T(8,128)(2,1)S(1)}, u32[]{:S(2)}, u32[]{:S(2)}) collective-permute-start(bf16[2,4,352,128]{3,2,1,0:T(8,128)(2,1)S(1)} %get-tuple-element.175), channel_id=1, source_target_pairs={{0,16},{4,20},{8,24},{12,28},{16,32},{20,36},{24,40},{28,44},{32,4... | collective-permute-start | bytes 2162696 | tf_op jit(solution)/shard_map/ppermute | solution.py:883
  140.9 35.1 %collective-permute-start.25 = (bf16[2,4,352,128]{3,2,1,0:T(8,128)(2,1)S(1)}, bf16[2,4,352,128]{3,2,1,0:T(8,128)(2,1)S(1)}, u32[]{:S(2)}, u32[]{:S(2)}) collective-permute-start(bf16[2,4,352,128]{3,2,1,0:T(8,128)(2,1)S(1)} %get-tuple-element.176), channel_id=1, source_target_pairs={{0,48},{4,52},{8,56},{12,60},{16,0},{20,4},{24,8},{28,12},{32,16},... | collective-permute-start | bytes 2162696 | tf_op jit(solution)/shard_map/ppermute | solution.py:883
  144.1 33.1 %collective-permute-start.26 = (bf16[2,4,352,128]{3,2,1,0:T(8,128)(2,1)S(1)}, bf16[2,4,352,128]{3,2,1,0:T(8,128)(2,1)S(1)}, u32[]{:S(2)}, u32[]{:S(2)}) collective-permute-start(bf16[2,4,352,128]{3,2,1,0:T(8,128)(2,1)S(1)} %get-tuple-element.177), channel_id=1, source_target_pairs={{0,32},{4,36},{8,40},{12,44},{16,48},{20,52},{24,56},{28,60},{32,0... | collective-permute-start | bytes 2162696 | tf_op jit(solution)/shard_map/ppermute | solution.py:883
  144.1 33.1 %collective-permute-start.27 = (bf16[2,4,352,128]{3,2,1,0:T(8,128)(2,1)S(1)}, bf16[2,4,352,128]{3,2,1,0:T(8,128)(2,1)S(1)}, u32[]{:S(2)}, u32[]{:S(2)}) collective-permute-start(bf16[2,4,352,128]{3,2,1,0:T(8,128)(2,1)S(1)} %get-tuple-element.179), channel_id=1, source_target_pairs={{0,4},{4,8},{8,12},{12,0},{16,20},{20,24},{24,28},{28,16},{32,36},... | collective-permute-start | bytes 2162696 | tf_op jit(solution)/shard_map/ppermute | solution.py:887
  144.1 47.9 %collective-permute-start.28 = (bf16[2,4,352,128]{3,2,1,0:T(8,128)(2,1)S(1)}, bf16[2,4,352,128]{3,2,1,0:T(8,128)(2,1)S(1)}, u32[]{:S(2)}, u32[]{:S(2)}) collective-permute-start(bf16[2,4,352,128]{3,2,1,0:T(8,128)(2,1)S(1)} %get-tuple-element.180), channel_id=1, source_target_pairs={{0,12},{4,0},{8,4},{12,8},{16,28},{20,16},{24,20},{28,24},{32,44},... | collective-permute-start | bytes 2162696 | tf_op jit(solution)/shard_map/ppermute | solution.py:887
  175.9 19.1 %collective-permute-start.29 = (bf16[2,4,352,128]{3,2,1,0:T(8,128)(2,1)S(1)}, bf16[2,4,352,128]{3,2,1,0:T(8,128)(2,1)S(1)}, u32[]{:S(2)}, u32[]{:S(2)}) collective-permute-start(bf16[2,4,352,128]{3,2,1,0:T(8,128)(2,1)S(1)} %get-tuple-element.181), channel_id=1, source_target_pairs={{0,8},{4,12},{8,0},{12,4},{16,24},{20,28},{24,16},{28,20},{32,40},... | collective-permute-start | bytes 2162696 | tf_op jit(solution)/shard_map/ppermute | solution.py:887
  175.9 47.1 %collective-permute-start.39 = (bf16[512,640]{1,0:T(8,128)(2,1)S(1)}, bf16[512,640]{1,0:T(8,128)(2,1)S(1)}, u32[]{:S(2)}, u32[]{:S(2)}) collective-permute-start(bf16[512,640]{1,0:T(8,128)(2,1)S(1)} %copy-done.16), channel_id=1, source_target_pairs={{4,0},{8,4},{12,8},{16,12},{20,16},{24,20},{28,24},{32,28},{36,32}... | collective-permute-start | bytes 1966088 | tf_op jit(solution)/shard_map/ppermute | solution.py:892
  196.3 10.6 %collective-permute-start.30 = (bf16[2,352,128]{2,1,0:T(8,128)(2,1)S(1)}, bf16[2,352,128]{2,1,0:T(8,128)(2,1)S(1)}, u32[]{:S(2)}, u32[]{:S(2)}) collective-permute-start(bf16[2,352,128]{2,1,0:T(8,128)(2,1)S(1)} %get-tuple-element.183), channel_id=1, source_target_pairs={{0,4},{4,8},{8,12},{12,0},{16,20},{20,24},{24,28},{28,16},{32,36},... | collective-permute-start | bytes 540680 | tf_op jit(solution)/shard_map/ppermute | solution.py:887
  196.4 10.6 %collective-permute-start.31 = (bf16[2,352,128]{2,1,0:T(8,128)(2,1)S(1)}, bf16[2,352,128]{2,1,0:T(8,128)(2,1)S(1)}, u32[]{:S(2)}, u32[]{:S(2)}) collective-permute-start(bf16[2,352,128]{2,1,0:T(8,128)(2,1)S(1)} %get-tuple-element.184), channel_id=1, source_target_pairs={{0,12},{4,0},{8,4},{12,8},{16,28},{20,16},{24,20},{28,24},{32,44},... | collective-permute-start | bytes 540680 | tf_op jit(solution)/shard_map/ppermute | solution.py:887
  239.1 11.5 %collective-permute-start.47 = (bf16[4,352,128]{2,1,0:T(8,128)(2,1)S(1)}, bf16[4,352,128]{2,1,0:T(8,128)(2,1)S(1)}, u32[]{:S(2)}, u32[]{:S(2)}) collective-permute-start(bf16[4,352,128]{2,1,0:T(8,128)(2,1)S(1)} %pad_maximum_fusion.a0), channel_id=1, source_target_pairs={{0,32},{4,36},{8,40},{12,44},{16,48},{20,52},{24,56},{28,60},{32,0... | collective-permute-start | bytes 1081352 | tf_op jit(solution)/shard_map/ppermute | solution.py:883
  240.3 11.6 %collective-permute-start.46 = (bf16[4,352,128]{2,1,0:T(8,128)(2,1)S(1)}, bf16[4,352,128]{2,1,0:T(8,128)(2,1)S(1)}, u32[]{:S(2)}, u32[]{:S(2)}) collective-permute-start(bf16[4,352,128]{2,1,0:T(8,128)(2,1)S(1)} %pad_maximum_fusion.a0), channel_id=1, source_target_pairs={{0,16},{4,20},{8,24},{12,28},{16,32},{20,36},{24,40},{28,44},{32,4... | collective-permute-start | bytes 1081352 | tf_op jit(solution)/shard_map/ppermute | solution.py:883
  241.6 11.2 %collective-permute-start.51 = (bf16[4,352,128]{2,1,0:T(8,128)(2,1)S(1)}, bf16[4,352,128]{2,1,0:T(8,128)(2,1)S(1)}, u32[]{:S(2)}, u32[]{:S(2)}) collective-permute-start(bf16[4,352,128]{2,1,0:T(8,128)(2,1)S(1)} %pad_maximum_fusion.1.b0), channel_id=1, source_target_pairs={{0,12},{4,0},{8,4},{12,8},{16,28},{20,16},{24,20},{28,24},{32,44},... | collective-permute-start | bytes 1081352 | tf_op jit(solution)/shard_map/ppermute | solution.py:887
  (62 other events, 662.7 us)

commit v6 on v5

--- a/solution.py
+++ b/solution.py
@@ -748,6 +748,10 @@
     return whole.astype(bf16)
 
 
+def paired(parts):
+    return [part for pair in zip(parts[:4], parts[4:]) for part in pair]
+
+
 def turn_around(position, d):
     return lax.rem(position + d, 4)
 
@@ -779,7 +783,7 @@
 def second_kernel(spot, *refs):
     ins, outs = refs[:8], refs[8:]
     for half in range(2):
-        parts = ins[4 * half : 4 * half + 4]
+        parts = ins[half::2]
         for i, d in enumerate((0, 1, 3, 2)):
             at = turn_around(spot[1 - half], d)
             for z in range(2):
@@ -795,14 +799,14 @@
         out_shape=[spec(2, 352, 128, bf16)] * 8,
         compiler_params=params(12),
         cost_estimate=cost(1_000_000, 7_200_000),
-    )(spot, *parts)
+    )(spot, *paired(parts))
 
 
 def third_kernel(place, *refs):
     ins, (mine, other) = refs[:8], refs[8:]
     z = lax.div(place[0], 2)
     for half in range(2):
-        parts = ins[4 * half : 4 * half + 4]
+        parts = ins[half::2]
         mine[half] = sum_of([r[z] for r in parts])
         other[half] = sum_of([r[1 - z] for r in parts])
 
@@ -816,7 +820,7 @@
         out_shape=[spec(2, 352, 128, bf16)] * 2,
         compiler_params=params(10),
         cost_estimate=cost(1_000_000, 1_800_000),
-    )(place, *parts)
+    )(place, *paired(parts))
 
 
 def fourth_kernel(p0, p1, p2, p3, a, b):
@@ -896,21 +900,19 @@
 
 
 def move_first(parts):
-    return (
-        [parts[0]]
-        + [move_x(p, d) for p, d in zip(parts[1:4], steps)]
-        + [parts[4]]
-        + [move_y(p, d) for p, d in zip(parts[5:8], steps)]
-    )
+    moved = list(parts)
+    for i, d in zip((1, 2, 3), steps):
+        moved[i] = move_x(parts[i], d)
+        moved[4 + i] = move_y(parts[4 + i], d)
+    return moved
 
 
 def move_second(parts):
-    return (
-        [parts[0]]
-        + [move_y(p, d) for p, d in zip(parts[1:4], steps)]
-        + [parts[4]]
-        + [move_x(p, d) for p, d in zip(parts[5:8], steps)]
-    )
+    moved = list(parts)
+    for i, d in zip((1, 2, 3), steps):
+        moved[i] = move_y(parts[i], d)
+        moved[4 + i] = move_x(parts[4 + i], d)
+    return moved
 
 
 def together(*groups):

time: 271 us -> 267 us (0.985)
    ppermute x12, waiting for transfers between devices: 43.8 us -> 40.8 us  [move_x(): return lax.ppermute(value, 'seq', along_xy(d, 0))]
  transfers between devices with their start and end apart: 52 -> 52, of which waited for: 29 -> 31; matrix products, arithmetic and copies ran while one was open for 2% -> 3% of each run, Pallas kernels for 12% -> 12%
where the time goes in v6:
time: 267 us; the launch traced here: 264 us
  waiting for transfers between devices  106 us (40%)
  Pallas kernels  82.5 us (31%)
  starting transfers between devices  51.7 us (19%)
  local copies, waits for them, and re-layouts  18.4 us (7%)
  other arithmetic  3.5 us (1%)
    ppermute x12, waiting for transfers between devices, move_x(): return lax.ppermute(value, 'seq', along_xy(d, 0))  40.8 us
    pallas_call x1, Pallas kernels, middle_part(): pl.pallas_call(middle_kernel, name='middle_part', in_specs=[pl.BlockSpec(...  39 us
    ppermute x12, waiting for transfers between devices, move_y(): return lax.ppermute(value, 'seq', along_xy(0, d))  30.4 us
    ppermute x12, starting transfers between devices, move_y(): return lax.ppermute(value, 'seq', along_xy(0, d))  17.2 us
    unnamed x69, local copies, waits for them, and re-layouts  15 us
    ppermute x4, waiting for transfers between devices, swap_far(): return lax.ppermute(value, ('seq', 'fsdp'), along_z(lambda z: 3 - z))  11.8 us
    ppermute x12, starting transfers between devices, move_x(): return lax.ppermute(value, 'seq', along_xy(d, 0))  11.3 us
    pallas_call x1, Pallas kernels, attend_back(): pl.pallas_call(attend_back_kernel, name='attend_back', grid=(2,), in_spec...  10.7 us
  transfers between devices with their start and end apart: 52, of which 31 were waited for; matrix products, arithmetic and copies ran while one was open for 3% of the time, Pallas kernels for 12%

profile of v6, /device:TPU:0, one launch (start us, length us, event | category | flops | bytes accessed | tf_op | source)
XLA Modules:
  0.0 264.2 jit_solution(7318248849152031879)
XLA Ops:
  7.0 3.5 %collective-permute-start.6 = (bf16[512,640]{1,0:T(8,128)(2,1)}, bf16[512,640]{1,0:T(8,128)(2,1)S(1)}, u32[]{:S(2)}, u32[]{:S(2)}) collective-permute-start(bf16[512,640]{1,0:T(8,128)(2,1)} %bitcast.36), channel_id=1, source_target_pairs={{0,4},{4,8},{8,12},{12,16},{16,20},{20,24},{24,28},{28,32},{32,36}... | collective-permute-start | bytes 1966088 | tf_op jit(solution)/shard_map/ppermute | solution.py:896
  19.2 10.0 %collective-permute-done.9 = f32[8,256]{1,0:T(8,128)S(1)} collective-permute-done((f32[8,256]{1,0:T(8,128)S(1)}, f32[8,256]{1,0:T(8,128)S(1)}, u32[]{:S(2)}, u32[]{:S(2)}) %collective-permute-start.9) | collective-permute-done | bytes 8224 | tf_op jit(solution)/shard_map/ppermute | solution.py:875
  41.2 5.5 %project.1 = (bf16[1024,640]{1,0:T(8,128)(2,1)S(1)}, bf16[512,1024]{1,0:T(8,128)(2,1)S(1)}, bf16[1024,256]{1,0:T(8,128)(2,1)S(1)}, bf16[1024,256]{1,0:T(8,128)(2...) custom-call(s32[1]{0:T(128)} %bitcast.place, bf16[512,640]{1,0:T(8,128)(2,1)S(1)} %collective-permute-done.6.halo, ...), custom_call_target="tpu_custom_call" | custom-call | flops 1350000000 | bytes 9000000 | tf_op jit(solution)/shard_map/project/pallas_call | solution.py:183
  50.1 3.9 %attend.1 = (bf16[512,1024]{1,0:T(8,128)(2,1)S(1)}, f32[4,512,1]{2,1,0:T(8,128)S(1)}) custom-call(bf16[512,1024]{1,0:T(8,128)(2,1)S(1)} %get-tuple-element.137.q, bf16[1024,256]{1,0:T(8,128)(2,1)S(1)} %get-tuple-element.138.k, bf16[1024,256]{1,0:T(8,128)(2,1)S(1)} %get-tuple-element.139.v, s32[512,1]{1,0:T(8,128)S(1)} %copy.31.offsets), custom_call_target="tpu_custom_call" | custom-call | flops 1700000000 | bytes 4000000 | tf_op jit(solution)/shard_map/attend/pallas_call | solution.py:250
  56.0 7.2 %collective-permute-done.13.d2 = bf16[512,640]{1,0:T(8,128)(2,1)S(1)} collective-permute-done((bf16[512,640]{1,0:T(8,128)(2,1)}, bf16[512,640]{1,0:T(8,128)(2,1)S(1)}, u32[]{:S(2)}, u32[]{:S(2)}) %collective-permute-start.13) | collective-permute-done | bytes 655392 | tf_op jit(solution)/shard_map/ppermute | solution.py:879
  69.0 39.0 %middle_part.1 = (bf16[512,640]{1,0:T(8,128)(2,1)}, f32[512,640]{1,0:T(8,128)}, bf16[512,640]{1,0:T(8,128)(2,1)S(1)}, bf16[512,1024]{1,0:T(8,128)(2,1)}, f32[8,6...) custom-call(s32[1]{0:T(128)} %bitcast.place, bf16[512,640]{1,0:T(8,128)(2,1)S(1)} %bitcast.38, ...), custom_call_target="tpu_custom_call" | custom-call | flops 13400000512 | bytes 23000000 | tf_op jit(solution)/shard_map/middle_part/pallas_call | solution.py:393
  110.6 10.7 %attend_back.1 = (bf16[512,1024]{1,0:T(8,128)(2,1)S(1)}, bf16[1024,512]{1,0:T(8,128)(2,1)S(1)}, f32[8,256]{1,0:T(8,128)S(1)}, bf16[512,640]{1,0:T(8,128)(2,1)S(1)}) custom-call(bf16[512,1024]{1,0:T(8,128)(2,1)S(1)} %get-tuple-element.137.q, bf16[1024,256]{1,0:T(8,128)(2,1)S(1)} %get-tuple-element.138.k, bf16[1024,256]{1,0:T(8,128)(2,1)S(1)} %get-tuple-element.139.v, ...), custom_call_target="tpu_custom_call" | custom-call | flops 4300000256 | bytes 10000000 | tf_op jit(solution)/shard_map/attend_back/pallas_call | solution.py:504
  123.2 7.2 %weights_part.1 = (f32[512,640]{1,0:T(8,128)S(1)}, bf16[2,3584,128]{2,1,0:T(8,128)(2,1)S(1)}, bf16[2,3584,128]{2,1,0:T(8,128)(2,1)}) custom-call(s32[1]{0:T(128)} %bitcast.place, bf16[1024,640]{1,0:T(8,128)(2,1)S(1)} %get-tuple-element.159.normed, bf16[512,1024]{1,0:T(8,128)(2,1)S(1)} %get-tuple-element.164.back_q, ...), custom_call_target="tpu_custom_call" | custom-call | flops 3400000000 | bytes 14000000 | tf_op jit(solution)/shard_map/weights_part/pallas_call | solution.py:623
  130.9 3.7 %collective-permute-done.23 = bf16[2,3584,128]{2,1,0:T(8,128)(2,1)} collective-permute-done((bf16[2,3584,128]{2,1,0:T(8,128)(2,1)}, bf16[2,3584,128]{2,1,0:T(8,128)(2,1)}, u32[]{:S(2)}, u32[]{:S(2)}) %collective-permute-start.23) | collective-permute-done | bytes 1835040 | tf_op jit(solution)/shard_map/ppermute | solution.py:867
  136.7 4.1 %first_sums.1 = (bf16[2,4,352,128]{3,2,1,0:T(8,128)(2,1)S(1)}, bf16[2,4,352,128]{3,2,1,0:T(8,128)(2,1)S(1)}, bf16[2,4,352,128]{3,2,1,0:T(8,128)(2,1)S(1)}, bf16[...) custom-call(s32[2]{0:T(128)S(1)} %pad_add_fusion.spot, ...), custom_call_target="tpu_custom_call" | custom-call | flops 3000000 | bytes 17000000 | tf_op jit(solution)/shard_map/first_sums/pallas_call | solution.py:772
  141.0 3.2 %collective-permute-start.26 = (bf16[2,4,352,128]{3,2,1,0:T(8,128)(2,1)S(1)}, bf16[2,4,352,128]{3,2,1,0:T(8,128)(2,1)S(1)}, u32[]{:S(2)}, u32[]{:S(2)}) collective-permute-start(bf16[2,4,352,128]{3,2,1,0:T(8,128)(2,1)S(1)} %get-tuple-element.178), channel_id=1, source_target_pairs={{0,48},{4,52},{8,56},{12,60},{16,0},{20,4},{24,8},{28,12},{32,16},... | collective-permute-start | bytes 2162696 | tf_op jit(solution)/shard_map/ppermute | solution.py:887
  144.1 3.2 %collective-permute-start.27 = (bf16[2,4,352,128]{3,2,1,0:T(8,128)(2,1)S(1)}, bf16[2,4,352,128]{3,2,1,0:T(8,128)(2,1)S(1)}, u32[]{:S(2)}, u32[]{:S(2)}) collective-permute-start(bf16[2,4,352,128]{3,2,1,0:T(8,128)(2,1)S(1)} %get-tuple-element.179), channel_id=1, source_target_pairs={{0,12},{4,0},{8,4},{12,8},{16,28},{20,16},{24,20},{28,24},{32,44},... | collective-permute-start | bytes 2162696 | tf_op jit(solution)/shard_map/ppermute | solution.py:891
  147.5 28.4 %collective-permute-done.24.refs_2_ = bf16[2,4,352,128]{3,2,1,0:T(8,128)(2,1)S(1)} collective-permute-done((bf16[2,4,352,128]{3,2,1,0:T(8,128)(2,1)S(1)}, bf16[2,4,352,128]{3,2,1,0:T(8,128)(2,1)S(1)}, u32[]{:S(2)}, u32[]{:S(2)}) %collective-permute-start.24) | collective-permute-done | bytes 720928 | tf_op jit(solution)/shard_map/ppermute | solution.py:887
  177.2 14.7 %collective-permute-done.27.refs_5_ = bf16[2,4,352,128]{3,2,1,0:T(8,128)(2,1)S(1)} collective-permute-done((bf16[2,4,352,128]{3,2,1,0:T(8,128)(2,1)S(1)}, bf16[2,4,352,128]{3,2,1,0:T(8,128)(2,1)S(1)}, u32[]{:S(2)}, u32[]{:S(2)}) %collective-permute-start.27) | collective-permute-done | bytes 720928 | tf_op jit(solution)/shard_map/ppermute | solution.py:891
  191.9 3.1 %collective-permute-done.29.refs_7_ = bf16[2,4,352,128]{3,2,1,0:T(8,128)(2,1)S(1)} collective-permute-done((bf16[2,4,352,128]{3,2,1,0:T(8,128)(2,1)S(1)}, bf16[2,4,352,128]{3,2,1,0:T(8,128)(2,1)S(1)}, u32[]{:S(2)}, u32[]{:S(2)}) %collective-permute-start.29) | collective-permute-done | bytes 720928 | tf_op jit(solution)/shard_map/ppermute | solution.py:891
  196.4 3.1 %collective-permute-start.32 = (bf16[2,352,128]{2,1,0:T(8,128)(2,1)S(1)}, bf16[2,352,128]{2,1,0:T(8,128)(2,1)S(1)}, u32[]{:S(2)}, u32[]{:S(2)}) collective-permute-start(bf16[2,352,128]{2,1,0:T(8,128)(2,1)S(1)} %get-tuple-element.186), channel_id=1, source_target_pairs={{0,12},{4,0},{8,4},{12,8},{16,28},{20,16},{24,20},{28,24},{32,44},... | collective-permute-start | bytes 540680 | tf_op jit(solution)/shard_map/ppermute | solution.py:891
  199.6 3.2 %collective-permute-start.33 = (bf16[2,352,128]{2,1,0:T(8,128)(2,1)S(1)}, bf16[2,352,128]{2,1,0:T(8,128)(2,1)S(1)}, u32[]{:S(2)}, u32[]{:S(2)}) collective-permute-start(bf16[2,352,128]{2,1,0:T(8,128)(2,1)S(1)} %get-tuple-element.187), channel_id=1, source_target_pairs={{0,48},{4,52},{8,56},{12,60},{16,0},{20,4},{24,8},{28,12},{32,16},... | collective-permute-start | bytes 540680 | tf_op jit(solution)/shard_map/ppermute | solution.py:887
  203.1 3.4 %collective-permute-done.32.refs_4_ = bf16[2,352,128]{2,1,0:T(8,128)(2,1)S(1)} collective-permute-done((bf16[2,352,128]{2,1,0:T(8,128)(2,1)S(1)}, bf16[2,352,128]{2,1,0:T(8,128)(2,1)S(1)}, u32[]{:S(2)}, u32[]{:S(2)}) %collective-permute-start.32) | collective-permute-done | bytes 180256 | tf_op jit(solution)/shard_map/ppermute | solution.py:891
  213.9 3.6 %collective-permute-done.38.p3 = bf16[2,352,128]{2,1,0:T(8,128)(2,1)S(1)} collective-permute-done((bf16[2,352,128]{2,1,0:T(8,128)(2,1)S(1)}, bf16[2,352,128]{2,1,0:T(8,128)(2,1)S(1)}, u32[]{:S(2)}, u32[]{:S(2)}) %collective-permute-start.38) | collective-permute-done | bytes 180256 | tf_op jit(solution)/shard_map/ppermute | solution.py:883
  219.2 3.2 %collective-permute-start.42 = (bf16[352,128]{1,0:T(8,128)(2,1)S(1)}, bf16[352,128]{1,0:T(8,128)(2,1)S(1)}, u32[]{:S(2)}, u32[]{:S(2)}) collective-permute-start(bf16[352,128]{1,0:T(8,128)(2,1)S(1)} %get-tuple-element.197), channel_id=1, source_target_pairs={{0,12},{4,0},{8,4},{12,8},{16,28},{20,16},{24,20},{28,24},{32,44},... | collective-permute-start | bytes 270344 | tf_op jit(solution)/shard_map/ppermute | solution.py:891
  238.7 4.7 %collective-permute-done.48.a3 = bf16[4,352,128]{2,1,0:T(8,128)(2,1)S(1)} collective-permute-done((bf16[4,352,128]{2,1,0:T(8,128)(2,1)S(1)}, bf16[4,352,128]{2,1,0:T(8,128)(2,1)S(1)}, u32[]{:S(2)}, u32[]{:S(2)}) %collective-permute-start.48) | collective-permute-done | bytes 360480 | tf_op jit(solution)/shard_map/ppermute | solution.py:887
  246.9 3.1 %collective-permute-done.46.a1 = bf16[4,352,128]{2,1,0:T(8,128)(2,1)S(1)} collective-permute-done((bf16[4,352,128]{2,1,0:T(8,128)(2,1)S(1)}, bf16[4,352,128]{2,1,0:T(8,128)(2,1)S(1)}, u32[]{:S(2)}, u32[]{:S(2)}) %collective-permute-start.46) | collective-permute-done | bytes 360480 | tf_op jit(solution)/shard_map/ppermute | solution.py:887
  250.5 3.7 %collective-permute-done.49.b1 = bf16[4,352,128]{2,1,0:T(8,128)(2,1)S(1)} collective-permute-done((bf16[4,352,128]{2,1,0:T(8,128)(2,1)S(1)}, bf16[4,352,128]{2,1,0:T(8,128)(2,1)S(1)}, u32[]{:S(2)}, u32[]{:S(2)}) %collective-permute-start.49) | collective-permute-done | bytes 360480 | tf_op jit(solution)/shard_map/ppermute | solution.py:891
  254.2 8.7 %unpack.1 = (f32[160,1024]{1,0:T(8,128)}, f32[160,256]{1,0:T(8,128)}, f32[160,256]{1,0:T(8,128)}, f32[256,640]{1,0:T(8,128)}, f32[160,2048]{1,0:T(8,128)}, /*ind...) custom-call(s32[2]{0:T(128)S(1)} %pad_add_fusion.spot, bf16[4,352,128]{2,1,0:T(8,128)(2,1)S(1)} %pad_maximum_fusion.a0, ...), custom_call_target="tpu_custom_call" | custom-call | flops 4000000 | bytes 11000000 | tf_op jit(solution)/shard_map/unpack/pallas_call | solution.py:727
  (182 shorter events, 78.0 us)
Async XLA Ops:
  0.7 12.4 %collective-permute-start.1 = (bf16[160,1024]{1,0:T(8,128)(2,1)}, bf16[160,1024]{1,0:T(8,128)(2,1)S(1)}, u32[]{:S(2)}, u32[]{:S(2)}) collective-permute-start(bf16[160,1024]{1,0:T(8,128)(2,1)} %q0.1), channel_id=1, source_target_pairs={{0,2},{1,3},{2,0},{3,1},{4,6},{5,7},{6,4},{7,5},{8,10},{9,11},{10,... | collective-permute-start | bytes 983048 | tf_op jit(solution)/shard_map/ppermute | solution.py:871
  4.5 14.6 %collective-permute-start.4 = (bf16[160,512]{1,0:T(8,128)(2,1)S(1)}, bf16[160,512]{1,0:T(8,128)(2,1)S(1)}, u32[]{:S(2)}, u32[]{:S(2)}) collective-permute-start(bf16[160,512]{1,0:T(8,128)(2,1)S(1)} %constant_dynamic-update-slice_fusion.kv0), channel_id=1, source_target_pairs={{0,66},{1,67},{2,64},{3,65},{4,70},{5,71},{6,68},{7,69},{8,74},{9,... | collective-permute-start | bytes 491528 | tf_op jit(solution)/shard_map/ppermute | solution.py:879
  7.0 28.9 %collective-permute-start.6 = (bf16[512,640]{1,0:T(8,128)(2,1)}, bf16[512,640]{1,0:T(8,128)(2,1)S(1)}, u32[]{:S(2)}, u32[]{:S(2)}) collective-permute-start(bf16[512,640]{1,0:T(8,128)(2,1)} %bitcast.36), channel_id=1, source_target_pairs={{0,4},{4,8},{8,12},{12,16},{16,20},{20,24},{24,28},{28,32},{32,36}... | collective-permute-start | bytes 1966088 | tf_op jit(solution)/shard_map/ppermute | solution.py:896
  17.1 12.1 %collective-permute-start.9 = (f32[8,256]{1,0:T(8,128)S(1)}, f32[8,256]{1,0:T(8,128)S(1)}, u32[]{:S(2)}, u32[]{:S(2)}) collective-permute-start(f32[8,256]{1,0:T(8,128)S(1)} %pack.1), channel_id=1, source_target_pairs={{0,3},{1,2},{2,1},{3,0},{4,7},{5,6},{6,5},{7,4},{8,11},{9,10},{10,... | collective-permute-start | bytes 24584 | tf_op jit(solution)/shard_map/ppermute | solution.py:875
  17.2 12.1 %collective-permute-start.8 = (f32[8,256]{1,0:T(8,128)S(1)}, f32[8,256]{1,0:T(8,128)S(1)}, u32[]{:S(2)}, u32[]{:S(2)}) collective-permute-start(f32[8,256]{1,0:T(8,128)S(1)} %pack.1), channel_id=1, source_target_pairs={{0,2},{1,3},{2,0},{3,1},{4,6},{5,7},{6,4},{7,5},{8,10},{9,11},{10,... | collective-permute-start | bytes 24584 | tf_op jit(solution)/shard_map/ppermute | solution.py:871
  18.3 11.0 %collective-permute-start.7 = (f32[8,256]{1,0:T(8,128)S(1)}, f32[8,256]{1,0:T(8,128)S(1)}, u32[]{:S(2)}, u32[]{:S(2)}) collective-permute-start(f32[8,256]{1,0:T(8,128)S(1)} %pack.1), channel_id=1, source_target_pairs={{0,1},{1,0},{2,3},{3,2},{4,5},{5,4},{6,7},{7,6},{8,9},{9,8},{10,11... | collective-permute-start | bytes 24584 | tf_op jit(solution)/shard_map/ppermute | solution.py:867
  19.1 14.6 %collective-permute-start.3 = (bf16[160,512]{1,0:T(8,128)(2,1)S(1)}, bf16[160,512]{1,0:T(8,128)(2,1)S(1)}, u32[]{:S(2)}, u32[]{:S(2)}) collective-permute-start(bf16[160,512]{1,0:T(8,128)(2,1)S(1)} %constant_dynamic-update-slice_fusion.kv0), channel_id=1, source_target_pairs={{0,1},{1,0},{2,3},{3,2},{4,5},{5,4},{6,7},{7,6},{8,9},{9,8},{10,11... | collective-permute-start | bytes 491528 | tf_op jit(solution)/shard_map/ppermute | solution.py:867
  29.3 17.9 %collective-permute-start.10 = (bf16[160,2048]{1,0:T(8,128)(2,1)}, bf16[160,2048]{1,0:T(8,128)(2,1)}, u32[]{:S(2)}, u32[]{:S(2)}) collective-permute-start(bf16[160,2048]{1,0:T(8,128)(2,1)} %g0.1), channel_id=1, source_target_pairs={{0,2},{1,3},{2,0},{3,1},{4,6},{5,7},{6,4},{7,5},{8,10},{9,11},{10,... | collective-permute-start | bytes 1966088 | tf_op jit(solution)/shard_map/ppermute | solution.py:871
  30.9 19.1 %collective-permute-start.11 = (bf16[160,2048]{1,0:T(8,128)(2,1)}, bf16[160,2048]{1,0:T(8,128)(2,1)}, u32[]{:S(2)}, u32[]{:S(2)}) collective-permute-start(bf16[160,2048]{1,0:T(8,128)(2,1)} %u0), channel_id=1, source_target_pairs={{0,66},{1,67},{2,64},{3,65},{4,70},{5,71},{6,68},{7,69},{8,74},{9,... | collective-permute-start | bytes 1966088 | tf_op jit(solution)/shard_map/ppermute | solution.py:879
  35.9 19.0 %collective-permute-start.12 = (bf16[256,640]{1,0:T(8,128)(2,1)}, bf16[256,640]{1,0:T(8,128)(2,1)S(1)}, u32[]{:S(2)}, u32[]{:S(2)}) collective-permute-start(bf16[256,640]{1,0:T(8,128)(2,1)} %o0), channel_id=1, source_target_pairs={{0,2},{1,3},{2,0},{3,1},{4,6},{5,7},{6,4},{7,5},{8,10},{9,11},{10,... | collective-permute-start | bytes 983048 | tf_op jit(solution)/shard_map/ppermute | solution.py:871
  36.4 26.8 %collective-permute-start.13 = (bf16[512,640]{1,0:T(8,128)(2,1)}, bf16[512,640]{1,0:T(8,128)(2,1)S(1)}, u32[]{:S(2)}, u32[]{:S(2)}) collective-permute-start(bf16[512,640]{1,0:T(8,128)(2,1)} %d0), channel_id=1, source_target_pairs={{0,66},{1,67},{2,64},{3,65},{4,70},{5,71},{6,68},{7,69},{8,74},{9,... | collective-permute-start | bytes 1966088 | tf_op jit(solution)/shard_map/ppermute | solution.py:879
  107.9 26.7 %collective-permute-start.22 = (bf16[2,7680,128]{2,1,0:T(8,128)(2,1)}, bf16[2,7680,128]{2,1,0:T(8,128)(2,1)}, u32[]{:S(2)}, u32[]{:S(2)}) collective-permute-start(bf16[2,7680,128]{2,1,0:T(8,128)(2,1)} %get-tuple-element.171), channel_id=1, source_target_pairs={{0,1},{1,0},{2,3},{3,2},{4,5},{5,4},{6,7},{7,6},{8,9},{9,8},{10,11... | collective-permute-start | bytes 11796488 | tf_op jit(solution)/shard_map/ppermute | solution.py:867
  140.8 35.1 %collective-permute-start.24 = (bf16[2,4,352,128]{3,2,1,0:T(8,128)(2,1)S(1)}, bf16[2,4,352,128]{3,2,1,0:T(8,128)(2,1)S(1)}, u32[]{:S(2)}, u32[]{:S(2)}) collective-permute-start(bf16[2,4,352,128]{3,2,1,0:T(8,128)(2,1)S(1)} %get-tuple-element.176), channel_id=1, source_target_pairs={{0,16},{4,20},{8,24},{12,28},{16,32},{20,36},{24,40},{28,44},{32,4... | collective-permute-start | bytes 2162696 | tf_op jit(solution)/shard_map/ppermute | solution.py:887
  140.9 35.1 %collective-permute-start.25 = (bf16[2,4,352,128]{3,2,1,0:T(8,128)(2,1)S(1)}, bf16[2,4,352,128]{3,2,1,0:T(8,128)(2,1)S(1)}, u32[]{:S(2)}, u32[]{:S(2)}) collective-permute-start(bf16[2,4,352,128]{3,2,1,0:T(8,128)(2,1)S(1)} %get-tuple-element.177), channel_id=1, source_target_pairs={{0,4},{4,8},{8,12},{12,0},{16,20},{20,24},{24,28},{28,16},{32,36},... | collective-permute-start | bytes 2162696 | tf_op jit(solution)/shard_map/ppermute | solution.py:891
  141.0 36.3 %collective-permute-start.26 = (bf16[2,4,352,128]{3,2,1,0:T(8,128)(2,1)S(1)}, bf16[2,4,352,128]{3,2,1,0:T(8,128)(2,1)S(1)}, u32[]{:S(2)}, u32[]{:S(2)}) collective-permute-start(bf16[2,4,352,128]{3,2,1,0:T(8,128)(2,1)S(1)} %get-tuple-element.178), channel_id=1, source_target_pairs={{0,48},{4,52},{8,56},{12,60},{16,0},{20,4},{24,8},{28,12},{32,16},... | collective-permute-start | bytes 2162696 | tf_op jit(solution)/shard_map/ppermute | solution.py:887
  144.1 47.8 %collective-permute-start.27 = (bf16[2,4,352,128]{3,2,1,0:T(8,128)(2,1)S(1)}, bf16[2,4,352,128]{3,2,1,0:T(8,128)(2,1)S(1)}, u32[]{:S(2)}, u32[]{:S(2)}) collective-permute-start(bf16[2,4,352,128]{3,2,1,0:T(8,128)(2,1)S(1)} %get-tuple-element.179), channel_id=1, source_target_pairs={{0,12},{4,0},{8,4},{12,8},{16,28},{20,16},{24,20},{28,24},{32,44},... | collective-permute-start | bytes 2162696 | tf_op jit(solution)/shard_map/ppermute | solution.py:891
  147.3 44.6 %collective-permute-start.28 = (bf16[2,4,352,128]{3,2,1,0:T(8,128)(2,1)S(1)}, bf16[2,4,352,128]{3,2,1,0:T(8,128)(2,1)S(1)}, u32[]{:S(2)}, u32[]{:S(2)}) collective-permute-start(bf16[2,4,352,128]{3,2,1,0:T(8,128)(2,1)S(1)} %get-tuple-element.180), channel_id=1, source_target_pairs={{0,32},{4,36},{8,40},{12,44},{16,48},{20,52},{24,56},{28,60},{32,0... | collective-permute-start | bytes 2162696 | tf_op jit(solution)/shard_map/ppermute | solution.py:887
  175.9 19.1 %collective-permute-start.29 = (bf16[2,4,352,128]{3,2,1,0:T(8,128)(2,1)S(1)}, bf16[2,4,352,128]{3,2,1,0:T(8,128)(2,1)S(1)}, u32[]{:S(2)}, u32[]{:S(2)}) collective-permute-start(bf16[2,4,352,128]{3,2,1,0:T(8,128)(2,1)S(1)} %get-tuple-element.181), channel_id=1, source_target_pairs={{0,8},{4,12},{8,0},{12,4},{16,24},{20,28},{24,16},{28,20},{32,40},... | collective-permute-start | bytes 2162696 | tf_op jit(solution)/shard_map/ppermute | solution.py:891
  175.9 43.3 %collective-permute-start.39 = (bf16[512,640]{1,0:T(8,128)(2,1)S(1)}, bf16[512,640]{1,0:T(8,128)(2,1)S(1)}, u32[]{:S(2)}, u32[]{:S(2)}) collective-permute-start(bf16[512,640]{1,0:T(8,128)(2,1)S(1)} %copy-done.16), channel_id=1, source_target_pairs={{4,0},{8,4},{12,8},{16,12},{20,16},{24,20},{28,24},{32,28},{36,32}... | collective-permute-start | bytes 1966088 | tf_op jit(solution)/shard_map/ppermute | solution.py:896
  232.0 11.4 %collective-permute-start.48 = (bf16[4,352,128]{2,1,0:T(8,128)(2,1)S(1)}, bf16[4,352,128]{2,1,0:T(8,128)(2,1)S(1)}, u32[]{:S(2)}, u32[]{:S(2)}) collective-permute-start(bf16[4,352,128]{2,1,0:T(8,128)(2,1)S(1)} %pad_maximum_fusion.a0), channel_id=1, source_target_pairs={{0,48},{4,52},{8,56},{12,60},{16,0},{20,4},{24,8},{28,12},{32,16},... | collective-permute-start | bytes 1081352 | tf_op jit(solution)/shard_map/ppermute | solution.py:887
  233.5 13.4 %collective-permute-start.47 = (bf16[4,352,128]{2,1,0:T(8,128)(2,1)S(1)}, bf16[4,352,128]{2,1,0:T(8,128)(2,1)S(1)}, u32[]{:S(2)}, u32[]{:S(2)}) collective-permute-start(bf16[4,352,128]{2,1,0:T(8,128)(2,1)S(1)} %pad_maximum_fusion.a0), channel_id=1, source_target_pairs={{0,32},{4,36},{8,40},{12,44},{16,48},{20,52},{24,56},{28,60},{32,0... | collective-permute-start | bytes 1081352 | tf_op jit(solution)/shard_map/ppermute | solution.py:887
  234.4 15.6 %collective-permute-start.46 = (bf16[4,352,128]{2,1,0:T(8,128)(2,1)S(1)}, bf16[4,352,128]{2,1,0:T(8,128)(2,1)S(1)}, u32[]{:S(2)}, u32[]{:S(2)}) collective-permute-start(bf16[4,352,128]{2,1,0:T(8,128)(2,1)S(1)} %pad_maximum_fusion.a0), channel_id=1, source_target_pairs={{0,16},{4,20},{8,24},{12,28},{16,32},{20,36},{24,40},{28,44},{32,4... | collective-permute-start | bytes 1081352 | tf_op jit(solution)/shard_map/ppermute | solution.py:887
  234.6 15.9 %collective-permute-start.51 = (bf16[4,352,128]{2,1,0:T(8,128)(2,1)S(1)}, bf16[4,352,128]{2,1,0:T(8,128)(2,1)S(1)}, u32[]{:S(2)}, u32[]{:S(2)}) collective-permute-start(bf16[4,352,128]{2,1,0:T(8,128)(2,1)S(1)} %pad_maximum_fusion.1.b0), channel_id=1, source_target_pairs={{0,12},{4,0},{8,4},{12,8},{16,28},{20,16},{24,20},{28,24},{32,44},... | collective-permute-start | bytes 1081352 | tf_op jit(solution)/shard_map/ppermute | solution.py:891
  237.2 13.2 %collective-permute-start.50 = (bf16[4,352,128]{2,1,0:T(8,128)(2,1)S(1)}, bf16[4,352,128]{2,1,0:T(8,128)(2,1)S(1)}, u32[]{:S(2)}, u32[]{:S(2)}) collective-permute-start(bf16[4,352,128]{2,1,0:T(8,128)(2,1)S(1)} %pad_maximum_fusion.1.b0), channel_id=1, source_target_pairs={{0,8},{4,12},{8,0},{12,4},{16,24},{20,28},{24,16},{28,20},{32,40},... | collective-permute-start | bytes 1081352 | tf_op jit(solution)/shard_map/ppermute | solution.py:891
  (62 other events, 653.6 us)
